TPU v7x, 32 devices: a whole 2x2x4 slice. The times are simulated.
32 devices in a mesh: gx: 8 (over z, x), gy: 4 (over y, core).
Axes of the slice: x: 2, y: 2, z: 4, core: 2. Of those that a mesh axis runs over, the one named last changes fastest.
Arguments:
- model_image: float32 [128, 64, 128], P('gx', 'gy'), may hold values from -6 to 6
- data_residual: float32 [128, 64, 2048], P('gx', 'gy'), may hold values from -6 to 6
- direction: float32 [128, 64, 128], P('gx', 'gy'), may hold values from -6 to 6
- old_gradient: float32 [128, 64, 128], P('gx', 'gy'), may hold values from -18 to 18
- aperture: int32 [128, 64, 16], P('gx', 'gy'), may hold values from 0 to 288
- travel_times: int32 [128, 64, 16, 128], P('gx', 'gy'), may hold values from 0 to 2047, as said below
- amplitude: float32 [128, 64, 16], P('gx', 'gy'), may hold values from 0.02 to 0.2
- trace_counts: int32 [128, 64], P('gx', 'gy'), may hold values from 1 to 24
Outputs:
- new_image: float32 [128, 64, 128], P('gx', 'gy')
- new_residual: float32 [128, 64, 2048], P('gx', 'gy')
- new_direction: float32 [128, 64, 128], P('gx', 'gy')
Inputs may be any that keep to these rules, and one draw needn't show every extreme that they name: `travel_times`: along each aperture entry the time sample index never decreases with depth.
All inputs are finite; a program needn't handle non-finite values.
Results may differ from a plain program's by a relative error of at most 0.0003.
Values sent between devices are 32-bit elements; how exact they have to be, the bound alone decides.
No kernel may reach another device: no remote copies, remote signals or barrier semaphores. Data moves between devices by JAX's collectives and lax.ppermute only.
A program may use at most 64 MiB of HBM per device.

v0:
```python
import functools

import jax
import jax.numpy as jnp
from jax import lax
from jax.experimental import pallas as pl
from jax.experimental.pallas import tpu as pltpu
from jax.sharding import PartitionSpec as P

RADIUS = 8
SIDE = 2 * RADIUS + 1
LANES = 128
SUB = 8
F32 = jnp.float32
BF16 = jnp.bfloat16
VMEM_LIMIT = 48 * 1024 * 1024


def params(**extra):
    return pltpu.CompilerParams(vmem_limit_bytes=VMEM_LIMIT, **extra)


def to_rows(traces):
    bins_x, bins_y, samples = traces.shape
    parts = traces.reshape(bins_x, bins_y // SUB, SUB, samples // LANES, LANES)
    return parts.transpose(0, 1, 3, 2, 4).reshape(-1, LANES)


def from_rows(rows, shape):
    bins_x, bins_y, samples = shape
    parts = rows.reshape(bins_x, bins_y // SUB, samples // LANES, SUB, LANES)
    return parts.transpose(0, 1, 3, 2, 4).reshape(shape)


def trace_row(b, highs):
    return (b // SUB) * (SUB * highs) + b % SUB


def sample_row(res_ref, times_ref, wt_ref, vals, bins_y, entries, highs):
    for b in range(bins_y):
        times = times_ref[b]
        high = times // LANES
        low = times % LANES
        acc = jnp.zeros(times.shape, F32)
        first = trace_row(b, highs)
        for h in range(highs):
            row = res_ref[pl.ds(first + SUB * h, 1), :]
            table = jnp.broadcast_to(row, times.shape)
            got = jnp.take_along_axis(table, low, axis=1, mode="promise_in_bounds")
            acc = jnp.where(high == h, got, acc)
        vals[pl.ds(b * entries, entries), :] = acc * wt_ref[0][:, b : b + 1]


def spread_row(vals, place_ref, s_ref, row, wide_y, span):
    value = vals[...]
    upper = value.astype(BF16)
    lower = (value - upper.astype(F32)).astype(BF16)
    both = jnp.concatenate([upper, lower], axis=1)
    place = place_ref[0]
    step = 32
    for m in range(0, span, step):
        iota = lax.broadcasted_iota(jnp.int32, (step, place.shape[1]), 0) + m
        table = jnp.where(iota == place, 1.0, 0.0).astype(BF16)
        part = jnp.dot(table, both, preferred_element_type=F32)
        at = pl.ds(pl.multiple_of(row * wide_y + m, SUB), step)
        s_ref[at, :] += part[:, :LANES] + part[:, LANES:]


def first_kernel(geo, row0, res_ref, times_ref, wt_ref, place_ref, prev_ref, s_ref, vals):
    bins_y, entries, highs, wide_y = geo
    step = pl.program_id(0)

    @pl.when(step == 0)
    def _():
        s_ref[...] = prev_ref[...]

    sample_row(res_ref, times_ref, wt_ref, vals, bins_y, entries, highs)
    spread_row(vals, place_ref, s_ref, step + row0, wide_y, SIDE * wide_y)


def main_kernel(
    geo,
    unroll,
    col_ref,
    weight_ref,
    times_ref,
    wt_ref,
    place_ref,
    mid_ref,
    left_ref,
    right_ref,
    s1_ref,
    data_ref,
    curv_ref,
    out_left,
    out_mid,
    out_right,
    image,
    s_ref,
    vals,
    work,
):
    bins_y, entries, highs, wide_y = geo
    step = pl.program_id(0)
    wide_x = mid_ref.shape[0]

    @pl.when(step == 0)
    def _():
        s_ref[...] = jnp.zeros_like(s_ref)
        curv_ref[...] = jnp.zeros_like(curv_ref)
        for x in range(wide_x):
            image[pl.ds(x * wide_y, RADIUS), :] = left_ref[x]
            image[pl.ds(x * wide_y + RADIUS, bins_y), :] = mid_ref[x]
            image[pl.ds(x * wide_y + RADIUS + bins_y, RADIUS), :] = right_ref[x]

    half = LANES // 2
    iota_lo = lax.broadcasted_iota(jnp.int32, (half, LANES), 0).astype(F32).astype(BF16)
    iota_hi = lax.broadcasted_iota(jnp.int32, (2 * highs, LANES), 0).astype(F32).astype(BF16)
    zero = jnp.zeros((), BF16)
    one = jnp.ones((), BF16)

    def one_bin(b, slot):
        for e in range(entries):
            column = col_ref[0, b, e]
            work[slot, 0, pl.ds(e, 1), :] = image[pl.ds(column, 1), :] * weight_ref[0, b, e]
        value = work[slot, 0]
        upper = value.astype(BF16).astype(F32)
        work[slot, 0] = upper
        work[slot, 1] = value - upper
        times = times_ref[b]
        work[slot, 2] = (times % half).astype(F32)
        work[slot, 3] = (times // LANES + ((times // half) % 2) * highs).astype(F32)
        lefts = []
        rights = []
        for e in range(entries):

            def wide(k, rows):
                row = work[slot, k, pl.ds(e, 1), :]
                return jnp.broadcast_to(
                    jnp.broadcast_to(row, (16, LANES)).astype(BF16)[None], (rows // 16, 16, LANES)
                ).reshape(rows, LANES)

            hit = wide(3, 2 * highs) == iota_hi
            lefts.append(
                jnp.concatenate(
                    [
                        jnp.where(hit, wide(0, 2 * highs), zero),
                        jnp.where(hit, wide(1, 2 * highs), zero),
                    ],
                    axis=0,
                )
            )
            rights.append(jnp.where(wide(2, half) == iota_lo, one, zero))
        out = lax.dot_general(
            jnp.concatenate(lefts, axis=1),
            jnp.concatenate(rights, axis=1),
            (((1,), (1,)), ((), ())),
            preferred_element_type=F32,
        )
        out = out[: 2 * highs] + out[2 * highs :]
        trace = jnp.concatenate([out[:highs], out[highs:]], axis=1)
        data_ref[pl.ds(trace_row(b, highs), highs, stride=SUB), :] = trace
        return trace * trace

    def some_bins(k, total):
        for u in range(unroll):
            total = total + one_bin(k * unroll + u, u)
        return total

    total = lax.fori_loop(0, bins_y // unroll, some_bins, jnp.zeros((highs, LANES), F32))
    curv_ref[...] += total
    sample_row(data_ref, times_ref, wt_ref, vals, bins_y, entries, highs)
    spread_row(vals, place_ref, s_ref, step, wide_y, SIDE * wide_y)

    @pl.when(step == pl.num_programs(0) - 1)
    def _():
        for k, ref in enumerate((s1_ref, s_ref)):
            for x in range(wide_x):
                out_left[k, x] = ref[pl.ds(x * wide_y, RADIUS), :]
                out_mid[k, x] = ref[pl.ds(x * wide_y + RADIUS, bins_y), :]
                out_right[k, x] = ref[pl.ds(x * wide_y + RADIUS + bins_y, RADIUS), :]


def fold_y_kernel(mid_ref, low_ref, high_ref, out_head, out_mid, out_tail):
    wide_x, bins_y = mid_ref.shape[1], mid_ref.shape[2]
    bins_x = wide_x - 2 * RADIUS
    for k in range(2):
        for x in range(wide_x):
            if x < RADIUS:
                ref, at = out_head, x
            elif x < RADIUS + bins_x:
                ref, at = out_mid, x - RADIUS
            else:
                ref, at = out_tail, x - RADIUS - bins_x
            ref[k, at, pl.ds(0, RADIUS), :] = mid_ref[k, x, pl.ds(0, RADIUS), :] + low_ref[k, x]
            high = pl.ds(bins_y - RADIUS, RADIUS)
            ref[k, at, high, :] = mid_ref[k, x, high, :] + high_ref[k, x]


def fold_x_kernel(mid_ref, low_ref, high_ref, grad_ref, curv_ref, out_ref, stats_ref):
    bins_x = mid_ref.shape[1]
    sums = [jnp.zeros((1, LANES), F32) for _ in range(5)]
    for x in range(bins_x):
        pair = []
        for k in range(2):
            cells = mid_ref[k, x]
            if x < RADIUS:
                cells = cells + low_ref[k, x]
            else:
                cells = cells + high_ref[k, x - RADIUS]
            out_ref[k, x] = cells
            pair.append(cells)
        old = grad_ref[x]
        terms = (old * old, None, pair[0] * pair[0], pair[0] * pair[1], pair[1] * pair[1])
        for n, term in enumerate(terms):
            if term is not None:
                sums[n] = sums[n] + jnp.sum(term, axis=0, keepdims=True)
    sums[1] = jnp.sum(curv_ref[...], axis=0, keepdims=True)
    lane = lax.broadcasted_iota(jnp.int32, (1, LANES), 1)
    stats = jnp.zeros((1, LANES), F32)
    for n, term in enumerate(sums):
        stats = jnp.where(lane == n, jnp.sum(term, axis=1, keepdims=True), stats)
    stats_ref[...] = stats


def last_kernel(
    stats_ref, res_ref, data_ref, model_ref, dir_ref, grad_ref, new_image, new_residual, new_dir
):
    stats = jnp.sum(stats_ref[...], axis=0, keepdims=True)
    lane = lax.broadcasted_iota(jnp.int32, stats.shape, 1)

    def pick(n):
        return jnp.sum(jnp.where(lane == n, stats, 0.0), axis=1, keepdims=True)

    gamma, curvature, one_one, one_two, two_two = (pick(n) for n in range(5))
    alpha = gamma / curvature
    gamma_new = one_one - 2.0 * (alpha * one_two) + alpha * (alpha * two_two)
    beta = gamma_new / gamma
    new_residual[...] = res_ref[...] - alpha * data_ref[...]
    step = dir_ref[...]
    new_image[...] = model_ref[...] + alpha[None] * step
    new_dir[...] = (grad_ref[0] - alpha[None] * grad_ref[1]) + beta[None] * step


def shift(cells, axis, by):
    count = lax.axis_size(axis)
    pairs = [(i, i + by) for i in range(count) if 0 <= i + by < count]
    return lax.ppermute(cells, axis, pairs)


def body(
    model_image,
    data_residual,
    direction,
    old_gradient,
    aperture,
    travel_times,
    amplitude,
    trace_counts,
):
    bins_x, bins_y, samples = data_residual.shape
    entries, depths = travel_times.shape[2], travel_times.shape[3]
    highs = samples // LANES
    wide_x, wide_y = bins_x + 2 * RADIUS, bins_y + 2 * RADIUS
    columns = wide_x * wide_y
    span = SIDE * wide_y
    geo = (bins_y, entries, highs, wide_y)
    rows_per = bins_y * highs

    from_prev = shift(direction[bins_x - RADIUS :], "gx", 1)
    from_next = shift(direction[:RADIUS], "gx", -1)

    times = travel_times.reshape(bins_x * bins_y, entries, depths)
    res_rows = to_rows(data_residual)
    weight = amplitude * trace_counts.astype(F32)[:, :, None]
    weight_t = weight.transpose(0, 2, 1)
    off = (aperture // SIDE) * wide_y + aperture % SIDE
    window = off + jnp.arange(bins_y, dtype=jnp.int32)[None, :, None]
    column = window + wide_y * jnp.arange(bins_x, dtype=jnp.int32)[:, None, None]
    place = window.reshape(bins_x, 1, bins_y * entries)

    def first(row0, count, prev):
        return pl.pallas_call(
            functools.partial(first_kernel, geo, row0),
            grid=(count,),
            in_specs=[
                pl.BlockSpec((rows_per, LANES), lambda i: (i + row0, 0)),
                pl.BlockSpec((bins_y, entries, depths), lambda i: (i + row0, 0, 0)),
                pl.BlockSpec((1, entries, bins_y), lambda i: (i + row0, 0, 0)),
                pl.BlockSpec((1, 1, bins_y * entries), lambda i: (i + row0, 0, 0)),
                pl.BlockSpec((columns, depths), lambda i: (0, 0)),
            ],
            out_specs=pl.BlockSpec((columns, depths), lambda i: (0, 0)),
            out_shape=jax.ShapeDtypeStruct((columns, depths), F32),
            scratch_shapes=[pltpu.VMEM((bins_y * entries, depths), F32)],
            compiler_params=params(),
            cost_estimate=pl.CostEstimate(
                flops=4 * 10**9, bytes_accessed=4 * 10**6, transcendentals=0
            ),
            name="sample_residual",
        )(res_rows, times, weight_t, place, prev)

    s1 = first(0, bins_x // 2, jnp.zeros((columns, depths), F32))
    ext = jnp.concatenate([from_prev, direction, from_next], axis=0)
    left = shift(ext[:, bins_y - RADIUS :], "gy", 1)
    right = shift(ext[:, :RADIUS], "gy", -1)
    s1 = first(bins_x // 2, bins_x - bins_x // 2, s1)

    unroll = 4
    whole3 = lambda i: (0, 0, 0)
    whole4 = lambda i: (0, 0, 0, 0)
    strip = (2, wide_x, RADIUS, depths)
    middle = (2, wide_x, bins_y, depths)
    data_rows, curv, out_left, out_mid, out_right = pl.pallas_call(
        functools.partial(main_kernel, geo, unroll),
        grid=(bins_x,),
        in_specs=[
            pl.BlockSpec((1, bins_y, entries), lambda i: (i, 0, 0), memory_space=pltpu.SMEM),
            pl.BlockSpec((1, bins_y, entries), lambda i: (i, 0, 0), memory_space=pltpu.SMEM),
            pl.BlockSpec((bins_y, entries, depths), lambda i: (i, 0, 0)),
            pl.BlockSpec((1, entries, bins_y), lambda i: (i, 0, 0)),
            pl.BlockSpec((1, 1, bins_y * entries), lambda i: (i, 0, 0)),
            pl.BlockSpec((wide_x, bins_y, depths), whole3),
            pl.BlockSpec((wide_x, RADIUS, depths), whole3),
            pl.BlockSpec((wide_x, RADIUS, depths), whole3),
            pl.BlockSpec((columns, depths), lambda i: (0, 0)),
        ],
        out_specs=[
            pl.BlockSpec((rows_per, LANES), lambda i: (i, 0)),
            pl.BlockSpec((highs, LANES), lambda i: (0, 0)),
            pl.BlockSpec(strip, whole4),
            pl.BlockSpec(middle, whole4),
            pl.BlockSpec(strip, whole4),
        ],
        out_shape=[
            jax.ShapeDtypeStruct((bins_x * rows_per, LANES), F32),
            jax.ShapeDtypeStruct((highs, LANES), F32),
            jax.ShapeDtypeStruct(strip, F32),
            jax.ShapeDtypeStruct(middle, F32),
            jax.ShapeDtypeStruct(strip, F32),
        ],
        scratch_shapes=[
            pltpu.VMEM((columns, depths), F32),
            pltpu.VMEM((columns, depths), F32),
            pltpu.VMEM((bins_y * entries, depths), F32),
            pltpu.VMEM((unroll, 4, entries, LANES), F32),
        ],
        compiler_params=params(),
        cost_estimate=pl.CostEstimate(
            flops=20 * 10**9, bytes_accessed=8 * 10**6, transcendentals=0
        ),
        name="demigrate_and_sample",
    )(column, weight, times, weight_t, place, ext, left, right, s1)

    from_low = shift(out_right, "gy", 1)
    from_high = shift(out_left, "gy", -1)
    edge = jax.ShapeDtypeStruct((2, RADIUS, bins_y, depths), F32)
    out_head, inner, out_tail = pl.pallas_call(
        fold_y_kernel,
        out_shape=[edge, jax.ShapeDtypeStruct((2, bins_x, bins_y, depths), F32), edge],
        compiler_params=params(),
        name="fold_y",
    )(out_mid, from_low, from_high)
    from_low = shift(out_tail, "gx", 1)
    from_high = shift(out_head, "gx", -1)
    grads, stats = pl.pallas_call(
        fold_x_kernel,
        out_shape=[
            jax.ShapeDtypeStruct((2, bins_x, bins_y, depths), F32),
            jax.ShapeDtypeStruct((1, LANES), F32),
        ],
        compiler_params=params(),
        name="fold_x",
    )(inner, from_low, from_high, old_gradient, curv)
    stats = lax.all_gather(stats, ("gx", "gy"), axis=0, tiled=True)

    steps = 8
    rows_step = bins_x * rows_per // steps
    x_step = bins_x // steps
    cells = pl.BlockSpec((x_step, bins_y, depths), lambda i: (i, 0, 0))
    rows = pl.BlockSpec((rows_step, LANES), lambda i: (i, 0))
    image_shape = jax.ShapeDtypeStruct(direction.shape, F32)
    new_image, new_rows, new_direction = pl.pallas_call(
        last_kernel,
        grid=(steps,),
        in_specs=[
            pl.BlockSpec(stats.shape, lambda i: (0, 0)),
            rows,
            rows,
            cells,
            cells,
            pl.BlockSpec((2, x_step, bins_y, depths), lambda i: (0, i, 0, 0)),
        ],
        out_specs=[cells, rows, cells],
        out_shape=[image_shape, jax.ShapeDtypeStruct(res_rows.shape, F32), image_shape],
        compiler_params=params(),
        name="update",
    )(stats, res_rows, data_rows, model_image, direction, grads)
    return (new_image, from_rows(new_rows, data_residual.shape), new_direction)


def solution(mesh):
    in_specs = (
        P("gx", "gy", None),
        P("gx", "gy", None),
        P("gx", "gy", None),
        P("gx", "gy", None),
        P("gx", "gy", None),
        P("gx", "gy", None, None),
        P("gx", "gy", None),
        P("gx", "gy"),
    )
    out_specs = (P("gx", "gy", None), P("gx", "gy", None), P("gx", "gy", None))
    return jax.shard_map(body, mesh=mesh, in_specs=in_specs, out_specs=out_specs, check_vma=False)
```

profile of v0, /device:TPU:0, one launch (start us, length us, event | category | flops | bytes accessed | tf_op | source)
XLA Modules:
  0.0 178.8 jit_solution(7774904444076285008)
XLA Ops:
  0.6 0.9 fusion.6
  1.5 1.3 collective-permute-start.1
  2.8 5.5 %collective-permute-start = (f32[8,16,128]{2,1,0:T(8,128)S(1)}, f32[8,16,128]{2,1,0:T(8,128)S(1)}, u32[]{:S(2)}, u32[]{:S(2)}) collective-permute-start(f32[8,16,128]{2,1,0:T(8,128)S(1)} %get-tuple-element.34), channel_id=1, source_target_pairs={{0,4},{4,8},{8,12},{12,16},{16,20},{20,24},{24,28},{1,5},{5,9},{9,... | collective-permute-start | bytes 196616 | tf_op jit(solution)/shard_map/ppermute | solution.py:248
  8.3 0.7 convert_element_type.3
  9.0 1.0 copy.14
  10.0 1.1 broadcast_add_fusion
  11.1 0.1 reshape.31.place_ref
  11.2 0.0 copy-start
  11.3 1.6 copy-done
  12.8 0.0 copy-start.5
  12.8 1.6 copy-done.5
  14.4 14.5 %sample_residual.2.prev_ref = f32[1024,128]{1,0:T(8,128)S(1)} custom-call(f32[4096,128]{1,0:T(8,128)S(1)} %bitcast.15, s32[256,16,128]{2,1,0:T(8,128)S(1)} %bitcast.21, f32[16,16,16]{2,1,0:T(8,128)S(1)} %fusion.7.wt_ref, s32[16,1,256]{2,1,0:T(1,128)S(1)} %reshape.31.place_ref, f32[1024,128]{1,0:T(8,128)S(1)} %broadcast_in_dim.2.prev_ref), custom_call_target="tpu_custom_call" | custom-call | flops 4000000000 | bytes 4000000 | tf_op jit(solution)/shard_map/sample_residual/pallas_call | solution.py:283
  28.9 0.0 copy-start.2
  28.9 14.5 %sample_residual.3.s1_ref = f32[1024,128]{1,0:T(8,128)S(1)} custom-call(f32[4096,128]{1,0:T(8,128)S(1)} %bitcast.16, s32[256,16,128]{2,1,0:T(8,128)S(1)} %bitcast.22, f32[16,16,16]{2,1,0:T(8,128)S(1)} %fusion.7.wt_ref, s32[16,1,256]{2,1,0:T(1,128)S(1)} %reshape.31.place_ref, f32[1024,128]{1,0:T(8,128)S(1)} %sample_residual.2.prev_ref), custom_call_target="tpu_custom_call" | custom-call | flops 4000000000 | bytes 4000000 | tf_op jit(solution)/shard_map/sample_residual/pallas_call | solution.py:283
  43.4 0.0 collective-permute-done
  43.4 0.0 copy-done.2
  43.4 0.0 collective-permute-done.1
  43.5 1.3 collective-permute-start.3
  44.8 3.0 %collective-permute-start.2 = (f32[32,8,128]{2,1,0:T(8,128)S(1)}, f32[32,8,128]{2,1,0:T(8,128)S(1)}, u32[]{:S(2)}, u32[]{:S(2)}) collective-permute-start(f32[32,8,128]{2,1,0:T(8,128)S(1)} %get-tuple-element.32), channel_id=1, source_target_pairs={{0,1},{1,2},{2,3},{4,5},{5,6},{6,7},{8,9},{9,10},{10,11},{12,13},{... | collective-permute-start | bytes 393224 | tf_op jit(solution)/shard_map/ppermute | solution.py:248
  47.8 0.1 copy.15.weight_ref
  47.9 0.0 collective-permute-done.3.right_ref
  48.0 0.8 collective-permute-done.2.left_ref
  48.8 0.0 copy-start.4
  48.8 0.0 copy-start.1
  48.8 0.0 copy-start.3
  48.8 64.6 %demigrate_and_sample.1 = (f32[4096,128]{1,0:T(8,128)S(1)}, f32[16,128]{1,0:T(8,128)S(1)}, f32[2,32,8,128]{3,2,1,0:T(8,128)S(1)}, f32[2,32,16,128]{3,2,1,0:T(8,128)S(1)}, f32[2,32,8,128]{3,2,1,0:T(8,128)S(1)}) custom-call(s32[16,16,16]{2,1,0:T(8,128)S(1)} %get-tuple-element.29.col_ref, f32[16,16,16]{2,1,0:T(8,128)S(1)} %copy.15.weight_ref, ...), custom_call_target="tpu_custom_call" | custom-call | flops 20000000000 | bytes 8000000 | tf_op jit(solution)/shard_map/demigrate_and_sample/pallas_call | solution.py:314
  113.4 4.6 %collective-permute-start.4 = (f32[2,32,8,128]{3,2,1,0:T(8,128)S(1)}, f32[2,32,8,128]{3,2,1,0:T(8,128)S(1)}, u32[]{:S(2)}, u32[]{:S(2)}) collective-permute-start(f32[2,32,8,128]{3,2,1,0:T(8,128)S(1)} %get-tuple-element.17), channel_id=1, source_target_pairs={{0,1},{1,2},{2,3},{4,5},{5,6},{6,7},{8,9},{9,10},{10,11},{12,13},{... | collective-permute-start | bytes 786440 | tf_op jit(solution)/shard_map/ppermute | solution.py:248
  117.9 1.3 collective-permute-start.5
  119.2 0.0 collective-permute-done.4.low_ref
  119.2 4.0 %collective-permute-done.5.high_ref = f32[2,32,8,128]{3,2,1,0:T(8,128)S(1)} collective-permute-done((f32[2,32,8,128]{3,2,1,0:T(8,128)S(1)}, f32[2,32,8,128]{3,2,1,0:T(8,128)S(1)}, u32[]{:S(2)}, u32[]{:S(2)}) %collective-permute-start.5) | collective-permute-done | bytes 262176 | tf_op jit(solution)/shard_map/ppermute | solution.py:248
  123.3 0.1 fold_y.1
  123.3 4.3 %collective-permute-start.6 = (f32[2,8,16,128]{3,2,1,0:T(8,128)S(1)}, f32[2,8,16,128]{3,2,1,0:T(8,128)S(1)}, u32[]{:S(2)}, u32[]{:S(2)}) collective-permute-start(f32[2,8,16,128]{3,2,1,0:T(8,128)S(1)} %get-tuple-element.20), channel_id=1, source_target_pairs={{0,4},{4,8},{8,12},{12,16},{16,20},{20,24},{24,28},{1,5},{5,9},{9,... | collective-permute-start | bytes 393224 | tf_op jit(solution)/shard_map/ppermute | solution.py:248
  127.7 1.3 collective-permute-start.7
  129.0 1.2 collective-permute-done.6.low_ref
  130.2 4.4 %collective-permute-done.7.high_ref = f32[2,8,16,128]{3,2,1,0:T(8,128)S(1)} collective-permute-done((f32[2,8,16,128]{3,2,1,0:T(8,128)S(1)}, f32[2,8,16,128]{3,2,1,0:T(8,128)S(1)}, u32[]{:S(2)}, u32[]{:S(2)}) %collective-permute-start.7) | collective-permute-done | bytes 131104 | tf_op jit(solution)/shard_map/ppermute | solution.py:248
  134.5 0.0 copy-done.4
  134.5 0.2 fold_x.1
  134.7 40.6 %all-gather = f32[32,1,128]{2,1,0:T(1,128)S(1)} all-gather(f32[1,1,128]{2,1,0:T(1,128)S(1)} %bitcast.19), channel_id=1, replica_groups=mesh['gx'=8,'gy'=4] {'gx','gy'}, dimensions={0}, use_global_device_ids=true | all-gather | bytes 16896 | tf_op jit(solution)/shard_map/all_gather | solution.py:375
  175.3 0.0 copy-done.1
  175.3 0.0 copy-done.3
  175.3 3.5 %update.1 = (f32[16,16,128]{2,1,0:T(8,128)}, f32[4096,128]{1,0:T(8,128)}, f32[16,16,128]{2,1,0:T(8,128)}) custom-call(f32[32,128]{1,0:T(8,128)S(1)} %bitcast.18, f32[4096,128]{1,0:T(8,128)S(1)} %bitcast.17, f32[4096,128]{1,0:T(8,128)S(1)} %get-tuple-element.24.data_ref, f32[16,16,128]{2,1,0:T(8,128)S(1)} %copy-done.3, f32[16,16,128]{2,1,0:T(8,128)S(1)} %copy-done.2, ...), custom_call_target="tpu_custom_call" | custom-call | tf_op jit(solution)/shard_map/update/pallas_call | solution.py:383
  (8 shorter events, 0.1 us)
Async XLA Ops:
  1.5 41.9 %collective-permute-start.1 = (f32[8,16,128]{2,1,0:T(8,128)S(1)}, f32[8,16,128]{2,1,0:T(8,128)S(1)}, u32[]{:S(2)}, u32[]{:S(2)}) collective-permute-start(f32[8,16,128]{2,1,0:T(8,128)S(1)} %get-tuple-element.33), channel_id=1, source_target_pairs={{4,0},{8,4},{12,8},{16,12},{20,16},{24,20},{28,24},{5,1},{9,5},{13... | collective-permute-start | bytes 196616 | tf_op jit(solution)/shard_map/ppermute | solution.py:248
  2.8 40.6 %collective-permute-start = (f32[8,16,128]{2,1,0:T(8,128)S(1)}, f32[8,16,128]{2,1,0:T(8,128)S(1)}, u32[]{:S(2)}, u32[]{:S(2)}) collective-permute-start(f32[8,16,128]{2,1,0:T(8,128)S(1)} %get-tuple-element.34), channel_id=1, source_target_pairs={{0,4},{4,8},{8,12},{12,16},{16,20},{20,24},{24,28},{1,5},{5,9},{9,... | collective-permute-start | bytes 196616 | tf_op jit(solution)/shard_map/ppermute | solution.py:248
  11.2 1.6 copy-start
  12.8 1.6 copy-start.5
  28.9 14.5 %copy-start.2 = (f32[16,16,128]{2,1,0:T(8,128)S(1)}, f32[16,16,128]{2,1,0:T(8,128)}, u32[]{:S(2)}) copy-start(f32[16,16,128]{2,1,0:T(8,128)} %dir_ref.1) | copy-start | bytes 393220
  43.5 4.5 %collective-permute-start.3 = (f32[32,8,128]{2,1,0:T(8,128)S(1)}, f32[32,8,128]{2,1,0:T(8,128)S(1)}, u32[]{:S(2)}, u32[]{:S(2)}) collective-permute-start(f32[32,8,128]{2,1,0:T(8,128)S(1)} %get-tuple-element.31), channel_id=1, source_target_pairs={{1,0},{2,1},{3,2},{5,4},{6,5},{7,6},{9,8},{10,9},{11,10},{13,12},{... | collective-permute-start | bytes 393224 | tf_op jit(solution)/shard_map/ppermute | solution.py:248
  44.8 4.0 %collective-permute-start.2 = (f32[32,8,128]{2,1,0:T(8,128)S(1)}, f32[32,8,128]{2,1,0:T(8,128)S(1)}, u32[]{:S(2)}, u32[]{:S(2)}) collective-permute-start(f32[32,8,128]{2,1,0:T(8,128)S(1)} %get-tuple-element.32), channel_id=1, source_target_pairs={{0,1},{1,2},{2,3},{4,5},{5,6},{6,7},{8,9},{9,10},{10,11},{12,13},{... | collective-permute-start | bytes 393224 | tf_op jit(solution)/shard_map/ppermute | solution.py:248
  48.8 85.7 %copy-start.4 = (f32[16,16,128]{2,1,0:T(8,128)S(1)}, f32[16,16,128]{2,1,0:T(8,128)}, u32[]{:S(2)}) copy-start(f32[16,16,128]{2,1,0:T(8,128)} %grad_ref.1) | copy-start | bytes 393220
  48.8 126.5 %copy-start.1 = (f32[16,16,2048]{2,1,0:T(8,128)S(1)}, f32[16,16,2048]{2,1,0:T(8,128)}, u32[]{:S(2)}) copy-start(f32[16,16,2048]{2,1,0:T(8,128)} %param.9) | copy-start | bytes 6291460
  48.8 126.5 %copy-start.3 = (f32[16,16,128]{2,1,0:T(8,128)S(1)}, f32[16,16,128]{2,1,0:T(8,128)}, u32[]{:S(2)}) copy-start(f32[16,16,128]{2,1,0:T(8,128)} %model_ref.1) | copy-start | bytes 393220
  113.4 5.9 %collective-permute-start.4 = (f32[2,32,8,128]{3,2,1,0:T(8,128)S(1)}, f32[2,32,8,128]{3,2,1,0:T(8,128)S(1)}, u32[]{:S(2)}, u32[]{:S(2)}) collective-permute-start(f32[2,32,8,128]{3,2,1,0:T(8,128)S(1)} %get-tuple-element.17), channel_id=1, source_target_pairs={{0,1},{1,2},{2,3},{4,5},{5,6},{6,7},{8,9},{9,10},{10,11},{12,13},{... | collective-permute-start | bytes 786440 | tf_op jit(solution)/shard_map/ppermute | solution.py:248
  117.9 5.3 %collective-permute-start.5 = (f32[2,32,8,128]{3,2,1,0:T(8,128)S(1)}, f32[2,32,8,128]{3,2,1,0:T(8,128)S(1)}, u32[]{:S(2)}, u32[]{:S(2)}) collective-permute-start(f32[2,32,8,128]{3,2,1,0:T(8,128)S(1)} %get-tuple-element.18), channel_id=1, source_target_pairs={{1,0},{2,1},{3,2},{5,4},{6,5},{7,6},{9,8},{10,9},{11,10},{13,12},{... | collective-permute-start | bytes 786440 | tf_op jit(solution)/shard_map/ppermute | solution.py:248
  123.3 6.8 %collective-permute-start.6 = (f32[2,8,16,128]{3,2,1,0:T(8,128)S(1)}, f32[2,8,16,128]{3,2,1,0:T(8,128)S(1)}, u32[]{:S(2)}, u32[]{:S(2)}) collective-permute-start(f32[2,8,16,128]{3,2,1,0:T(8,128)S(1)} %get-tuple-element.20), channel_id=1, source_target_pairs={{0,4},{4,8},{8,12},{12,16},{16,20},{20,24},{24,28},{1,5},{5,9},{9,... | collective-permute-start | bytes 393224 | tf_op jit(solution)/shard_map/ppermute | solution.py:248
  127.7 6.9 %collective-permute-start.7 = (f32[2,8,16,128]{3,2,1,0:T(8,128)S(1)}, f32[2,8,16,128]{3,2,1,0:T(8,128)S(1)}, u32[]{:S(2)}, u32[]{:S(2)}) collective-permute-start(f32[2,8,16,128]{3,2,1,0:T(8,128)S(1)} %get-tuple-element.21), channel_id=1, source_target_pairs={{4,0},{8,4},{12,8},{16,12},{20,16},{24,20},{28,24},{5,1},{9,5},{13... | collective-permute-start | bytes 393224 | tf_op jit(solution)/shard_map/ppermute | solution.py:248
where the time goes:
time: 179 us
  Pallas kernels  97.3 us (54%)
  blocking collectives  40.6 us (23%)
  starting transfers between devices  22.6 us (13%)
  waiting for transfers between devices  10.4 us (6%)
  local copies, waits for them, and re-layouts  5.35 us (3%)
  other arithmetic  1.79 us (1%)
    pallas_call x1, Pallas kernels, body(): pl.pallas_call(functools.partial(main_kernel, geo, unroll), grid=(bins_x,...  64.6 us
    all_gather x1, blocking collectives, body(): stats = lax.all_gather(stats, ('gx', 'gy'), axis=0, tiled=True)  40.6 us
    pallas_call x2, Pallas kernels, first(): pl.pallas_call(functools.partial(first_kernel, geo, row0), grid=(count,),...  28.9 us
    ppermute x8, starting transfers between devices, shift(): return lax.ppermute(cells, axis, pairs)  22.6 us
    ppermute x8, waiting for transfers between devices, shift(): return lax.ppermute(cells, axis, pairs)  10.4 us
    unnamed x15, local copies, waits for them, and re-layouts  4.21 us
  transfers between devices with their start and end apart: 8, of which 4 were waited for; matrix products, arithmetic and copies ran while one was open for 2% of the time, Pallas kernels for 16%

commit v1 on v0

--- a/solution.py
+++ b/solution.py
@@ -38,17 +38,18 @@
 
 def sample_row(res_ref, times_ref, wt_ref, vals, bins_y, entries, highs):
     for b in range(bins_y):
-        times = times_ref[b]
-        high = times // LANES
-        low = times % LANES
-        acc = jnp.zeros(times.shape, F32)
         first = trace_row(b, highs)
-        for h in range(highs):
-            row = res_ref[pl.ds(first + SUB * h, 1), :]
-            table = jnp.broadcast_to(row, times.shape)
-            got = jnp.take_along_axis(table, low, axis=1, mode="promise_in_bounds")
-            acc = jnp.where(high == h, got, acc)
-        vals[pl.ds(b * entries, entries), :] = acc * wt_ref[0][:, b : b + 1]
+        for part in range(0, entries, SUB):
+            times = times_ref[b, pl.ds(part, SUB), :]
+            high = jnp.right_shift(times, LANES.bit_length() - 1)
+            low = jnp.bitwise_and(times, LANES - 1)
+            acc = jnp.zeros(times.shape, F32)
+            for h in range(highs):
+                table = res_ref[pl.ds(first + SUB * h, SUB, stride=0), :]
+                got = jnp.take_along_axis(table, low, axis=1, mode="promise_in_bounds")
+                acc = jnp.where(high == h, got, acc)
+            scale = wt_ref[0][part : part + SUB, b : b + 1]
+            vals[pl.ds(b * entries + part, SUB), :] = acc * scale
 
 
 def spread_row(vals, place_ref, s_ref, row, wide_y, span):
@@ -114,8 +115,10 @@
             image[pl.ds(x * wide_y + RADIUS + bins_y, RADIUS), :] = right_ref[x]
 
     half = LANES // 2
-    iota_lo = lax.broadcasted_iota(jnp.int32, (half, LANES), 0).astype(F32).astype(BF16)
-    iota_hi = lax.broadcasted_iota(jnp.int32, (2 * highs, LANES), 0).astype(F32).astype(BF16)
+    half_bits = half.bit_length() - 1
+    iota16 = lax.broadcasted_iota(jnp.int32, (16, LANES), 0)
+    iota_lo = [(iota16 + k).astype(F32).astype(BF16) for k in range(0, half, 16)]
+    iota_hi = [(iota16 + k).astype(F32).astype(BF16) for k in range(0, 2 * highs, 16)]
     zero = jnp.zeros((), BF16)
     one = jnp.ones((), BF16)
 
@@ -128,29 +131,24 @@
         work[slot, 0] = upper
         work[slot, 1] = value - upper
         times = times_ref[b]
-        work[slot, 2] = (times % half).astype(F32)
-        work[slot, 3] = (times // LANES + ((times // half) % 2) * highs).astype(F32)
+        work[slot, 2] = jnp.bitwise_and(times, half - 1).astype(F32)
+        middle = jnp.bitwise_and(jnp.right_shift(times, half_bits), 1)
+        work[slot, 3] = (jnp.right_shift(times, half_bits + 1) + middle * highs).astype(F32)
         lefts = []
         rights = []
         for e in range(entries):
 
-            def wide(k, rows):
-                row = work[slot, k, pl.ds(e, 1), :]
-                return jnp.broadcast_to(
-                    jnp.broadcast_to(row, (16, LANES)).astype(BF16)[None], (rows // 16, 16, LANES)
-                ).reshape(rows, LANES)
-
-            hit = wide(3, 2 * highs) == iota_hi
-            lefts.append(
-                jnp.concatenate(
-                    [
-                        jnp.where(hit, wide(0, 2 * highs), zero),
-                        jnp.where(hit, wide(1, 2 * highs), zero),
-                    ],
-                    axis=0,
-                )
+            def wide(k):
+                return work[slot, k, pl.ds(e, 16, stride=0), :].astype(BF16)
+
+            place = wide(3)
+            hits = [place == iota for iota in iota_hi]
+            parts = [jnp.where(hit, wide(k), zero) for k in range(2) for hit in hits]
+            lefts.append(jnp.concatenate(parts, axis=0))
+            low = wide(2)
+            rights.append(
+                jnp.concatenate([jnp.where(low == iota, one, zero) for iota in iota_lo], axis=0)
             )
-            rights.append(jnp.where(wide(2, half) == iota_lo, one, zero))
         out = lax.dot_general(
             jnp.concatenate(lefts, axis=1),
             jnp.concatenate(rights, axis=1),
@@ -372,7 +370,9 @@
         compiler_params=params(),
         name="fold_x",
     )(inner, from_low, from_high, old_gradient, curv)
-    stats = lax.all_gather(stats, ("gx", "gy"), axis=0, tiled=True)
+    devices = lax.axis_size("gx") * lax.axis_size("gy")
+    stats = jnp.broadcast_to(stats[:, None], (devices, 1, LANES))
+    stats = lax.all_to_all(stats, ("gx", "gy"), 0, 0, tiled=True).reshape(devices, LANES)
 
     steps = 8
     rows_step = bins_x * rows_per // steps

time: 179 us -> 145 us (0.81)
  blocking collectives: 40.6 us -> 14.8 us
  Pallas kernels: 97.3 us -> 88.7 us
    all_gather x1 -> x0, blocking collectives: 40.6 us -> none  [body(): stats = lax.all_gather(stats, ('gx', 'gy'), axis=0, tiled=True)]
    all_to_all x0 -> x1, blocking collectives: none -> 14.8 us  [body(): lax.all_to_all(stats, ('gx', 'gy'), 0, 0, tiled=True)]
    pallas_call x1, Pallas kernels: 64.6 us -> 60.1 us  [body(): pl.pallas_call(functools.partial(main_kernel, geo, unroll), grid=(bins_x,...]
    pallas_call x2, Pallas kernels: 28.9 us -> 24.8 us  [first(): pl.pallas_call(functools.partial(first_kernel, geo, row0), grid=(count,),...]
  transfers between devices with their start and end apart: 8 -> 8, of which waited for: 4 -> 4; matrix products, arithmetic and copies ran while one was open for 2% -> 2% of each run, Pallas kernels for 16% -> 17%
where the time goes in v1:
time: 145 us; the launch traced here: 144 us
  Pallas kernels  88.7 us (61%)
  starting transfers between devices  22.5 us (16%)
  blocking collectives  14.8 us (10%)
  waiting for transfers between devices  10.5 us (7%)
  local copies, waits for them, and re-layouts  5.36 us (4%)
  other arithmetic  1.79 us (1%)
    pallas_call x1, Pallas kernels, body(): pl.pallas_call(functools.partial(main_kernel, geo, unroll), grid=(bins_x,...  60.1 us
    pallas_call x2, Pallas kernels, first(): pl.pallas_call(functools.partial(first_kernel, geo, row0), grid=(count,),...  24.8 us
    ppermute x8, starting transfers between devices, shift(): return lax.ppermute(cells, axis, pairs)  22.5 us
    all_to_all x1, blocking collectives, body(): lax.all_to_all(stats, ('gx', 'gy'), 0, 0, tiled=True)  14.8 us
    ppermute x8, waiting for transfers between devices, shift(): return lax.ppermute(cells, axis, pairs)  10.5 us
    unnamed x15, local copies, waits for them, and re-layouts  4.21 us
    pallas_call x1, Pallas kernels, body(): pl.pallas_call(last_kernel, grid=(steps,), in_specs=[pl.BlockSpec(stats.s...  3.54 us
  transfers between devices with their start and end apart: 8, of which 4 were waited for; matrix products, arithmetic and copies ran while one was open for 2% of the time, Pallas kernels for 17%

profile of v1, /device:TPU:0, one launch (start us, length us, event | category | flops | bytes accessed | tf_op | source)
XLA Modules:
  0.0 144.5 jit_solution(12452959144549254689)
XLA Ops:
  0.6 0.9 fusion.6
  1.5 1.3 collective-permute-start.1
  2.8 5.5 %collective-permute-start = (f32[8,16,128]{2,1,0:T(8,128)S(1)}, f32[8,16,128]{2,1,0:T(8,128)S(1)}, u32[]{:S(2)}, u32[]{:S(2)}) collective-permute-start(f32[8,16,128]{2,1,0:T(8,128)S(1)} %get-tuple-element.34), channel_id=1, source_target_pairs={{0,4},{4,8},{8,12},{12,16},{16,20},{20,24},{24,28},{1,5},{5,9},{9,... | collective-permute-start | bytes 196616 | tf_op jit(solution)/shard_map/ppermute | solution.py:246
  8.3 0.7 convert_element_type.3
  9.0 1.0 copy.13
  10.0 1.1 broadcast_add_fusion
  11.1 0.1 reshape.37.place_ref
  11.2 0.0 copy-start
  11.3 1.6 %copy-done = f32[16,16,2048]{2,1,0:T(8,128)S(1)} copy-done((f32[16,16,2048]{2,1,0:T(8,128)S(1)}, f32[16,16,2048]{2,1,0:T(8,128)}, u32[]{:S(2)}) %copy-start) | copy-done | bytes 2097176
  12.8 0.0 copy-start.5
  12.8 1.6 %copy-done.5 = s32[16,16,16,128]{3,2,1,0:T(8,128)S(1)} copy-done((s32[16,16,16,128]{3,2,1,0:T(8,128)S(1)}, s32[16,16,16,128]{3,2,1,0:T(8,128)}, u32[]{:S(2)}) %copy-start.5) | copy-done | bytes 2097176
  14.4 12.4 %sample_residual.2.prev_ref = f32[1024,128]{1,0:T(8,128)S(1)} custom-call(f32[4096,128]{1,0:T(8,128)S(1)} %bitcast.15, s32[256,16,128]{2,1,0:T(8,128)S(1)} %bitcast.21, f32[16,16,16]{2,1,0:T(8,128)S(1)} %fusion.7.wt_ref, s32[16,1,256]{2,1,0:T(1,128)S(1)} %reshape.37.place_ref, f32[1024,128]{1,0:T(8,128)S(1)} %broadcast_in_dim.6.prev_ref), custom_call_target="tpu_custom_call" | custom-call | flops 4000000000 | bytes 4000000 | tf_op jit(solution)/shard_map/sample_residual/pallas_call | solution.py:281
  26.8 0.0 copy-start.2
  26.8 12.4 %sample_residual.3.s1_ref = f32[1024,128]{1,0:T(8,128)S(1)} custom-call(f32[4096,128]{1,0:T(8,128)S(1)} %bitcast.16, s32[256,16,128]{2,1,0:T(8,128)S(1)} %bitcast.22, f32[16,16,16]{2,1,0:T(8,128)S(1)} %fusion.7.wt_ref, s32[16,1,256]{2,1,0:T(1,128)S(1)} %reshape.37.place_ref, f32[1024,128]{1,0:T(8,128)S(1)} %sample_residual.2.prev_ref), custom_call_target="tpu_custom_call" | custom-call | flops 4000000000 | bytes 4000000 | tf_op jit(solution)/shard_map/sample_residual/pallas_call | solution.py:281
  39.2 0.0 collective-permute-done
  39.2 0.0 copy-done.2
  39.3 0.0 collective-permute-done.1
  39.3 1.3 collective-permute-start.3
  40.6 3.0 %collective-permute-start.2 = (f32[32,8,128]{2,1,0:T(8,128)S(1)}, f32[32,8,128]{2,1,0:T(8,128)S(1)}, u32[]{:S(2)}, u32[]{:S(2)}) collective-permute-start(f32[32,8,128]{2,1,0:T(8,128)S(1)} %get-tuple-element.32), channel_id=1, source_target_pairs={{0,1},{1,2},{2,3},{4,5},{5,6},{6,7},{8,9},{9,10},{10,11},{12,13},{... | collective-permute-start | bytes 393224 | tf_op jit(solution)/shard_map/ppermute | solution.py:246
  43.7 0.1 copy.14.weight_ref
  43.8 0.0 collective-permute-done.3.right_ref
  43.8 0.8 collective-permute-done.2.left_ref
  44.6 0.0 copy-start.4
  44.6 0.0 copy-start.1
  44.6 0.0 copy-start.3
  44.6 60.1 %demigrate_and_sample.1 = (f32[4096,128]{1,0:T(8,128)S(1)}, f32[16,128]{1,0:T(8,128)S(1)}, f32[2,32,8,128]{3,2,1,0:T(8,128)S(1)}, f32[2,32,16,128]{3,2,1,0:T(8,128)S(1)}, f32[2,32,8,128]{3,2,1,0:T(8,128)S(1)}) custom-call(s32[16,16,16]{2,1,0:T(8,128)S(1)} %get-tuple-element.29.col_ref, f32[16,16,16]{2,1,0:T(8,128)S(1)} %copy.14.weight_ref, ...), custom_call_target="tpu_custom_call" | custom-call | flops 20000000000 | bytes 8000000 | tf_op jit(solution)/shard_map/demigrate_and_sample/pallas_call | solution.py:312
  104.8 4.5 %collective-permute-start.4 = (f32[2,32,8,128]{3,2,1,0:T(8,128)S(1)}, f32[2,32,8,128]{3,2,1,0:T(8,128)S(1)}, u32[]{:S(2)}, u32[]{:S(2)}) collective-permute-start(f32[2,32,8,128]{3,2,1,0:T(8,128)S(1)} %get-tuple-element.17), channel_id=1, source_target_pairs={{0,1},{1,2},{2,3},{4,5},{5,6},{6,7},{8,9},{9,10},{10,11},{12,13},{... | collective-permute-start | bytes 786440 | tf_op jit(solution)/shard_map/ppermute | solution.py:246
  109.3 1.3 collective-permute-start.5
  110.6 0.0 collective-permute-done.4.low_ref
  110.6 4.1 %collective-permute-done.5.high_ref = f32[2,32,8,128]{3,2,1,0:T(8,128)S(1)} collective-permute-done((f32[2,32,8,128]{3,2,1,0:T(8,128)S(1)}, f32[2,32,8,128]{3,2,1,0:T(8,128)S(1)}, u32[]{:S(2)}, u32[]{:S(2)}) %collective-permute-start.5) | collective-permute-done | bytes 262176 | tf_op jit(solution)/shard_map/ppermute | solution.py:246
  114.7 0.1 fold_y.1
  114.8 4.3 %collective-permute-start.6 = (f32[2,8,16,128]{3,2,1,0:T(8,128)S(1)}, f32[2,8,16,128]{3,2,1,0:T(8,128)S(1)}, u32[]{:S(2)}, u32[]{:S(2)}) collective-permute-start(f32[2,8,16,128]{3,2,1,0:T(8,128)S(1)} %get-tuple-element.20), channel_id=1, source_target_pairs={{0,4},{4,8},{8,12},{12,16},{16,20},{20,24},{24,28},{1,5},{5,9},{9,... | collective-permute-start | bytes 393224 | tf_op jit(solution)/shard_map/ppermute | solution.py:246
  119.1 1.3 collective-permute-start.7
  120.4 1.2 collective-permute-done.6.low_ref
  121.5 4.4 %collective-permute-done.7.high_ref = f32[2,8,16,128]{3,2,1,0:T(8,128)S(1)} collective-permute-done((f32[2,8,16,128]{3,2,1,0:T(8,128)S(1)}, f32[2,8,16,128]{3,2,1,0:T(8,128)S(1)}, u32[]{:S(2)}, u32[]{:S(2)}) %collective-permute-start.7) | collective-permute-done | bytes 131104 | tf_op jit(solution)/shard_map/ppermute | solution.py:246
  125.9 0.0 copy-done.4
  125.9 0.2 fold_x.1
  126.1 14.8 %all_to_all.5 = f32[32,1,128]{2,1,0:T(1,128)S(1)} all-to-all(f32[32,1,128]{2,1,0:T(1,128)S(1)} %broadcast_in_dim.16), channel_id=1, replica_groups=mesh['gx'=8,'gy'=4] {'gx','gy'}, dimensions={0} | all-to-all | bytes 32768 | tf_op jit(solution)/shard_map/all_to_all | solution.py:375
  141.0 0.0 copy-done.1
  141.0 0.0 copy-done.3
  141.0 3.5 %update.1 = (f32[16,16,128]{2,1,0:T(8,128)}, f32[4096,128]{1,0:T(8,128)}, f32[16,16,128]{2,1,0:T(8,128)}) custom-call(f32[32,128]{1,0:T(8,128)S(1)} %bitcast.18, f32[4096,128]{1,0:T(8,128)S(1)} %bitcast.17, f32[4096,128]{1,0:T(8,128)S(1)} %get-tuple-element.24.data_ref, f32[16,16,128]{2,1,0:T(8,128)S(1)} %copy-done.3, f32[16,16,128]{2,1,0:T(8,128)S(1)} %copy-done.2, ...), custom_call_target="tpu_custom_call" | custom-call | tf_op jit(solution)/shard_map/update/pallas_call | solution.py:383
  (9 shorter events, 0.1 us)
Async XLA Ops:
  1.5 37.8 %collective-permute-start.1 = (f32[8,16,128]{2,1,0:T(8,128)S(1)}, f32[8,16,128]{2,1,0:T(8,128)S(1)}, u32[]{:S(2)}, u32[]{:S(2)}) collective-permute-start(f32[8,16,128]{2,1,0:T(8,128)S(1)} %get-tuple-element.33), channel_id=1, source_target_pairs={{4,0},{8,4},{12,8},{16,12},{20,16},{24,20},{28,24},{5,1},{9,5},{13... | collective-permute-start | bytes 196616 | tf_op jit(solution)/shard_map/ppermute | solution.py:246
  2.8 36.4 %collective-permute-start = (f32[8,16,128]{2,1,0:T(8,128)S(1)}, f32[8,16,128]{2,1,0:T(8,128)S(1)}, u32[]{:S(2)}, u32[]{:S(2)}) collective-permute-start(f32[8,16,128]{2,1,0:T(8,128)S(1)} %get-tuple-element.34), channel_id=1, source_target_pairs={{0,4},{4,8},{8,12},{12,16},{16,20},{20,24},{24,28},{1,5},{5,9},{9,... | collective-permute-start | bytes 196616 | tf_op jit(solution)/shard_map/ppermute | solution.py:246
  11.2 1.6 %copy-start = (f32[16,16,2048]{2,1,0:T(8,128)S(1)}, f32[16,16,2048]{2,1,0:T(8,128)}, u32[]{:S(2)}) copy-start(f32[16,16,2048]{2,1,0:T(8,128)} %param.9) | copy-start | bytes 6291460
  12.8 1.6 %copy-start.5 = (s32[16,16,16,128]{3,2,1,0:T(8,128)S(1)}, s32[16,16,16,128]{3,2,1,0:T(8,128)}, u32[]{:S(2)}) copy-start(s32[16,16,16,128]{3,2,1,0:T(8,128)} %param.13) | copy-start | bytes 6291460
  26.8 12.4 %copy-start.2 = (f32[16,16,128]{2,1,0:T(8,128)S(1)}, f32[16,16,128]{2,1,0:T(8,128)}, u32[]{:S(2)}) copy-start(f32[16,16,128]{2,1,0:T(8,128)} %dir_ref.1) | copy-start | bytes 393220
  39.3 4.5 %collective-permute-start.3 = (f32[32,8,128]{2,1,0:T(8,128)S(1)}, f32[32,8,128]{2,1,0:T(8,128)S(1)}, u32[]{:S(2)}, u32[]{:S(2)}) collective-permute-start(f32[32,8,128]{2,1,0:T(8,128)S(1)} %get-tuple-element.31), channel_id=1, source_target_pairs={{1,0},{2,1},{3,2},{5,4},{6,5},{7,6},{9,8},{10,9},{11,10},{13,12},{... | collective-permute-start | bytes 393224 | tf_op jit(solution)/shard_map/ppermute | solution.py:246
  40.6 4.0 %collective-permute-start.2 = (f32[32,8,128]{2,1,0:T(8,128)S(1)}, f32[32,8,128]{2,1,0:T(8,128)S(1)}, u32[]{:S(2)}, u32[]{:S(2)}) collective-permute-start(f32[32,8,128]{2,1,0:T(8,128)S(1)} %get-tuple-element.32), channel_id=1, source_target_pairs={{0,1},{1,2},{2,3},{4,5},{5,6},{6,7},{8,9},{9,10},{10,11},{12,13},{... | collective-permute-start | bytes 393224 | tf_op jit(solution)/shard_map/ppermute | solution.py:246
  44.6 81.3 %copy-start.4 = (f32[16,16,128]{2,1,0:T(8,128)S(1)}, f32[16,16,128]{2,1,0:T(8,128)}, u32[]{:S(2)}) copy-start(f32[16,16,128]{2,1,0:T(8,128)} %grad_ref.1) | copy-start | bytes 393220
  44.6 96.3 %copy-start.1 = (f32[16,16,2048]{2,1,0:T(8,128)S(1)}, f32[16,16,2048]{2,1,0:T(8,128)}, u32[]{:S(2)}) copy-start(f32[16,16,2048]{2,1,0:T(8,128)} %param.9) | copy-start | bytes 6291460
  44.6 96.3 %copy-start.3 = (f32[16,16,128]{2,1,0:T(8,128)S(1)}, f32[16,16,128]{2,1,0:T(8,128)}, u32[]{:S(2)}) copy-start(f32[16,16,128]{2,1,0:T(8,128)} %model_ref.1) | copy-start | bytes 393220
  104.8 5.8 %collective-permute-start.4 = (f32[2,32,8,128]{3,2,1,0:T(8,128)S(1)}, f32[2,32,8,128]{3,2,1,0:T(8,128)S(1)}, u32[]{:S(2)}, u32[]{:S(2)}) collective-permute-start(f32[2,32,8,128]{3,2,1,0:T(8,128)S(1)} %get-tuple-element.17), channel_id=1, source_target_pairs={{0,1},{1,2},{2,3},{4,5},{5,6},{6,7},{8,9},{9,10},{10,11},{12,13},{... | collective-permute-start | bytes 786440 | tf_op jit(solution)/shard_map/ppermute | solution.py:246
  109.3 5.4 %collective-permute-start.5 = (f32[2,32,8,128]{3,2,1,0:T(8,128)S(1)}, f32[2,32,8,128]{3,2,1,0:T(8,128)S(1)}, u32[]{:S(2)}, u32[]{:S(2)}) collective-permute-start(f32[2,32,8,128]{3,2,1,0:T(8,128)S(1)} %get-tuple-element.18), channel_id=1, source_target_pairs={{1,0},{2,1},{3,2},{5,4},{6,5},{7,6},{9,8},{10,9},{11,10},{13,12},{... | collective-permute-start | bytes 786440 | tf_op jit(solution)/shard_map/ppermute | solution.py:246
  114.8 6.8 %collective-permute-start.6 = (f32[2,8,16,128]{3,2,1,0:T(8,128)S(1)}, f32[2,8,16,128]{3,2,1,0:T(8,128)S(1)}, u32[]{:S(2)}, u32[]{:S(2)}) collective-permute-start(f32[2,8,16,128]{3,2,1,0:T(8,128)S(1)} %get-tuple-element.20), channel_id=1, source_target_pairs={{0,4},{4,8},{8,12},{12,16},{16,20},{20,24},{24,28},{1,5},{5,9},{9,... | collective-permute-start | bytes 393224 | tf_op jit(solution)/shard_map/ppermute | solution.py:246
  119.1 6.9 %collective-permute-start.7 = (f32[2,8,16,128]{3,2,1,0:T(8,128)S(1)}, f32[2,8,16,128]{3,2,1,0:T(8,128)S(1)}, u32[]{:S(2)}, u32[]{:S(2)}) collective-permute-start(f32[2,8,16,128]{3,2,1,0:T(8,128)S(1)} %get-tuple-element.21), channel_id=1, source_target_pairs={{4,0},{8,4},{12,8},{16,12},{20,16},{24,20},{28,24},{5,1},{9,5},{13... | collective-permute-start | bytes 393224 | tf_op jit(solution)/shard_map/ppermute | solution.py:246

commit v2 on v1

--- a/solution.py
+++ b/solution.py
@@ -13,11 +13,12 @@
 SUB = 8
 F32 = jnp.float32
 BF16 = jnp.bfloat16
-VMEM_LIMIT = 48 * 1024 * 1024
-
-
-def params(**extra):
-    return pltpu.CompilerParams(vmem_limit_bytes=VMEM_LIMIT, **extra)
+VMEM_LIMIT = 51 * 1024 * 1024
+SMALL_LIMIT = 24 * 1024 * 1024
+
+
+def params(limit=VMEM_LIMIT):
+    return pltpu.CompilerParams(vmem_limit_bytes=limit)
 
 
 def to_rows(traces):
@@ -36,7 +37,14 @@
     return (b // SUB) * (SUB * highs) + b % SUB
 
 
-def sample_row(res_ref, times_ref, wt_ref, vals, bins_y, entries, highs):
+def fill_weights(amp_ref, counts_ref, scales, bins_y, entries, row):
+    weight = amp_ref[0].T * counts_ref[pl.ds(row, 1), :].astype(F32)
+    for b in range(bins_y):
+        column = jnp.broadcast_to(weight[:, b : b + 1], (entries, LANES))
+        scales[pl.ds(b * entries, entries), :] = column
+
+
+def sample_row(res_ref, times_ref, scales, vals, bins_y, entries, highs):
     for b in range(bins_y):
         first = trace_row(b, highs)
         for part in range(0, entries, SUB):
@@ -48,8 +56,8 @@
                 table = res_ref[pl.ds(first + SUB * h, SUB, stride=0), :]
                 got = jnp.take_along_axis(table, low, axis=1, mode="promise_in_bounds")
                 acc = jnp.where(high == h, got, acc)
-            scale = wt_ref[0][part : part + SUB, b : b + 1]
-            vals[pl.ds(b * entries + part, SUB), :] = acc * scale
+            at = pl.ds(b * entries + part, SUB)
+            vals[at, :] = acc * scales[at, :]
 
 
 def spread_row(vals, place_ref, s_ref, row, wide_y, span):
@@ -58,16 +66,15 @@
     lower = (value - upper.astype(F32)).astype(BF16)
     both = jnp.concatenate([upper, lower], axis=1)
     place = place_ref[0]
-    step = 32
-    for m in range(0, span, step):
-        iota = lax.broadcasted_iota(jnp.int32, (step, place.shape[1]), 0) + m
-        table = jnp.where(iota == place, 1.0, 0.0).astype(BF16)
-        part = jnp.dot(table, both, preferred_element_type=F32)
-        at = pl.ds(pl.multiple_of(row * wide_y + m, SUB), step)
-        s_ref[at, :] += part[:, :LANES] + part[:, LANES:]
-
-
-def first_kernel(geo, row0, res_ref, times_ref, wt_ref, place_ref, prev_ref, s_ref, vals):
+    iota = lax.broadcasted_iota(jnp.int32, (span, place.shape[1]), 0)
+    table = jnp.where(iota == place, 1.0, 0.0).astype(BF16)
+    part = jnp.dot(table, both, preferred_element_type=F32)
+    s_ref[pl.ds(pl.multiple_of(row * wide_y, SUB), span), :] += part[:, :LANES] + part[:, LANES:]
+
+
+def first_kernel(
+    geo, row0, res_ref, times_ref, amp_ref, counts_ref, place_ref, prev_ref, s_ref, vals, scales
+):
     bins_y, entries, highs, wide_y = geo
     step = pl.program_id(0)
 
@@ -75,7 +82,8 @@
     def _():
         s_ref[...] = prev_ref[...]
 
-    sample_row(res_ref, times_ref, wt_ref, vals, bins_y, entries, highs)
+    fill_weights(amp_ref, counts_ref, scales, bins_y, entries, step + row0)
+    sample_row(res_ref, times_ref, scales, vals, bins_y, entries, highs)
     spread_row(vals, place_ref, s_ref, step + row0, wide_y, SIDE * wide_y)
 
 
@@ -83,9 +91,9 @@
     geo,
     unroll,
     col_ref,
-    weight_ref,
     times_ref,
-    wt_ref,
+    amp_ref,
+    counts_ref,
     place_ref,
     mid_ref,
     left_ref,
@@ -99,6 +107,7 @@
     image,
     s_ref,
     vals,
+    scales,
     work,
 ):
     bins_y, entries, highs, wide_y = geo
@@ -114,6 +123,7 @@
             image[pl.ds(x * wide_y + RADIUS, bins_y), :] = mid_ref[x]
             image[pl.ds(x * wide_y + RADIUS + bins_y, RADIUS), :] = right_ref[x]
 
+    fill_weights(amp_ref, counts_ref, scales, bins_y, entries, step)
     half = LANES // 2
     half_bits = half.bit_length() - 1
     iota16 = lax.broadcasted_iota(jnp.int32, (16, LANES), 0)
@@ -125,8 +135,8 @@
     def one_bin(b, slot):
         for e in range(entries):
             column = col_ref[0, b, e]
-            work[slot, 0, pl.ds(e, 1), :] = image[pl.ds(column, 1), :] * weight_ref[0, b, e]
-        value = work[slot, 0]
+            work[slot, 0, pl.ds(e, 1), :] = image[pl.ds(column, 1), :]
+        value = work[slot, 0] * scales[pl.ds(pl.multiple_of(b * entries, SUB), entries), :]
         upper = value.astype(BF16).astype(F32)
         work[slot, 0] = upper
         work[slot, 1] = value - upper
@@ -167,7 +177,7 @@
 
     total = lax.fori_loop(0, bins_y // unroll, some_bins, jnp.zeros((highs, LANES), F32))
     curv_ref[...] += total
-    sample_row(data_ref, times_ref, wt_ref, vals, bins_y, entries, highs)
+    sample_row(data_ref, times_ref, scales, vals, bins_y, entries, highs)
     spread_row(vals, place_ref, s_ref, step, wide_y, SIDE * wide_y)
 
     @pl.when(step == pl.num_programs(0) - 1)
@@ -218,13 +228,13 @@
     stats = jnp.zeros((1, LANES), F32)
     for n, term in enumerate(sums):
         stats = jnp.where(lane == n, jnp.sum(term, axis=1, keepdims=True), stats)
-    stats_ref[...] = stats
+    stats_ref[...] = jnp.broadcast_to(stats[None], stats_ref.shape)
 
 
 def last_kernel(
     stats_ref, res_ref, data_ref, model_ref, dir_ref, grad_ref, new_image, new_residual, new_dir
 ):
-    stats = jnp.sum(stats_ref[...], axis=0, keepdims=True)
+    stats = jnp.sum(stats_ref[...], axis=0)
     lane = lax.broadcasted_iota(jnp.int32, stats.shape, 1)
 
     def pick(n):
@@ -270,8 +280,6 @@
 
     times = travel_times.reshape(bins_x * bins_y, entries, depths)
     res_rows = to_rows(data_residual)
-    weight = amplitude * trace_counts.astype(F32)[:, :, None]
-    weight_t = weight.transpose(0, 2, 1)
     off = (aperture // SIDE) * wide_y + aperture % SIDE
     window = off + jnp.arange(bins_y, dtype=jnp.int32)[None, :, None]
     column = window + wide_y * jnp.arange(bins_x, dtype=jnp.int32)[:, None, None]
@@ -284,24 +292,26 @@
             in_specs=[
                 pl.BlockSpec((rows_per, LANES), lambda i: (i + row0, 0)),
                 pl.BlockSpec((bins_y, entries, depths), lambda i: (i + row0, 0, 0)),
-                pl.BlockSpec((1, entries, bins_y), lambda i: (i + row0, 0, 0)),
+                pl.BlockSpec((1, bins_y, entries), lambda i: (i + row0, 0, 0)),
+                pl.BlockSpec((bins_x, bins_y), lambda i: (0, 0)),
                 pl.BlockSpec((1, 1, bins_y * entries), lambda i: (i + row0, 0, 0)),
                 pl.BlockSpec((columns, depths), lambda i: (0, 0)),
             ],
             out_specs=pl.BlockSpec((columns, depths), lambda i: (0, 0)),
             out_shape=jax.ShapeDtypeStruct((columns, depths), F32),
-            scratch_shapes=[pltpu.VMEM((bins_y * entries, depths), F32)],
+            scratch_shapes=[pltpu.VMEM((bins_y * entries, depths), F32)] * 2,
             compiler_params=params(),
             cost_estimate=pl.CostEstimate(
                 flops=4 * 10**9, bytes_accessed=4 * 10**6, transcendentals=0
             ),
             name="sample_residual",
-        )(res_rows, times, weight_t, place, prev)
+        )(res_rows, times, amplitude, trace_counts, place, prev)
 
     s1 = first(0, bins_x // 2, jnp.zeros((columns, depths), F32))
     ext = jnp.concatenate([from_prev, direction, from_next], axis=0)
-    left = shift(ext[:, bins_y - RADIUS :], "gy", 1)
-    right = shift(ext[:, :RADIUS], "gy", -1)
+    tail, head, s1 = lax.optimization_barrier((ext[:, bins_y - RADIUS :], ext[:, :RADIUS], s1))
+    left = shift(tail, "gy", 1)
+    right = shift(head, "gy", -1)
     s1 = first(bins_x // 2, bins_x - bins_x // 2, s1)
 
     unroll = 4
@@ -314,9 +324,9 @@
         grid=(bins_x,),
         in_specs=[
             pl.BlockSpec((1, bins_y, entries), lambda i: (i, 0, 0), memory_space=pltpu.SMEM),
-            pl.BlockSpec((1, bins_y, entries), lambda i: (i, 0, 0), memory_space=pltpu.SMEM),
             pl.BlockSpec((bins_y, entries, depths), lambda i: (i, 0, 0)),
-            pl.BlockSpec((1, entries, bins_y), lambda i: (i, 0, 0)),
+            pl.BlockSpec((1, bins_y, entries), lambda i: (i, 0, 0)),
+            pl.BlockSpec((bins_x, bins_y), lambda i: (0, 0)),
             pl.BlockSpec((1, 1, bins_y * entries), lambda i: (i, 0, 0)),
             pl.BlockSpec((wide_x, bins_y, depths), whole3),
             pl.BlockSpec((wide_x, RADIUS, depths), whole3),
@@ -341,6 +351,7 @@
             pltpu.VMEM((columns, depths), F32),
             pltpu.VMEM((columns, depths), F32),
             pltpu.VMEM((bins_y * entries, depths), F32),
+            pltpu.VMEM((bins_y * entries, depths), F32),
             pltpu.VMEM((unroll, 4, entries, LANES), F32),
         ],
         compiler_params=params(),
@@ -348,7 +359,7 @@
             flops=20 * 10**9, bytes_accessed=8 * 10**6, transcendentals=0
         ),
         name="demigrate_and_sample",
-    )(column, weight, times, weight_t, place, ext, left, right, s1)
+    )(column, times, amplitude, trace_counts, place, ext, left, right, s1)
 
     from_low = shift(out_right, "gy", 1)
     from_high = shift(out_left, "gy", -1)
@@ -356,23 +367,22 @@
     out_head, inner, out_tail = pl.pallas_call(
         fold_y_kernel,
         out_shape=[edge, jax.ShapeDtypeStruct((2, bins_x, bins_y, depths), F32), edge],
-        compiler_params=params(),
+        compiler_params=params(SMALL_LIMIT),
         name="fold_y",
     )(out_mid, from_low, from_high)
     from_low = shift(out_tail, "gx", 1)
     from_high = shift(out_head, "gx", -1)
+    devices = lax.axis_size("gx") * lax.axis_size("gy")
     grads, stats = pl.pallas_call(
         fold_x_kernel,
         out_shape=[
             jax.ShapeDtypeStruct((2, bins_x, bins_y, depths), F32),
-            jax.ShapeDtypeStruct((1, LANES), F32),
-        ],
-        compiler_params=params(),
+            jax.ShapeDtypeStruct((devices, 1, LANES), F32),
+        ],
+        compiler_params=params(SMALL_LIMIT),
         name="fold_x",
     )(inner, from_low, from_high, old_gradient, curv)
-    devices = lax.axis_size("gx") * lax.axis_size("gy")
-    stats = jnp.broadcast_to(stats[:, None], (devices, 1, LANES))
-    stats = lax.all_to_all(stats, ("gx", "gy"), 0, 0, tiled=True).reshape(devices, LANES)
+    stats = lax.all_to_all(stats, ("gx", "gy"), 0, 0, tiled=True)
 
     steps = 8
     rows_step = bins_x * rows_per // steps
@@ -384,7 +394,7 @@
         last_kernel,
         grid=(steps,),
         in_specs=[
-            pl.BlockSpec(stats.shape, lambda i: (0, 0)),
+            pl.BlockSpec(stats.shape, lambda i: (0, 0, 0)),
             rows,
             rows,
             cells,
@@ -393,7 +403,7 @@
         ],
         out_specs=[cells, rows, cells],
         out_shape=[image_shape, jax.ShapeDtypeStruct(res_rows.shape, F32), image_shape],
-        compiler_params=params(),
+        compiler_params=params(SMALL_LIMIT),
         name="update",
     )(stats, res_rows, data_rows, model_image, direction, grads)
     return (new_image, from_rows(new_rows, data_residual.shape), new_direction)

time: 145 us -> 134 us (0.924)
  Pallas kernels: 88.7 us -> 81.6 us
  waiting for transfers between devices: 10.5 us -> 8.91 us
    pallas_call x1, Pallas kernels: 60.1 us -> 56.1 us  [body(): pl.pallas_call(functools.partial(main_kernel, geo, unroll), grid=(bins_x,...]
    pallas_call x2, Pallas kernels: 24.8 us -> 21.6 us  [first(): pl.pallas_call(functools.partial(first_kernel, geo, row0), grid=(count,),...]
    ppermute x8, waiting for transfers between devices: 10.5 us -> 8.91 us  [shift(): return lax.ppermute(cells, axis, pairs)]
    unnamed x15 -> x16, local copies, waits for them, and re-layouts: 4.21 us -> 3.23 us
  transfers between devices with their start and end apart: 8 -> 8, of which waited for: 4 -> 3; matrix products, arithmetic and copies ran while one was open for 2% -> 1% of each run, Pallas kernels for 17% -> 16%
where the time goes in v2:
time: 134 us; the launch traced here: 133 us
  Pallas kernels  81.6 us (61%)
  starting transfers between devices  21.6 us (16%)
  blocking collectives  14.8 us (11%)
  waiting for transfers between devices  8.91 us (7%)
  local copies, waits for them, and re-layouts  4.28 us (3%)
    pallas_call x1, Pallas kernels, body(): pl.pallas_call(functools.partial(main_kernel, geo, unroll), grid=(bins_x,...  56.1 us
    pallas_call x2, Pallas kernels, first(): pl.pallas_call(functools.partial(first_kernel, geo, row0), grid=(count,),...  21.6 us
    ppermute x8, starting transfers between devices, shift(): return lax.ppermute(cells, axis, pairs)  21.6 us
    all_to_all x1, blocking collectives, body(): stats = lax.all_to_all(stats, ('gx', 'gy'), 0, 0, tiled=True)  14.8 us
    ppermute x8, waiting for transfers between devices, shift(): return lax.ppermute(cells, axis, pairs)  8.91 us
    pallas_call x1, Pallas kernels, body(): pl.pallas_call(last_kernel, grid=(steps,), in_specs=[pl.BlockSpec(stats.s...  3.62 us
    unnamed x16, local copies, waits for them, and re-layouts  3.23 us
  transfers between devices with their start and end apart: 8, of which 3 were waited for; matrix products, arithmetic and copies ran while one was open for 1% of the time, Pallas kernels for 16%

profile of v2, /device:TPU:0, one launch (start us, length us, event | category | flops | bytes accessed | tf_op | source)
XLA Modules:
  0.0 133.1 jit_solution(17012817468043925503)
XLA Ops:
  0.6 0.9 fusion.6
  1.5 1.3 collective-permute-start.1
  2.8 5.5 %collective-permute-start = (f32[8,16,128]{2,1,0:T(8,128)S(1)}, f32[8,16,128]{2,1,0:T(8,128)S(1)}, u32[]{:S(2)}, u32[]{:S(2)}) collective-permute-start(f32[8,16,128]{2,1,0:T(8,128)S(1)} %get-tuple-element.40), channel_id=1, source_target_pairs={{0,4},{4,8},{8,12},{12,16},{16,20},{20,24},{24,28},{1,5},{5,9},{9,... | collective-permute-start | bytes 196616 | tf_op jit(solution)/shard_map/ppermute | solution.py:256
  8.3 1.1 broadcast_add_fusion
  9.4 0.1 reshape.30.place_ref
  9.5 0.0 copy-start.5
  9.5 0.9 copy-done.5
  10.4 0.0 copy-start.6
  10.4 0.7 copy-done.6
  11.1 0.0 copy-start.2
  11.1 10.8 %sample_residual.2.prev_ref = f32[1024,128]{1,0:T(8,128)S(1)} custom-call(f32[4096,128]{1,0:T(8,128)} %bitcast.11, s32[256,16,128]{2,1,0:T(8,128)} %bitcast.14, f32[16,16,16]{2,1,0:T(8,128)S(1)} %copy-done.5, s32[16,16]{1,0:T(8,128)S(1)} %copy-done.6, s32[16,1,256]{2,1,0:T(1,128)S(1)} %reshape.30.place_ref, f32[1024,128]{1,0:T(8,128)S(1)} %broadcast_in_dim.2.prev_ref), custom_call_target="tpu_custom_call" | custom-call | flops 4000000000 | bytes 4000000 | tf_op jit(solution)/shard_map/sample_residual/pallas_call | solution.py:289
  22.0 0.0 collective-permute-done
  22.0 0.0 copy-done.2
  22.0 0.0 collective-permute-done.1
  22.1 1.5 %collective-permute-start.2 = (f32[32,8,128]{2,1,0:T(8,128)S(1)}, f32[32,8,128]{2,1,0:T(8,128)S(1)}, u32[]{:S(2)}, u32[]{:S(2)}) collective-permute-start(f32[32,8,128]{2,1,0:T(8,128)S(1)} %get-tuple-element.19), channel_id=1, source_target_pairs={{0,1},{1,2},{2,3},{4,5},{5,6},{6,7},{8,9},{9,10},{10,11},{12,13},{... | collective-permute-start | bytes 393224 | tf_op jit(solution)/shard_map/ppermute | solution.py:256
  23.5 1.3 collective-permute-start.3
  24.8 10.8 %sample_residual.3.s1_ref = f32[1024,128]{1,0:T(8,128)S(1)} custom-call(f32[4096,128]{1,0:T(8,128)} %bitcast.12, s32[256,16,128]{2,1,0:T(8,128)} %bitcast.15, f32[16,16,16]{2,1,0:T(8,128)S(1)} %copy-done.5, s32[16,16]{1,0:T(8,128)S(1)} %copy-done.6, s32[16,1,256]{2,1,0:T(1,128)S(1)} %reshape.30.place_ref, f32[1024,128]{1,0:T(8,128)S(1)} %sample_residual.2.prev_ref), custom_call_target="tpu_custom_call" | custom-call | flops 4000000000 | bytes 4000000 | tf_op jit(solution)/shard_map/sample_residual/pallas_call | solution.py:289
  35.7 0.0 collective-permute-done.2.left_ref
  35.7 0.0 collective-permute-done.3.right_ref
  35.7 0.0 copy-start.4
  35.7 0.0 copy-start
  35.7 0.0 copy-start.3
  35.7 56.1 %demigrate_and_sample.1 = (f32[4096,128]{1,0:T(8,128)}, f32[16,128]{1,0:T(8,128)S(1)}, f32[2,32,8,128]{3,2,1,0:T(8,128)S(1)}, f32[2,32,16,128]{3,2,1,0:T(8,128)S(1)}, f32[2,32,8,128]{3,2,1,0:T(8,128)S(1)}) custom-call(s32[16,16,16]{2,1,0:T(8,128)S(1)} %get-tuple-element.35.col_ref, s32[256,16,128]{2,1,0:T(8,128)} %bitcast.16, f32[16,16,16]{2,1,0:T(8,128)S(1)} %copy-done.5, ...), custom_call_target="tpu_custom_call" | custom-call | flops 20000000000 | bytes 8000000 | tf_op jit(solution)/shard_map/demigrate_and_sample/pallas_call | solution.py:322
  91.9 5.2 %collective-permute-start.4 = (f32[2,32,8,128]{3,2,1,0:T(8,128)S(1)}, f32[2,32,8,128]{3,2,1,0:T(8,128)S(1)}, u32[]{:S(2)}, u32[]{:S(2)}) collective-permute-start(f32[2,32,8,128]{3,2,1,0:T(8,128)S(1)} %get-tuple-element.23), channel_id=1, source_target_pairs={{0,1},{1,2},{2,3},{4,5},{5,6},{6,7},{8,9},{9,10},{10,11},{12,13},{... | collective-permute-start | bytes 786440 | tf_op jit(solution)/shard_map/ppermute | solution.py:256
  97.1 1.3 collective-permute-start.5
  98.4 0.0 collective-permute-done.4.low_ref
  98.4 3.3 %collective-permute-done.5.high_ref = f32[2,32,8,128]{3,2,1,0:T(8,128)S(1)} collective-permute-done((f32[2,32,8,128]{3,2,1,0:T(8,128)S(1)}, f32[2,32,8,128]{3,2,1,0:T(8,128)S(1)}, u32[]{:S(2)}, u32[]{:S(2)}) %collective-permute-start.5) | collective-permute-done | bytes 262176 | tf_op jit(solution)/shard_map/ppermute | solution.py:256
  101.7 0.1 fold_y.1
  101.8 4.3 %collective-permute-start.6 = (f32[2,8,16,128]{3,2,1,0:T(8,128)S(1)}, f32[2,8,16,128]{3,2,1,0:T(8,128)S(1)}, u32[]{:S(2)}, u32[]{:S(2)}) collective-permute-start(f32[2,8,16,128]{3,2,1,0:T(8,128)S(1)} %get-tuple-element.26), channel_id=1, source_target_pairs={{0,4},{4,8},{8,12},{12,16},{16,20},{20,24},{24,28},{1,5},{5,9},{9,... | collective-permute-start | bytes 393224 | tf_op jit(solution)/shard_map/ppermute | solution.py:256
  106.1 1.3 collective-permute-start.7
  107.4 1.2 collective-permute-done.6.low_ref
  108.6 4.4 %collective-permute-done.7.high_ref = f32[2,8,16,128]{3,2,1,0:T(8,128)S(1)} collective-permute-done((f32[2,8,16,128]{3,2,1,0:T(8,128)S(1)}, f32[2,8,16,128]{3,2,1,0:T(8,128)S(1)}, u32[]{:S(2)}, u32[]{:S(2)}) %collective-permute-start.7) | collective-permute-done | bytes 131104 | tf_op jit(solution)/shard_map/ppermute | solution.py:256
  112.9 0.0 copy-done.4
  112.9 0.2 fold_x.1
  113.1 14.8 %all_to_all.5.stats_ref = f32[32,1,128]{2,1,0:T(1,128)S(1)} all-to-all(f32[32,1,128]{2,1,0:T(1,128)S(1)} %get-tuple-element.29), channel_id=1, replica_groups=mesh['gx'=8,'gy'=4] {'gx','gy'}, dimensions={0} | all-to-all | bytes 32768 | tf_op jit(solution)/shard_map/all_to_all | solution.py:385
  127.9 0.0 copy-done
  127.9 0.0 copy-done.3
  127.9 0.0 copy-start.1
  127.9 1.6 %copy-done.1 = f32[4096,128]{1,0:T(8,128)S(1)} copy-done((f32[4096,128]{1,0:T(8,128)S(1)}, f32[4096,128]{1,0:T(8,128)}, u32[]{:S(2)}) %copy-start.1) | copy-done | bytes 2097176
  129.5 3.6 %update.1 = (f32[16,16,128]{2,1,0:T(8,128)}, f32[4096,128]{1,0:T(8,128)}, f32[16,16,128]{2,1,0:T(8,128)}) custom-call(f32[32,1,128]{2,1,0:T(1,128)S(1)} %all_to_all.5.stats_ref, f32[4096,128]{1,0:T(8,128)S(1)} %bitcast.13, f32[4096,128]{1,0:T(8,128)S(1)} %copy-done.1, f32[16,16,128]{2,1,0:T(8,128)S(1)} %copy-done.3, f32[16,16,128]{2,1,0:T(8,128)S(1)} %copy-done.2, ...), custom_call_target="tpu_custom_call" | custom-call | tf_op jit(solution)/shard_map/update/pallas_call | solution.py:393
  (6 shorter events, 0.1 us)
Async XLA Ops:
  1.5 20.5 %collective-permute-start.1 = (f32[8,16,128]{2,1,0:T(8,128)S(1)}, f32[8,16,128]{2,1,0:T(8,128)S(1)}, u32[]{:S(2)}, u32[]{:S(2)}) collective-permute-start(f32[8,16,128]{2,1,0:T(8,128)S(1)} %get-tuple-element.39), channel_id=1, source_target_pairs={{4,0},{8,4},{12,8},{16,12},{20,16},{24,20},{28,24},{5,1},{9,5},{13... | collective-permute-start | bytes 196616 | tf_op jit(solution)/shard_map/ppermute | solution.py:256
  2.8 19.2 %collective-permute-start = (f32[8,16,128]{2,1,0:T(8,128)S(1)}, f32[8,16,128]{2,1,0:T(8,128)S(1)}, u32[]{:S(2)}, u32[]{:S(2)}) collective-permute-start(f32[8,16,128]{2,1,0:T(8,128)S(1)} %get-tuple-element.40), channel_id=1, source_target_pairs={{0,4},{4,8},{8,12},{12,16},{16,20},{20,24},{24,28},{1,5},{5,9},{9,... | collective-permute-start | bytes 196616 | tf_op jit(solution)/shard_map/ppermute | solution.py:256
  9.5 0.9 copy-start.5
  10.4 0.7 copy-start.6
  11.1 10.9 %copy-start.2 = (f32[16,16,128]{2,1,0:T(8,128)S(1)}, f32[16,16,128]{2,1,0:T(8,128)}, u32[]{:S(2)}) copy-start(f32[16,16,128]{2,1,0:T(8,128)} %dir_ref.1) | copy-start | bytes 393220
  22.1 13.6 %collective-permute-start.2 = (f32[32,8,128]{2,1,0:T(8,128)S(1)}, f32[32,8,128]{2,1,0:T(8,128)S(1)}, u32[]{:S(2)}, u32[]{:S(2)}) collective-permute-start(f32[32,8,128]{2,1,0:T(8,128)S(1)} %get-tuple-element.19), channel_id=1, source_target_pairs={{0,1},{1,2},{2,3},{4,5},{5,6},{6,7},{8,9},{9,10},{10,11},{12,13},{... | collective-permute-start | bytes 393224 | tf_op jit(solution)/shard_map/ppermute | solution.py:256
  23.5 12.1 %collective-permute-start.3 = (f32[32,8,128]{2,1,0:T(8,128)S(1)}, f32[32,8,128]{2,1,0:T(8,128)S(1)}, u32[]{:S(2)}, u32[]{:S(2)}) collective-permute-start(f32[32,8,128]{2,1,0:T(8,128)S(1)} %get-tuple-element.20), channel_id=1, source_target_pairs={{1,0},{2,1},{3,2},{5,4},{6,5},{7,6},{9,8},{10,9},{11,10},{13,12},{... | collective-permute-start | bytes 393224 | tf_op jit(solution)/shard_map/ppermute | solution.py:256
  35.7 77.3 %copy-start.4 = (f32[16,16,128]{2,1,0:T(8,128)S(1)}, f32[16,16,128]{2,1,0:T(8,128)}, u32[]{:S(2)}) copy-start(f32[16,16,128]{2,1,0:T(8,128)} %grad_ref.1) | copy-start | bytes 393220
  35.7 92.2 %copy-start = (f32[16,16,2048]{2,1,0:T(8,128)S(1)}, f32[16,16,2048]{2,1,0:T(8,128)}, u32[]{:S(2)}) copy-start(f32[16,16,2048]{2,1,0:T(8,128)} %param.9) | copy-start | bytes 6291460
  35.7 92.2 %copy-start.3 = (f32[16,16,128]{2,1,0:T(8,128)S(1)}, f32[16,16,128]{2,1,0:T(8,128)}, u32[]{:S(2)}) copy-start(f32[16,16,128]{2,1,0:T(8,128)} %model_ref.1) | copy-start | bytes 393220
  91.9 6.5 %collective-permute-start.4 = (f32[2,32,8,128]{3,2,1,0:T(8,128)S(1)}, f32[2,32,8,128]{3,2,1,0:T(8,128)S(1)}, u32[]{:S(2)}, u32[]{:S(2)}) collective-permute-start(f32[2,32,8,128]{3,2,1,0:T(8,128)S(1)} %get-tuple-element.23), channel_id=1, source_target_pairs={{0,1},{1,2},{2,3},{4,5},{5,6},{6,7},{8,9},{9,10},{10,11},{12,13},{... | collective-permute-start | bytes 786440 | tf_op jit(solution)/shard_map/ppermute | solution.py:256
  97.1 4.6 %collective-permute-start.5 = (f32[2,32,8,128]{3,2,1,0:T(8,128)S(1)}, f32[2,32,8,128]{3,2,1,0:T(8,128)S(1)}, u32[]{:S(2)}, u32[]{:S(2)}) collective-permute-start(f32[2,32,8,128]{3,2,1,0:T(8,128)S(1)} %get-tuple-element.24), channel_id=1, source_target_pairs={{1,0},{2,1},{3,2},{5,4},{6,5},{7,6},{9,8},{10,9},{11,10},{13,12},{... | collective-permute-start | bytes 786440 | tf_op jit(solution)/shard_map/ppermute | solution.py:256
  101.8 6.8 %collective-permute-start.6 = (f32[2,8,16,128]{3,2,1,0:T(8,128)S(1)}, f32[2,8,16,128]{3,2,1,0:T(8,128)S(1)}, u32[]{:S(2)}, u32[]{:S(2)}) collective-permute-start(f32[2,8,16,128]{3,2,1,0:T(8,128)S(1)} %get-tuple-element.26), channel_id=1, source_target_pairs={{0,4},{4,8},{8,12},{12,16},{16,20},{20,24},{24,28},{1,5},{5,9},{9,... | collective-permute-start | bytes 393224 | tf_op jit(solution)/shard_map/ppermute | solution.py:256
  106.1 6.9 %collective-permute-start.7 = (f32[2,8,16,128]{3,2,1,0:T(8,128)S(1)}, f32[2,8,16,128]{3,2,1,0:T(8,128)S(1)}, u32[]{:S(2)}, u32[]{:S(2)}) collective-permute-start(f32[2,8,16,128]{3,2,1,0:T(8,128)S(1)} %get-tuple-element.27), channel_id=1, source_target_pairs={{4,0},{8,4},{12,8},{16,12},{20,16},{24,20},{28,24},{5,1},{9,5},{13... | collective-permute-start | bytes 393224 | tf_op jit(solution)/shard_map/ppermute | solution.py:256
  127.9 1.6 %copy-start.1 = (f32[4096,128]{1,0:T(8,128)S(1)}, f32[4096,128]{1,0:T(8,128)}, u32[]{:S(2)}) copy-start(f32[4096,128]{1,0:T(8,128)} %get-tuple-element.30.data_ref) | copy-start | bytes 6291460

commit v3 on v2

--- a/solution.py
+++ b/solution.py
@@ -37,30 +37,32 @@
     return (b // SUB) * (SUB * highs) + b % SUB
 
 
-def fill_weights(amp_ref, counts_ref, scales, bins_y, entries, row):
-    weight = amp_ref[0].T * counts_ref[pl.ds(row, 1), :].astype(F32)
-    for b in range(bins_y):
+def fill_weights(amp_ref, counts, scales):
+    bins, entries = amp_ref.shape[1], amp_ref.shape[2]
+    weight = amp_ref[0].T * counts.astype(F32)
+    for b in range(bins):
         column = jnp.broadcast_to(weight[:, b : b + 1], (entries, LANES))
         scales[pl.ds(b * entries, entries), :] = column
 
 
-def sample_row(res_ref, times_ref, scales, vals, bins_y, entries, highs):
-    for b in range(bins_y):
-        first = trace_row(b, highs)
-        for part in range(0, entries, SUB):
-            times = times_ref[b, pl.ds(part, SUB), :]
-            high = jnp.right_shift(times, LANES.bit_length() - 1)
-            low = jnp.bitwise_and(times, LANES - 1)
-            acc = jnp.zeros(times.shape, F32)
-            for h in range(highs):
-                table = res_ref[pl.ds(first + SUB * h, SUB, stride=0), :]
-                got = jnp.take_along_axis(table, low, axis=1, mode="promise_in_bounds")
-                acc = jnp.where(high == h, got, acc)
-            at = pl.ds(b * entries + part, SUB)
-            vals[at, :] = acc * scales[at, :]
-
-
-def spread_row(vals, place_ref, s_ref, row, wide_y, span):
+def sample_bin(source, first, highs, times_ref, b, scales, vals):
+    entries = times_ref.shape[1]
+    for part in range(0, entries, SUB):
+        times = times_ref[b, pl.ds(part, SUB), :]
+        high = jnp.right_shift(times, LANES.bit_length() - 1)
+        low = jnp.bitwise_and(times, LANES - 1)
+        acc = jnp.zeros(times.shape, F32)
+        for h in range(highs):
+            table = source[pl.ds(first + SUB * h, SUB, stride=0), :]
+            got = jnp.take_along_axis(table, low, axis=1, mode="promise_in_bounds")
+            acc = jnp.where(high == h, got, acc)
+        at = b * entries + part
+        at = pl.ds(at if isinstance(at, int) else pl.multiple_of(at, SUB), SUB)
+        vals[at, :] = acc * scales[at, :]
+
+
+def spread_bins(vals, place_ref, s_ref, row, wide_y):
+    span = SIDE * wide_y
     value = vals[...]
     upper = value.astype(BF16)
     lower = (value - upper.astype(F32)).astype(BF16)
@@ -82,48 +84,14 @@
     def _():
         s_ref[...] = prev_ref[...]
 
-    fill_weights(amp_ref, counts_ref, scales, bins_y, entries, step + row0)
-    sample_row(res_ref, times_ref, scales, vals, bins_y, entries, highs)
-    spread_row(vals, place_ref, s_ref, step + row0, wide_y, SIDE * wide_y)
-
-
-def main_kernel(
-    geo,
-    unroll,
-    col_ref,
-    times_ref,
-    amp_ref,
-    counts_ref,
-    place_ref,
-    mid_ref,
-    left_ref,
-    right_ref,
-    s1_ref,
-    data_ref,
-    curv_ref,
-    out_left,
-    out_mid,
-    out_right,
-    image,
-    s_ref,
-    vals,
-    scales,
-    work,
-):
+    fill_weights(amp_ref, counts_ref[pl.ds(step + row0, 1), :], scales)
+    for b in range(bins_y):
+        sample_bin(res_ref, trace_row(b, highs), highs, times_ref, b, scales, vals)
+    spread_bins(vals, place_ref, s_ref, step + row0, wide_y)
+
+
+def scatter_bin(geo, b, image, col_ref, times_ref, scales, work):
     bins_y, entries, highs, wide_y = geo
-    step = pl.program_id(0)
-    wide_x = mid_ref.shape[0]
-
-    @pl.when(step == 0)
-    def _():
-        s_ref[...] = jnp.zeros_like(s_ref)
-        curv_ref[...] = jnp.zeros_like(curv_ref)
-        for x in range(wide_x):
-            image[pl.ds(x * wide_y, RADIUS), :] = left_ref[x]
-            image[pl.ds(x * wide_y + RADIUS, bins_y), :] = mid_ref[x]
-            image[pl.ds(x * wide_y + RADIUS + bins_y, RADIUS), :] = right_ref[x]
-
-    fill_weights(amp_ref, counts_ref, scales, bins_y, entries, step)
     half = LANES // 2
     half_bits = half.bit_length() - 1
     iota16 = lax.broadcasted_iota(jnp.int32, (16, LANES), 0)
@@ -131,58 +99,129 @@
     iota_hi = [(iota16 + k).astype(F32).astype(BF16) for k in range(0, 2 * highs, 16)]
     zero = jnp.zeros((), BF16)
     one = jnp.ones((), BF16)
-
-    def one_bin(b, slot):
-        for e in range(entries):
-            column = col_ref[0, b, e]
-            work[slot, 0, pl.ds(e, 1), :] = image[pl.ds(column, 1), :]
-        value = work[slot, 0] * scales[pl.ds(pl.multiple_of(b * entries, SUB), entries), :]
-        upper = value.astype(BF16).astype(F32)
-        work[slot, 0] = upper
-        work[slot, 1] = value - upper
-        times = times_ref[b]
-        work[slot, 2] = jnp.bitwise_and(times, half - 1).astype(F32)
-        middle = jnp.bitwise_and(jnp.right_shift(times, half_bits), 1)
-        work[slot, 3] = (jnp.right_shift(times, half_bits + 1) + middle * highs).astype(F32)
-        lefts = []
-        rights = []
-        for e in range(entries):
-
-            def wide(k):
-                return work[slot, k, pl.ds(e, 16, stride=0), :].astype(BF16)
-
-            place = wide(3)
-            hits = [place == iota for iota in iota_hi]
-            parts = [jnp.where(hit, wide(k), zero) for k in range(2) for hit in hits]
-            lefts.append(jnp.concatenate(parts, axis=0))
-            low = wide(2)
-            rights.append(
-                jnp.concatenate([jnp.where(low == iota, one, zero) for iota in iota_lo], axis=0)
-            )
-        out = lax.dot_general(
-            jnp.concatenate(lefts, axis=1),
-            jnp.concatenate(rights, axis=1),
-            (((1,), (1,)), ((), ())),
-            preferred_element_type=F32,
+    for e in range(entries):
+        column = col_ref[0, b, e]
+        work[0, pl.ds(e, 1), :] = image[pl.ds(column, 1), :]
+    value = work[0, pl.ds(0, entries), :]
+    value = value * scales[pl.ds(pl.multiple_of(b * entries, SUB), entries), :]
+    upper = value.astype(BF16).astype(F32)
+    times = times_ref[b]
+    middle = jnp.bitwise_and(jnp.right_shift(times, half_bits), 1)
+    rows = pl.ds(0, entries)
+    work[0, rows, :] = upper
+    work[1, rows, :] = value - upper
+    work[2, rows, :] = jnp.bitwise_and(times, half - 1).astype(F32)
+    work[3, rows, :] = (jnp.right_shift(times, half_bits + 1) + middle * highs).astype(F32)
+    lefts = []
+    rights = []
+    for e in range(entries):
+
+        def wide(k):
+            row = work[k, pl.ds(e, SUB, stride=0), :]
+            return jnp.concatenate([row, row], axis=0).astype(BF16)
+
+        place = wide(3)
+        hits = [place == iota for iota in iota_hi]
+        parts = [jnp.where(hit, wide(k), zero) for k in range(2) for hit in hits]
+        lefts.append(jnp.concatenate(parts, axis=0))
+        low = wide(2)
+        rights.append(
+            jnp.concatenate([jnp.where(low == iota, one, zero) for iota in iota_lo], axis=0)
         )
-        out = out[: 2 * highs] + out[2 * highs :]
-        trace = jnp.concatenate([out[:highs], out[highs:]], axis=1)
-        data_ref[pl.ds(trace_row(b, highs), highs, stride=SUB), :] = trace
-        return trace * trace
+    out = lax.dot_general(
+        jnp.concatenate(lefts, axis=1),
+        jnp.concatenate(rights, axis=1),
+        (((1,), (1,)), ((), ())),
+        preferred_element_type=F32,
+    )
+    out = out[: 2 * highs] + out[2 * highs :]
+    return jnp.concatenate([out[:highs], out[highs:]], axis=1)
+
+
+def main_kernel(
+    geo,
+    unroll,
+    row0,
+    col_ref,
+    times_ref,
+    old_times_ref,
+    res_times_ref,
+    amp_ref,
+    res_amp_ref,
+    counts_ref,
+    res_counts_ref,
+    old_place_ref,
+    last_place_ref,
+    res_place_ref,
+    res_ref,
+    mid_ref,
+    left_ref,
+    right_ref,
+    s1_in_ref,
+    data_ref,
+    curv_ref,
+    out_left,
+    out_mid,
+    out_right,
+    image,
+    s1_ref,
+    s2_ref,
+    vals,
+    res_vals,
+    scales,
+    old_scales,
+    res_scales,
+    old_data,
+    *works,
+):
+    bins_y, entries, highs, wide_y = geo
+    step = pl.program_id(0)
+    wide_x = mid_ref.shape[0]
+    groups = bins_y // unroll
+    res_bins = res_times_ref.shape[0]
+    res_unroll = res_bins // groups
+
+    @pl.when(step == 0)
+    def _():
+        s1_ref[...] = s1_in_ref[...]
+        s2_ref[...] = jnp.zeros_like(s2_ref)
+        curv_ref[...] = jnp.zeros_like(curv_ref)
+        old_data[...] = jnp.zeros_like(old_data)
+        scales[...] = jnp.zeros_like(scales)
+        for x in range(wide_x):
+            image[pl.ds(x * wide_y, RADIUS), :] = left_ref[x]
+            image[pl.ds(x * wide_y + RADIUS, bins_y), :] = mid_ref[x]
+            image[pl.ds(x * wide_y + RADIUS + bins_y, RADIUS), :] = right_ref[x]
+
+    old_scales[...] = scales[...]
+    fill_weights(amp_ref, counts_ref[pl.ds(step, 1), :], scales)
+    fill_weights(res_amp_ref, res_counts_ref[0], res_scales)
 
     def some_bins(k, total):
         for u in range(unroll):
-            total = total + one_bin(k * unroll + u, u)
+            b = k * unroll + u
+            trace = scatter_bin(geo, b, image, col_ref, times_ref, scales, works[u])
+            data_ref[pl.ds(trace_row(b, highs), highs, stride=SUB), :] = trace
+            total = total + trace * trace
+            first = trace_row(b, highs)
+            sample_bin(old_data, first, highs, old_times_ref, b, old_scales, vals)
+            if u < res_unroll:
+                r = k * res_unroll + u
+                first = trace_row(r, highs)
+                sample_bin(res_ref, first, highs, res_times_ref, r, res_scales, res_vals)
         return total
 
-    total = lax.fori_loop(0, bins_y // unroll, some_bins, jnp.zeros((highs, LANES), F32))
-    curv_ref[...] += total
-    sample_row(data_ref, times_ref, scales, vals, bins_y, entries, highs)
-    spread_row(vals, place_ref, s_ref, step, wide_y, SIDE * wide_y)
+    curv_ref[...] += lax.fori_loop(0, groups, some_bins, jnp.zeros((highs, LANES), F32))
+    spread_bins(vals, old_place_ref, s2_ref, jnp.maximum(step - 1, 0), wide_y)
+    spread_bins(res_vals, res_place_ref, s1_ref, row0 + (step * res_bins) // bins_y, wide_y)
+    old_data[...] = data_ref[...]
 
     @pl.when(step == pl.num_programs(0) - 1)
     def _():
-        for k, ref in enumerate((s1_ref, s_ref)):
+        for b in range(bins_y):
+            sample_bin(old_data, trace_row(b, highs), highs, times_ref, b, scales, vals)
+        spread_bins(vals, last_place_ref, s2_ref, step, wide_y)
+        for k, ref in enumerate((s1_ref, s2_ref)):
             for x in range(wide_x):
                 out_left[k, x] = ref[pl.ds(x * wide_y, RADIUS), :]
                 out_mid[k, x] = ref[pl.ds(x * wide_y + RADIUS, bins_y), :]
@@ -307,27 +346,45 @@
             name="sample_residual",
         )(res_rows, times, amplitude, trace_counts, place, prev)
 
-    s1 = first(0, bins_x // 2, jnp.zeros((columns, depths), F32))
+    early = bins_x // 4
+    row0 = 2 * early
+    s1 = first(0, early, jnp.zeros((columns, depths), F32))
     ext = jnp.concatenate([from_prev, direction, from_next], axis=0)
     tail, head, s1 = lax.optimization_barrier((ext[:, bins_y - RADIUS :], ext[:, :RADIUS], s1))
     left = shift(tail, "gy", 1)
     right = shift(head, "gy", -1)
-    s1 = first(bins_x // 2, bins_x - bins_x // 2, s1)
+    s1 = first(early, early, s1)
 
     unroll = 4
+    cut = bins_x // (bins_x - row0)
+    res_bins = bins_y // cut
+    counts_cut = trace_counts.reshape(bins_x * cut, 1, res_bins)
     whole3 = lambda i: (0, 0, 0)
     whole4 = lambda i: (0, 0, 0, 0)
+    before = lambda i: (jnp.maximum(i - 1, 0), 0, 0)
+    this = lambda i: (i, 0, 0)
+    late = lambda i: (row0 * cut + i, 0, 0)
     strip = (2, wide_x, RADIUS, depths)
     middle = (2, wide_x, bins_y, depths)
+    vals_shape = pltpu.VMEM((bins_y * entries, depths), F32)
+    res_shape = pltpu.VMEM((res_bins * entries, depths), F32)
+    columns_shape = pltpu.VMEM((columns, depths), F32)
     data_rows, curv, out_left, out_mid, out_right = pl.pallas_call(
-        functools.partial(main_kernel, geo, unroll),
+        functools.partial(main_kernel, geo, unroll, row0),
         grid=(bins_x,),
         in_specs=[
-            pl.BlockSpec((1, bins_y, entries), lambda i: (i, 0, 0), memory_space=pltpu.SMEM),
-            pl.BlockSpec((bins_y, entries, depths), lambda i: (i, 0, 0)),
-            pl.BlockSpec((1, bins_y, entries), lambda i: (i, 0, 0)),
+            pl.BlockSpec((1, bins_y, entries), this, memory_space=pltpu.SMEM),
+            pl.BlockSpec((bins_y, entries, depths), this),
+            pl.BlockSpec((bins_y, entries, depths), before),
+            pl.BlockSpec((res_bins, entries, depths), late),
+            pl.BlockSpec((1, bins_y, entries), this),
+            pl.BlockSpec((1, res_bins, entries), late),
             pl.BlockSpec((bins_x, bins_y), lambda i: (0, 0)),
-            pl.BlockSpec((1, 1, bins_y * entries), lambda i: (i, 0, 0)),
+            pl.BlockSpec((1, 1, res_bins), late),
+            pl.BlockSpec((1, 1, bins_y * entries), before),
+            pl.BlockSpec((1, 1, bins_y * entries), lambda i: (bins_x - 1, 0, 0)),
+            pl.BlockSpec((1, 1, res_bins * entries), late),
+            pl.BlockSpec((res_bins * highs, LANES), lambda i: (row0 * cut + i, 0)),
             pl.BlockSpec((wide_x, bins_y, depths), whole3),
             pl.BlockSpec((wide_x, RADIUS, depths), whole3),
             pl.BlockSpec((wide_x, RADIUS, depths), whole3),
@@ -347,19 +404,33 @@
             jax.ShapeDtypeStruct(middle, F32),
             jax.ShapeDtypeStruct(strip, F32),
         ],
-        scratch_shapes=[
-            pltpu.VMEM((columns, depths), F32),
-            pltpu.VMEM((columns, depths), F32),
-            pltpu.VMEM((bins_y * entries, depths), F32),
-            pltpu.VMEM((bins_y * entries, depths), F32),
-            pltpu.VMEM((unroll, 4, entries, LANES), F32),
-        ],
+        scratch_shapes=[columns_shape, columns_shape, columns_shape]
+        + [vals_shape, res_shape, vals_shape, vals_shape, res_shape]
+        + [pltpu.VMEM((rows_per, LANES), F32)]
+        + [pltpu.VMEM((4, entries + SUB, LANES), F32)] * unroll,
         compiler_params=params(),
         cost_estimate=pl.CostEstimate(
             flops=20 * 10**9, bytes_accessed=8 * 10**6, transcendentals=0
         ),
         name="demigrate_and_sample",
-    )(column, times, amplitude, trace_counts, place, ext, left, right, s1)
+    )(
+        column,
+        times,
+        times,
+        times,
+        amplitude,
+        amplitude.reshape(bins_x * cut, res_bins, entries),
+        trace_counts,
+        counts_cut,
+        place,
+        place,
+        place.reshape(bins_x * cut, 1, res_bins * entries),
+        res_rows,
+        ext,
+        left,
+        right,
+        s1,
+    )
 
     from_low = shift(out_right, "gy", 1)
     from_high = shift(out_left, "gy", -1)
@@ -403,7 +474,7 @@
         ],
         out_specs=[cells, rows, cells],
         out_shape=[image_shape, jax.ShapeDtypeStruct(res_rows.shape, F32), image_shape],
-        compiler_params=params(SMALL_LIMIT),
+        compiler_params=params(),
         name="update",
     )(stats, res_rows, data_rows, model_image, direction, grads)
     return (new_image, from_rows(new_rows, data_residual.shape), new_direction)

time: 134 us -> 115 us (0.86)
  Pallas kernels: 81.6 us -> 64.6 us
  local copies, waits for them, and re-layouts: 4.28 us -> 2.88 us
    pallas_call x1, Pallas kernels: 56.1 us -> 46.3 us  [body(): pl.pallas_call(functools.partial(main_kernel, geo, unroll, row0), grid=(b...]
    pallas_call x2, Pallas kernels: 21.6 us -> 11.9 us  [first(): pl.pallas_call(functools.partial(first_kernel, geo, row0), grid=(count,),...]
    pallas_call x1, Pallas kernels: 3.62 us -> 6.11 us  [body(): pl.pallas_call(last_kernel, grid=(steps,), in_specs=[pl.BlockSpec(stats.s...]
    unnamed x16 -> x18, local copies, waits for them, and re-layouts: 3.23 us -> 1.64 us
  transfers between devices with their start and end apart: 8 -> 8, of which waited for: 3 -> 3; matrix products, arithmetic and copies ran while one was open for 1% -> 1% of each run, Pallas kernels for 16% -> 10%
where the time goes in v3:
time: 115 us
  Pallas kernels  64.6 us (56%)
  starting transfers between devices  21.5 us (19%)
  blocking collectives  14.8 us (13%)
  waiting for transfers between devices  8.94 us (8%)
  local copies, waits for them, and re-layouts  2.88 us (3%)
    pallas_call x1, Pallas kernels, body(): pl.pallas_call(functools.partial(main_kernel, geo, unroll, row0), grid=(b...  46.3 us
    ppermute x8, starting transfers between devices, shift(): return lax.ppermute(cells, axis, pairs)  21.5 us
    all_to_all x1, blocking collectives, body(): stats = lax.all_to_all(stats, ('gx', 'gy'), 0, 0, tiled=True)  14.8 us
    pallas_call x2, Pallas kernels, first(): pl.pallas_call(functools.partial(first_kernel, geo, row0), grid=(count,),...  11.9 us
    ppermute x8, waiting for transfers between devices, shift(): return lax.ppermute(cells, axis, pairs)  8.94 us
    pallas_call x1, Pallas kernels, body(): pl.pallas_call(last_kernel, grid=(steps,), in_specs=[pl.BlockSpec(stats.s...  6.11 us
  transfers between devices with their start and end apart: 8, of which 3 were waited for; matrix products, arithmetic and copies ran while one was open for 1% of the time, Pallas kernels for 10%

profile of v3, /device:TPU:0, one launch (start us, length us, event | category | flops | bytes accessed | tf_op | source)
XLA Modules:
  0.0 114.6 jit_solution(10844743672211190007)
XLA Ops:
  0.6 0.9 fusion.6
  1.5 1.3 %collective-permute-start.1 = (f32[8,16,128]{2,1,0:T(8,128)S(1)}, f32[8,16,128]{2,1,0:T(8,128)S(1)}, u32[]{:S(2)}, u32[]{:S(2)}) collective-permute-start(f32[8,16,128]{2,1,0:T(8,128)S(1)} %get-tuple-element.39), channel_id=1, source_target_pairs={{4,0},{8,4},{12,8},{16,12},{20,16},{24,20},{28,24},{5,1},{9,5},{13... | collective-permute-start | bytes 196616 | tf_op jit(solution)/shard_map/ppermute | solution.py:295
  2.8 5.5 %collective-permute-start = (f32[8,16,128]{2,1,0:T(8,128)S(1)}, f32[8,16,128]{2,1,0:T(8,128)S(1)}, u32[]{:S(2)}, u32[]{:S(2)}) collective-permute-start(f32[8,16,128]{2,1,0:T(8,128)S(1)} %get-tuple-element.40), channel_id=1, source_target_pairs={{0,4},{4,8},{8,12},{12,16},{16,20},{20,24},{24,28},{1,5},{5,9},{9,... | collective-permute-start | bytes 196616 | tf_op jit(solution)/shard_map/ppermute | solution.py:295
  8.3 1.1 broadcast_add_fusion
  9.4 0.1 reshape.38.place_ref.old_place_ref.last_place_ref
  9.5 0.0 copy-start.4
  9.5 0.7 copy-done.4
  10.2 0.0 copy-start.6
  10.2 0.9 copy-done.6
  11.1 0.0 copy-start.5
  11.1 0.0 copy-start.1
  11.1 0.0 copy-start.7
  11.1 6.0 %sample_residual.2.prev_ref = f32[1024,128]{1,0:T(8,128)S(1)} custom-call(f32[4096,128]{1,0:T(8,128)} %bitcast.13, s32[256,16,128]{2,1,0:T(8,128)} %bitcast.19, f32[16,16,16]{2,1,0:T(8,128)S(1)} %copy-done.6, s32[16,16]{1,0:T(8,128)S(1)} %copy-done.4, s32[16,1,256]{2,1,0:T(1,128)S(1)} %reshape.38.place_ref.old_place_ref.last_place_ref, ...), custom_call_target="tpu_custom_call" | custom-call | flops 4000000000 | bytes 4000000 | tf_op jit(solution)/shard_map/sample_residual/pallas_call | solution.py:328
  17.1 0.0 copy-done.5
  17.1 0.1 reshape.37
  17.2 0.1 reshape_reshape.3.res_place_ref
  17.3 0.0 collective-permute-done
  17.3 0.0 copy-done.1
  17.4 0.0 collective-permute-done.1
  17.4 1.4 %collective-permute-start.2 = (f32[32,8,128]{2,1,0:T(8,128)S(1)}, f32[32,8,128]{2,1,0:T(8,128)S(1)}, u32[]{:S(2)}, u32[]{:S(2)}) collective-permute-start(f32[32,8,128]{2,1,0:T(8,128)S(1)} %get-tuple-element.19), channel_id=1, source_target_pairs={{0,1},{1,2},{2,3},{4,5},{5,6},{6,7},{8,9},{9,10},{10,11},{12,13},{... | collective-permute-start | bytes 393224 | tf_op jit(solution)/shard_map/ppermute | solution.py:295
  18.9 1.3 %collective-permute-start.3 = (f32[32,8,128]{2,1,0:T(8,128)S(1)}, f32[32,8,128]{2,1,0:T(8,128)S(1)}, u32[]{:S(2)}, u32[]{:S(2)}) collective-permute-start(f32[32,8,128]{2,1,0:T(8,128)S(1)} %get-tuple-element.20), channel_id=1, source_target_pairs={{1,0},{2,1},{3,2},{5,4},{6,5},{7,6},{9,8},{10,9},{11,10},{13,12},{... | collective-permute-start | bytes 393224 | tf_op jit(solution)/shard_map/ppermute | solution.py:295
  20.2 0.0 copy-done.7
  20.2 5.9 %sample_residual.3.s1_in_ref = f32[1024,128]{1,0:T(8,128)S(1)} custom-call(f32[4096,128]{1,0:T(8,128)} %bitcast.14, s32[256,16,128]{2,1,0:T(8,128)} %bitcast.20, f32[16,16,16]{2,1,0:T(8,128)S(1)} %copy-done.7, s32[16,16]{1,0:T(8,128)S(1)} %copy-done.5, s32[16,1,256]{2,1,0:T(1,128)S(1)} %reshape.38.place_ref.old_place_ref.last_place_ref, ...), custom_call_target="tpu_custom_call" | custom-call | flops 4000000000 | bytes 4000000 | tf_op jit(solution)/shard_map/sample_residual/pallas_call | solution.py:328
  26.1 0.0 collective-permute-done.2.left_ref
  26.1 0.0 collective-permute-done.3.right_ref
  26.1 0.0 copy-start.3
  26.1 0.0 copy-start
  26.1 0.0 copy-start.2
  26.2 46.3 %demigrate_and_sample.1 = (f32[4096,128]{1,0:T(8,128)}, f32[16,128]{1,0:T(8,128)S(1)}, f32[2,32,8,128]{3,2,1,0:T(8,128)S(1)}, f32[2,32,16,128]{3,2,1,0:T(8,128)S(1)}, f32[2,32,8,128]{3,2,1,0:T(8,128)S(1)}) custom-call(s32[16,16,16]{2,1,0:T(8,128)S(1)} %get-tuple-element.35.col_ref, s32[256,16,128]{2,1,0:T(8,128)} %bitcast.21, s32[256,16,128]{2,1,0:T(8,128)} %bitcast.22, ...), custom_call_target="tpu_custom_call" | custom-call | flops 20000000000 | bytes 8000000 | tf_op jit(solution)/shard_map/demigrate_and_sample/pallas_call | solution.py:372
  72.5 5.1 %collective-permute-start.4 = (f32[2,32,8,128]{3,2,1,0:T(8,128)S(1)}, f32[2,32,8,128]{3,2,1,0:T(8,128)S(1)}, u32[]{:S(2)}, u32[]{:S(2)}) collective-permute-start(f32[2,32,8,128]{3,2,1,0:T(8,128)S(1)} %get-tuple-element.23), channel_id=1, source_target_pairs={{0,1},{1,2},{2,3},{4,5},{5,6},{6,7},{8,9},{9,10},{10,11},{12,13},{... | collective-permute-start | bytes 786440 | tf_op jit(solution)/shard_map/ppermute | solution.py:295
  77.6 1.3 %collective-permute-start.5 = (f32[2,32,8,128]{3,2,1,0:T(8,128)S(1)}, f32[2,32,8,128]{3,2,1,0:T(8,128)S(1)}, u32[]{:S(2)}, u32[]{:S(2)}) collective-permute-start(f32[2,32,8,128]{3,2,1,0:T(8,128)S(1)} %get-tuple-element.24), channel_id=1, source_target_pairs={{1,0},{2,1},{3,2},{5,4},{6,5},{7,6},{9,8},{10,9},{11,10},{13,12},{... | collective-permute-start | bytes 786440 | tf_op jit(solution)/shard_map/ppermute | solution.py:295
  78.9 0.0 collective-permute-done.4.low_ref
  78.9 3.4 %collective-permute-done.5.high_ref = f32[2,32,8,128]{3,2,1,0:T(8,128)S(1)} collective-permute-done((f32[2,32,8,128]{3,2,1,0:T(8,128)S(1)}, f32[2,32,8,128]{3,2,1,0:T(8,128)S(1)}, u32[]{:S(2)}, u32[]{:S(2)}) %collective-permute-start.5) | collective-permute-done | bytes 262176 | tf_op jit(solution)/shard_map/ppermute | solution.py:295
  82.3 0.1 fold_y.1
  82.4 4.3 %collective-permute-start.6 = (f32[2,8,16,128]{3,2,1,0:T(8,128)S(1)}, f32[2,8,16,128]{3,2,1,0:T(8,128)S(1)}, u32[]{:S(2)}, u32[]{:S(2)}) collective-permute-start(f32[2,8,16,128]{3,2,1,0:T(8,128)S(1)} %get-tuple-element.26), channel_id=1, source_target_pairs={{0,4},{4,8},{8,12},{12,16},{16,20},{20,24},{24,28},{1,5},{5,9},{9,... | collective-permute-start | bytes 393224 | tf_op jit(solution)/shard_map/ppermute | solution.py:295
  86.7 1.3 %collective-permute-start.7 = (f32[2,8,16,128]{3,2,1,0:T(8,128)S(1)}, f32[2,8,16,128]{3,2,1,0:T(8,128)S(1)}, u32[]{:S(2)}, u32[]{:S(2)}) collective-permute-start(f32[2,8,16,128]{3,2,1,0:T(8,128)S(1)} %get-tuple-element.27), channel_id=1, source_target_pairs={{4,0},{8,4},{12,8},{16,12},{20,16},{24,20},{28,24},{5,1},{9,5},{13... | collective-permute-start | bytes 393224 | tf_op jit(solution)/shard_map/ppermute | solution.py:295
  88.0 1.2 %collective-permute-done.6.low_ref = f32[2,8,16,128]{3,2,1,0:T(8,128)S(1)} collective-permute-done((f32[2,8,16,128]{3,2,1,0:T(8,128)S(1)}, f32[2,8,16,128]{3,2,1,0:T(8,128)S(1)}, u32[]{:S(2)}, u32[]{:S(2)}) %collective-permute-start.6) | collective-permute-done | bytes 131104 | tf_op jit(solution)/shard_map/ppermute | solution.py:295
  89.2 4.4 %collective-permute-done.7.high_ref = f32[2,8,16,128]{3,2,1,0:T(8,128)S(1)} collective-permute-done((f32[2,8,16,128]{3,2,1,0:T(8,128)S(1)}, f32[2,8,16,128]{3,2,1,0:T(8,128)S(1)}, u32[]{:S(2)}, u32[]{:S(2)}) %collective-permute-start.7) | collective-permute-done | bytes 131104 | tf_op jit(solution)/shard_map/ppermute | solution.py:295
  93.5 0.0 copy-done.3
  93.5 0.2 fold_x.1
  93.7 14.8 %all_to_all.5.stats_ref = f32[32,1,128]{2,1,0:T(1,128)S(1)} all-to-all(f32[32,1,128]{2,1,0:T(1,128)S(1)} %get-tuple-element.29), channel_id=1, replica_groups=mesh['gx'=8,'gy'=4] {'gx','gy'}, dimensions={0} | all-to-all | bytes 32768 | tf_op jit(solution)/shard_map/all_to_all | solution.py:456
  108.5 0.0 copy-done
  108.5 0.0 copy-done.2
  108.5 6.1 %update.1 = (f32[16,16,128]{2,1,0:T(8,128)}, f32[4096,128]{1,0:T(8,128)}, f32[16,16,128]{2,1,0:T(8,128)}) custom-call(f32[32,1,128]{2,1,0:T(1,128)S(1)} %all_to_all.5.stats_ref, f32[4096,128]{1,0:T(8,128)S(1)} %bitcast.16, f32[4096,128]{1,0:T(8,128)} %get-tuple-element.30.data_ref, f32[16,16,128]{2,1,0:T(8,128)S(1)} %copy-done.2, ...), custom_call_target="tpu_custom_call" | custom-call | tf_op jit(solution)/shard_map/update/pallas_call | solution.py:464
  (6 shorter events, 0.1 us)
Async XLA Ops:
  1.5 15.8 %collective-permute-start.1 = (f32[8,16,128]{2,1,0:T(8,128)S(1)}, f32[8,16,128]{2,1,0:T(8,128)S(1)}, u32[]{:S(2)}, u32[]{:S(2)}) collective-permute-start(f32[8,16,128]{2,1,0:T(8,128)S(1)} %get-tuple-element.39), channel_id=1, source_target_pairs={{4,0},{8,4},{12,8},{16,12},{20,16},{24,20},{28,24},{5,1},{9,5},{13... | collective-permute-start | bytes 196616 | tf_op jit(solution)/shard_map/ppermute | solution.py:295
  2.8 14.5 %collective-permute-start = (f32[8,16,128]{2,1,0:T(8,128)S(1)}, f32[8,16,128]{2,1,0:T(8,128)S(1)}, u32[]{:S(2)}, u32[]{:S(2)}) collective-permute-start(f32[8,16,128]{2,1,0:T(8,128)S(1)} %get-tuple-element.40), channel_id=1, source_target_pairs={{0,4},{4,8},{8,12},{12,16},{16,20},{20,24},{24,28},{1,5},{5,9},{9,... | collective-permute-start | bytes 196616 | tf_op jit(solution)/shard_map/ppermute | solution.py:295
  9.5 0.7 copy-start.4
  10.2 0.9 copy-start.6
  11.1 6.0 %copy-start.5 = (s32[16,16]{1,0:T(8,128)S(1)}, s32[16,16]{1,0:T(8,128)}, u32[]{:S(2)}) copy-start(s32[16,16]{1,0:T(8,128)} %counts_ref.5) | copy-start | bytes 3076
  11.1 6.2 %copy-start.1 = (f32[16,16,128]{2,1,0:T(8,128)S(1)}, f32[16,16,128]{2,1,0:T(8,128)}, u32[]{:S(2)}) copy-start(f32[16,16,128]{2,1,0:T(8,128)} %dir_ref.1) | copy-start | bytes 393220
  11.1 9.0 %copy-start.7 = (f32[16,16,16]{2,1,0:T(8,128)S(1)}, f32[16,16,16]{2,1,0:T(8,128)}, u32[]{:S(2)}) copy-start(f32[16,16,16]{2,1,0:T(8,128)} %amp_ref.5) | copy-start | bytes 49156
  17.4 8.7 %collective-permute-start.2 = (f32[32,8,128]{2,1,0:T(8,128)S(1)}, f32[32,8,128]{2,1,0:T(8,128)S(1)}, u32[]{:S(2)}, u32[]{:S(2)}) collective-permute-start(f32[32,8,128]{2,1,0:T(8,128)S(1)} %get-tuple-element.19), channel_id=1, source_target_pairs={{0,1},{1,2},{2,3},{4,5},{5,6},{6,7},{8,9},{9,10},{10,11},{12,13},{... | collective-permute-start | bytes 393224 | tf_op jit(solution)/shard_map/ppermute | solution.py:295
  18.9 7.3 %collective-permute-start.3 = (f32[32,8,128]{2,1,0:T(8,128)S(1)}, f32[32,8,128]{2,1,0:T(8,128)S(1)}, u32[]{:S(2)}, u32[]{:S(2)}) collective-permute-start(f32[32,8,128]{2,1,0:T(8,128)S(1)} %get-tuple-element.20), channel_id=1, source_target_pairs={{1,0},{2,1},{3,2},{5,4},{6,5},{7,6},{9,8},{10,9},{11,10},{13,12},{... | collective-permute-start | bytes 393224 | tf_op jit(solution)/shard_map/ppermute | solution.py:295
  26.1 67.4 %copy-start.3 = (f32[16,16,128]{2,1,0:T(8,128)S(1)}, f32[16,16,128]{2,1,0:T(8,128)}, u32[]{:S(2)}) copy-start(f32[16,16,128]{2,1,0:T(8,128)} %grad_ref.1) | copy-start | bytes 393220
  26.1 82.4 %copy-start = (f32[16,16,2048]{2,1,0:T(8,128)S(1)}, f32[16,16,2048]{2,1,0:T(8,128)}, u32[]{:S(2)}) copy-start(f32[16,16,2048]{2,1,0:T(8,128)} %param.9) | copy-start | bytes 6291460
  26.1 82.4 %copy-start.2 = (f32[16,16,128]{2,1,0:T(8,128)S(1)}, f32[16,16,128]{2,1,0:T(8,128)}, u32[]{:S(2)}) copy-start(f32[16,16,128]{2,1,0:T(8,128)} %model_ref.1) | copy-start | bytes 393220
  72.5 6.4 %collective-permute-start.4 = (f32[2,32,8,128]{3,2,1,0:T(8,128)S(1)}, f32[2,32,8,128]{3,2,1,0:T(8,128)S(1)}, u32[]{:S(2)}, u32[]{:S(2)}) collective-permute-start(f32[2,32,8,128]{3,2,1,0:T(8,128)S(1)} %get-tuple-element.23), channel_id=1, source_target_pairs={{0,1},{1,2},{2,3},{4,5},{5,6},{6,7},{8,9},{9,10},{10,11},{12,13},{... | collective-permute-start | bytes 786440 | tf_op jit(solution)/shard_map/ppermute | solution.py:295
  77.6 4.7 %collective-permute-start.5 = (f32[2,32,8,128]{3,2,1,0:T(8,128)S(1)}, f32[2,32,8,128]{3,2,1,0:T(8,128)S(1)}, u32[]{:S(2)}, u32[]{:S(2)}) collective-permute-start(f32[2,32,8,128]{3,2,1,0:T(8,128)S(1)} %get-tuple-element.24), channel_id=1, source_target_pairs={{1,0},{2,1},{3,2},{5,4},{6,5},{7,6},{9,8},{10,9},{11,10},{13,12},{... | collective-permute-start | bytes 786440 | tf_op jit(solution)/shard_map/ppermute | solution.py:295
  82.4 6.8 %collective-permute-start.6 = (f32[2,8,16,128]{3,2,1,0:T(8,128)S(1)}, f32[2,8,16,128]{3,2,1,0:T(8,128)S(1)}, u32[]{:S(2)}, u32[]{:S(2)}) collective-permute-start(f32[2,8,16,128]{3,2,1,0:T(8,128)S(1)} %get-tuple-element.26), channel_id=1, source_target_pairs={{0,4},{4,8},{8,12},{12,16},{16,20},{20,24},{24,28},{1,5},{5,9},{9,... | collective-permute-start | bytes 393224 | tf_op jit(solution)/shard_map/ppermute | solution.py:295
  86.7 6.9 %collective-permute-start.7 = (f32[2,8,16,128]{3,2,1,0:T(8,128)S(1)}, f32[2,8,16,128]{3,2,1,0:T(8,128)S(1)}, u32[]{:S(2)}, u32[]{:S(2)}) collective-permute-start(f32[2,8,16,128]{3,2,1,0:T(8,128)S(1)} %get-tuple-element.27), channel_id=1, source_target_pairs={{4,0},{8,4},{12,8},{16,12},{20,16},{24,20},{28,24},{5,1},{9,5},{13... | collective-permute-start | bytes 393224 | tf_op jit(solution)/shard_map/ppermute | solution.py:295

commit v4 on v3

--- a/solution.py
+++ b/solution.py
@@ -14,6 +14,7 @@
 F32 = jnp.float32
 BF16 = jnp.bfloat16
 VMEM_LIMIT = 51 * 1024 * 1024
+MAIN_LIMIT = 44 * 1024 * 1024
 SMALL_LIMIT = 24 * 1024 * 1024
 
 
@@ -314,8 +315,8 @@
     geo = (bins_y, entries, highs, wide_y)
     rows_per = bins_y * highs
 
-    from_prev = shift(direction[bins_x - RADIUS :], "gx", 1)
-    from_next = shift(direction[:RADIUS], "gx", -1)
+    from_prev = shift(direction, "gx", 1)[bins_x - RADIUS :]
+    from_next = shift(direction, "gx", -1)[:RADIUS]
 
     times = travel_times.reshape(bins_x * bins_y, entries, depths)
     res_rows = to_rows(data_residual)
@@ -355,7 +356,7 @@
     right = shift(head, "gy", -1)
     s1 = first(early, early, s1)
 
-    unroll = 4
+    unroll = 8
     cut = bins_x // (bins_x - row0)
     res_bins = bins_y // cut
     counts_cut = trace_counts.reshape(bins_x * cut, 1, res_bins)
@@ -408,7 +409,7 @@
         + [vals_shape, res_shape, vals_shape, vals_shape, res_shape]
         + [pltpu.VMEM((rows_per, LANES), F32)]
         + [pltpu.VMEM((4, entries + SUB, LANES), F32)] * unroll,
-        compiler_params=params(),
+        compiler_params=params(MAIN_LIMIT),
         cost_estimate=pl.CostEstimate(
             flops=20 * 10**9, bytes_accessed=8 * 10**6, transcendentals=0
         ),
@@ -474,7 +475,7 @@
         ],
         out_specs=[cells, rows, cells],
         out_shape=[image_shape, jax.ShapeDtypeStruct(res_rows.shape, F32), image_shape],
-        compiler_params=params(),
+        compiler_params=params(SMALL_LIMIT),
         name="update",
     )(stats, res_rows, data_rows, model_image, direction, grads)
     return (new_image, from_rows(new_rows, data_residual.shape), new_direction)

time: 115 us -> 103 us (0.90)
  Pallas kernels: 64.6 us -> 53.4 us
    pallas_call x1, Pallas kernels: 46.3 us -> 37.6 us  [body(): pl.pallas_call(functools.partial(main_kernel, geo, unroll, row0), grid=(b...]
    pallas_call x1, Pallas kernels: 6.11 us -> 3.65 us  [body(): pl.pallas_call(last_kernel, grid=(steps,), in_specs=[pl.BlockSpec(stats.s...]
  transfers between devices with their start and end apart: 8 -> 8, of which waited for: 3 -> 3; matrix products, arithmetic and copies ran while one was open for 1% -> 1% of each run, Pallas kernels for 10% -> 12%
where the time goes in v4:
time: 103 us
  Pallas kernels  53.4 us (52%)
  starting transfers between devices  21.8 us (21%)
  blocking collectives  14.8 us (14%)
  waiting for transfers between devices  8.92 us (9%)
  local copies, waits for them, and re-layouts  1.99 us (2%)
  other arithmetic  1.08 us (1%)
    pallas_call x1, Pallas kernels, body(): pl.pallas_call(functools.partial(main_kernel, geo, unroll, row0), grid=(b...  37.6 us
    ppermute x8, starting transfers between devices, shift(): return lax.ppermute(cells, axis, pairs)  21.8 us
    all_to_all x1, blocking collectives, body(): stats = lax.all_to_all(stats, ('gx', 'gy'), 0, 0, tiled=True)  14.8 us
    pallas_call x2, Pallas kernels, first(): pl.pallas_call(functools.partial(first_kernel, geo, row0), grid=(count,),...  11.9 us
    ppermute x8, waiting for transfers between devices, shift(): return lax.ppermute(cells, axis, pairs)  8.92 us
    pallas_call x1, Pallas kernels, body(): pl.pallas_call(last_kernel, grid=(steps,), in_specs=[pl.BlockSpec(stats.s...  3.65 us
  transfers between devices with their start and end apart: 8, of which 3 were waited for; matrix products, arithmetic and copies ran while one was open for 1% of the time, Pallas kernels for 12%

profile of v4, /device:TPU:0, one launch (start us, length us, event | category | flops | bytes accessed | tf_op | source)
XLA Modules:
  0.0 103.0 jit_solution(11402834067731349758)
XLA Ops:
  0.6 1.3 %collective-permute-start.1 = (f32[16,16,128]{2,1,0:T(8,128)}, f32[16,16,128]{2,1,0:T(8,128)S(1)}, u32[]{:S(2)}, u32[]{:S(2)}) collective-permute-start(f32[16,16,128]{2,1,0:T(8,128)} %dir_ref.1), channel_id=1, source_target_pairs={{4,0},{8,4},{12,8},{16,12},{20,16},{24,20},{28,24},{5,1},{9,5},{13... | collective-permute-start | bytes 393224 | tf_op jit(solution)/shard_map/ppermute | solution.py:296
  1.9 5.5 %collective-permute-start = (f32[16,16,128]{2,1,0:T(8,128)}, f32[16,16,128]{2,1,0:T(8,128)S(1)}, u32[]{:S(2)}, u32[]{:S(2)}) collective-permute-start(f32[16,16,128]{2,1,0:T(8,128)} %dir_ref.1), channel_id=1, source_target_pairs={{0,4},{4,8},{8,12},{12,16},{16,20},{20,24},{24,28},{1,5},{5,9},{9,... | collective-permute-start | bytes 393224 | tf_op jit(solution)/shard_map/ppermute | solution.py:296
  7.4 1.1 %broadcast_add_fusion = (s32[16,16,16]{2,1,0:T(8,128)S(1)}, s32[16,16,16]{2,1,0:T(8,128)S(1)}) fusion(s32[16]{0:T(128)S(1)} %iota_multiply_fusion, s32[16,16,16]{2,1,0:T(8,128)} %param.12), kind=kLoop, calls=%fused_computation.9 | loop fusion | flops 65536 | bytes 49216 | tf_op jit(solution)/shard_map/add | solution.py:325
  8.5 0.1 reshape.38.place_ref.old_place_ref.last_place_ref
  8.6 0.0 copy-start.4
  8.7 0.7 copy-done.4
  9.3 0.0 copy-start.7
  9.3 0.9 copy-done.7
  10.2 0.0 copy-start.5
  10.3 0.0 copy-start.1
  10.3 0.0 copy-start.8
  10.3 6.0 %sample_residual.2.prev_ref = f32[1024,128]{1,0:T(8,128)S(1)} custom-call(f32[4096,128]{1,0:T(8,128)} %bitcast.13, s32[256,16,128]{2,1,0:T(8,128)} %bitcast.18, f32[16,16,16]{2,1,0:T(8,128)S(1)} %copy-done.7, s32[16,16]{1,0:T(8,128)S(1)} %copy-done.4, s32[16,1,256]{2,1,0:T(1,128)S(1)} %reshape.38.place_ref.old_place_ref.last_place_ref, ...), custom_call_target="tpu_custom_call" | custom-call | flops 4000000000 | bytes 4000000 | tf_op jit(solution)/shard_map/sample_residual/pallas_call | solution.py:329
  16.2 0.0 copy-done.5
  16.2 0.1 reshape.37
  16.3 0.1 reshape_reshape.3.res_place_ref
  16.4 0.0 collective-permute-done.1
  16.4 0.0 collective-permute-done
  16.5 0.0 copy-done.1
  16.5 0.0 copy-start
  16.5 0.0 copy-start.6
  16.6 1.9 %collective-permute-start.2 = (f32[32,8,128]{2,1,0:T(8,128)S(1)}, f32[32,8,128]{2,1,0:T(8,128)S(1)}, u32[]{:S(2)}, u32[]{:S(2)}) collective-permute-start(f32[32,8,128]{2,1,0:T(8,128)S(1)} %get-tuple-element.19), channel_id=1, source_target_pairs={{0,1},{1,2},{2,3},{4,5},{5,6},{6,7},{8,9},{9,10},{10,11},{12,13},{... | collective-permute-start | bytes 393224 | tf_op jit(solution)/shard_map/ppermute | solution.py:296
  18.4 1.3 %collective-permute-start.3 = (f32[32,8,128]{2,1,0:T(8,128)S(1)}, f32[32,8,128]{2,1,0:T(8,128)S(1)}, u32[]{:S(2)}, u32[]{:S(2)}) collective-permute-start(f32[32,8,128]{2,1,0:T(8,128)S(1)} %get-tuple-element.20), channel_id=1, source_target_pairs={{1,0},{2,1},{3,2},{5,4},{6,5},{7,6},{9,8},{10,9},{11,10},{13,12},{... | collective-permute-start | bytes 393224 | tf_op jit(solution)/shard_map/ppermute | solution.py:296
  19.7 0.0 copy-done.8
  19.7 5.9 %sample_residual.3.s1_in_ref = f32[1024,128]{1,0:T(8,128)S(1)} custom-call(f32[4096,128]{1,0:T(8,128)} %bitcast.14, s32[256,16,128]{2,1,0:T(8,128)} %bitcast.19, f32[16,16,16]{2,1,0:T(8,128)S(1)} %copy-done.8, s32[16,16]{1,0:T(8,128)S(1)} %copy-done.5, s32[16,1,256]{2,1,0:T(1,128)S(1)} %reshape.38.place_ref.old_place_ref.last_place_ref, ...), custom_call_target="tpu_custom_call" | custom-call | flops 4000000000 | bytes 4000000 | tf_op jit(solution)/shard_map/sample_residual/pallas_call | solution.py:329
  25.7 0.0 collective-permute-done.2.left_ref
  25.7 0.0 collective-permute-done.3.right_ref
  25.7 0.0 copy-done
  25.7 0.0 copy-done.6
  25.7 0.0 copy-start.3
  25.7 0.0 copy-start.2
  25.7 37.6 %demigrate_and_sample.1 = (f32[4096,128]{1,0:T(8,128)S(1)}, f32[16,128]{1,0:T(8,128)S(1)}, f32[2,32,8,128]{3,2,1,0:T(8,128)S(1)}, f32[2,32,16,128]{3,2,1,0:T(8,128)S(1)}, f32[2,32,8,128]{3,2,1,0:T(8,128)S(1)}) custom-call(s32[16,16,16]{2,1,0:T(8,128)S(1)} %get-tuple-element.35.col_ref, s32[256,16,128]{2,1,0:T(8,128)S(1)} %bitcast.20, ...), custom_call_target="tpu_custom_call" | custom-call | flops 20000000000 | bytes 8000000 | tf_op jit(solution)/shard_map/demigrate_and_sample/pallas_call | solution.py:373
  63.4 5.0 %collective-permute-start.4 = (f32[2,32,8,128]{3,2,1,0:T(8,128)S(1)}, f32[2,32,8,128]{3,2,1,0:T(8,128)S(1)}, u32[]{:S(2)}, u32[]{:S(2)}) collective-permute-start(f32[2,32,8,128]{3,2,1,0:T(8,128)S(1)} %get-tuple-element.23), channel_id=1, source_target_pairs={{0,1},{1,2},{2,3},{4,5},{5,6},{6,7},{8,9},{9,10},{10,11},{12,13},{... | collective-permute-start | bytes 786440 | tf_op jit(solution)/shard_map/ppermute | solution.py:296
  68.4 1.3 %collective-permute-start.5 = (f32[2,32,8,128]{3,2,1,0:T(8,128)S(1)}, f32[2,32,8,128]{3,2,1,0:T(8,128)S(1)}, u32[]{:S(2)}, u32[]{:S(2)}) collective-permute-start(f32[2,32,8,128]{3,2,1,0:T(8,128)S(1)} %get-tuple-element.24), channel_id=1, source_target_pairs={{1,0},{2,1},{3,2},{5,4},{6,5},{7,6},{9,8},{10,9},{11,10},{13,12},{... | collective-permute-start | bytes 786440 | tf_op jit(solution)/shard_map/ppermute | solution.py:296
  69.7 0.0 collective-permute-done.4.low_ref
  69.7 3.3 %collective-permute-done.5.high_ref = f32[2,32,8,128]{3,2,1,0:T(8,128)S(1)} collective-permute-done((f32[2,32,8,128]{3,2,1,0:T(8,128)S(1)}, f32[2,32,8,128]{3,2,1,0:T(8,128)S(1)}, u32[]{:S(2)}, u32[]{:S(2)}) %collective-permute-start.5) | collective-permute-done | bytes 262176 | tf_op jit(solution)/shard_map/ppermute | solution.py:296
  73.1 0.1 fold_y.1
  73.1 4.3 %collective-permute-start.6 = (f32[2,8,16,128]{3,2,1,0:T(8,128)S(1)}, f32[2,8,16,128]{3,2,1,0:T(8,128)S(1)}, u32[]{:S(2)}, u32[]{:S(2)}) collective-permute-start(f32[2,8,16,128]{3,2,1,0:T(8,128)S(1)} %get-tuple-element.26), channel_id=1, source_target_pairs={{0,4},{4,8},{8,12},{12,16},{16,20},{20,24},{24,28},{1,5},{5,9},{9,... | collective-permute-start | bytes 393224 | tf_op jit(solution)/shard_map/ppermute | solution.py:296
  77.5 1.3 %collective-permute-start.7 = (f32[2,8,16,128]{3,2,1,0:T(8,128)S(1)}, f32[2,8,16,128]{3,2,1,0:T(8,128)S(1)}, u32[]{:S(2)}, u32[]{:S(2)}) collective-permute-start(f32[2,8,16,128]{3,2,1,0:T(8,128)S(1)} %get-tuple-element.27), channel_id=1, source_target_pairs={{4,0},{8,4},{12,8},{16,12},{20,16},{24,20},{28,24},{5,1},{9,5},{13... | collective-permute-start | bytes 393224 | tf_op jit(solution)/shard_map/ppermute | solution.py:296
  78.8 1.2 %collective-permute-done.6.low_ref = f32[2,8,16,128]{3,2,1,0:T(8,128)S(1)} collective-permute-done((f32[2,8,16,128]{3,2,1,0:T(8,128)S(1)}, f32[2,8,16,128]{3,2,1,0:T(8,128)S(1)}, u32[]{:S(2)}, u32[]{:S(2)}) %collective-permute-start.6) | collective-permute-done | bytes 131104 | tf_op jit(solution)/shard_map/ppermute | solution.py:296
  80.0 4.4 %collective-permute-done.7.high_ref = f32[2,8,16,128]{3,2,1,0:T(8,128)S(1)} collective-permute-done((f32[2,8,16,128]{3,2,1,0:T(8,128)S(1)}, f32[2,8,16,128]{3,2,1,0:T(8,128)S(1)}, u32[]{:S(2)}, u32[]{:S(2)}) %collective-permute-start.7) | collective-permute-done | bytes 131104 | tf_op jit(solution)/shard_map/ppermute | solution.py:296
  84.3 0.0 copy-done.3
  84.3 0.2 fold_x.1
  84.5 14.8 %all_to_all.5.stats_ref = f32[32,1,128]{2,1,0:T(1,128)S(1)} all-to-all(f32[32,1,128]{2,1,0:T(1,128)S(1)} %get-tuple-element.29), channel_id=1, replica_groups=mesh['gx'=8,'gy'=4] {'gx','gy'}, dimensions={0} | all-to-all | bytes 32768 | tf_op jit(solution)/shard_map/all_to_all | solution.py:457
  99.3 0.0 copy-done.2
  99.3 3.6 %update.1 = (f32[16,16,128]{2,1,0:T(8,128)}, f32[4096,128]{1,0:T(8,128)}, f32[16,16,128]{2,1,0:T(8,128)}) custom-call(f32[32,1,128]{2,1,0:T(1,128)S(1)} %all_to_all.5.stats_ref, f32[4096,128]{1,0:T(8,128)S(1)} %bitcast.16, f32[4096,128]{1,0:T(8,128)S(1)} %get-tuple-element.30.data_ref, f32[16,16,128]{2,1,0:T(8,128)S(1)} %copy-done.2, ...), custom_call_target="tpu_custom_call" | custom-call | tf_op jit(solution)/shard_map/update/pallas_call | solution.py:465
  (6 shorter events, 0.1 us)
Async XLA Ops:
  0.6 15.8 %collective-permute-start.1 = (f32[16,16,128]{2,1,0:T(8,128)}, f32[16,16,128]{2,1,0:T(8,128)S(1)}, u32[]{:S(2)}, u32[]{:S(2)}) collective-permute-start(f32[16,16,128]{2,1,0:T(8,128)} %dir_ref.1), channel_id=1, source_target_pairs={{4,0},{8,4},{12,8},{16,12},{20,16},{24,20},{28,24},{5,1},{9,5},{13... | collective-permute-start | bytes 393224 | tf_op jit(solution)/shard_map/ppermute | solution.py:296
  1.9 14.5 %collective-permute-start = (f32[16,16,128]{2,1,0:T(8,128)}, f32[16,16,128]{2,1,0:T(8,128)S(1)}, u32[]{:S(2)}, u32[]{:S(2)}) collective-permute-start(f32[16,16,128]{2,1,0:T(8,128)} %dir_ref.1), channel_id=1, source_target_pairs={{0,4},{4,8},{8,12},{12,16},{16,20},{20,24},{24,28},{1,5},{5,9},{9,... | collective-permute-start | bytes 393224 | tf_op jit(solution)/shard_map/ppermute | solution.py:296
  8.6 0.7 copy-start.4
  9.3 0.9 copy-start.7
  10.2 6.0 %copy-start.5 = (s32[16,16]{1,0:T(8,128)S(1)}, s32[16,16]{1,0:T(8,128)}, u32[]{:S(2)}) copy-start(s32[16,16]{1,0:T(8,128)} %counts_ref.5) | copy-start | bytes 3076
  10.3 6.2 %copy-start.1 = (f32[16,16,128]{2,1,0:T(8,128)S(1)}, f32[16,16,128]{2,1,0:T(8,128)}, u32[]{:S(2)}) copy-start(f32[16,16,128]{2,1,0:T(8,128)} %dir_ref.1) | copy-start | bytes 393220
  10.3 9.5 %copy-start.8 = (f32[16,16,16]{2,1,0:T(8,128)S(1)}, f32[16,16,16]{2,1,0:T(8,128)}, u32[]{:S(2)}) copy-start(f32[16,16,16]{2,1,0:T(8,128)} %amp_ref.5) | copy-start | bytes 49156
  16.5 9.2 %copy-start = (f32[16,16,2048]{2,1,0:T(8,128)S(1)}, f32[16,16,2048]{2,1,0:T(8,128)}, u32[]{:S(2)}) copy-start(f32[16,16,2048]{2,1,0:T(8,128)} %param.9) | copy-start | bytes 6291460
  16.5 9.2 %copy-start.6 = (s32[16,16,16,128]{3,2,1,0:T(8,128)S(1)}, s32[16,16,16,128]{3,2,1,0:T(8,128)}, u32[]{:S(2)}) copy-start(s32[16,16,16,128]{3,2,1,0:T(8,128)} %param.13) | copy-start | bytes 6291460
  16.6 9.1 %collective-permute-start.2 = (f32[32,8,128]{2,1,0:T(8,128)S(1)}, f32[32,8,128]{2,1,0:T(8,128)S(1)}, u32[]{:S(2)}, u32[]{:S(2)}) collective-permute-start(f32[32,8,128]{2,1,0:T(8,128)S(1)} %get-tuple-element.19), channel_id=1, source_target_pairs={{0,1},{1,2},{2,3},{4,5},{5,6},{6,7},{8,9},{9,10},{10,11},{12,13},{... | collective-permute-start | bytes 393224 | tf_op jit(solution)/shard_map/ppermute | solution.py:296
  18.4 7.3 %collective-permute-start.3 = (f32[32,8,128]{2,1,0:T(8,128)S(1)}, f32[32,8,128]{2,1,0:T(8,128)S(1)}, u32[]{:S(2)}, u32[]{:S(2)}) collective-permute-start(f32[32,8,128]{2,1,0:T(8,128)S(1)} %get-tuple-element.20), channel_id=1, source_target_pairs={{1,0},{2,1},{3,2},{5,4},{6,5},{7,6},{9,8},{10,9},{11,10},{13,12},{... | collective-permute-start | bytes 393224 | tf_op jit(solution)/shard_map/ppermute | solution.py:296
  25.7 58.6 %copy-start.3 = (f32[16,16,128]{2,1,0:T(8,128)S(1)}, f32[16,16,128]{2,1,0:T(8,128)}, u32[]{:S(2)}) copy-start(f32[16,16,128]{2,1,0:T(8,128)} %grad_ref.1) | copy-start | bytes 393220
  25.7 73.6 %copy-start.2 = (f32[16,16,128]{2,1,0:T(8,128)S(1)}, f32[16,16,128]{2,1,0:T(8,128)}, u32[]{:S(2)}) copy-start(f32[16,16,128]{2,1,0:T(8,128)} %model_ref.1) | copy-start | bytes 393220
  63.4 6.3 %collective-permute-start.4 = (f32[2,32,8,128]{3,2,1,0:T(8,128)S(1)}, f32[2,32,8,128]{3,2,1,0:T(8,128)S(1)}, u32[]{:S(2)}, u32[]{:S(2)}) collective-permute-start(f32[2,32,8,128]{3,2,1,0:T(8,128)S(1)} %get-tuple-element.23), channel_id=1, source_target_pairs={{0,1},{1,2},{2,3},{4,5},{5,6},{6,7},{8,9},{9,10},{10,11},{12,13},{... | collective-permute-start | bytes 786440 | tf_op jit(solution)/shard_map/ppermute | solution.py:296
  68.4 4.7 %collective-permute-start.5 = (f32[2,32,8,128]{3,2,1,0:T(8,128)S(1)}, f32[2,32,8,128]{3,2,1,0:T(8,128)S(1)}, u32[]{:S(2)}, u32[]{:S(2)}) collective-permute-start(f32[2,32,8,128]{3,2,1,0:T(8,128)S(1)} %get-tuple-element.24), channel_id=1, source_target_pairs={{1,0},{2,1},{3,2},{5,4},{6,5},{7,6},{9,8},{10,9},{11,10},{13,12},{... | collective-permute-start | bytes 786440 | tf_op jit(solution)/shard_map/ppermute | solution.py:296
  73.1 6.8 %collective-permute-start.6 = (f32[2,8,16,128]{3,2,1,0:T(8,128)S(1)}, f32[2,8,16,128]{3,2,1,0:T(8,128)S(1)}, u32[]{:S(2)}, u32[]{:S(2)}) collective-permute-start(f32[2,8,16,128]{3,2,1,0:T(8,128)S(1)} %get-tuple-element.26), channel_id=1, source_target_pairs={{0,4},{4,8},{8,12},{12,16},{16,20},{20,24},{24,28},{1,5},{5,9},{9,... | collective-permute-start | bytes 393224 | tf_op jit(solution)/shard_map/ppermute | solution.py:296
  77.5 6.9 %collective-permute-start.7 = (f32[2,8,16,128]{3,2,1,0:T(8,128)S(1)}, f32[2,8,16,128]{3,2,1,0:T(8,128)S(1)}, u32[]{:S(2)}, u32[]{:S(2)}) collective-permute-start(f32[2,8,16,128]{3,2,1,0:T(8,128)S(1)} %get-tuple-element.27), channel_id=1, source_target_pairs={{4,0},{8,4},{12,8},{16,12},{20,16},{24,20},{28,24},{5,1},{9,5},{13... | collective-permute-start | bytes 393224 | tf_op jit(solution)/shard_map/ppermute | solution.py:296

commit v5 on v4

--- a/solution.py
+++ b/solution.py
@@ -14,7 +14,8 @@
 F32 = jnp.float32
 BF16 = jnp.bfloat16
 VMEM_LIMIT = 51 * 1024 * 1024
-MAIN_LIMIT = 44 * 1024 * 1024
+FIRST_LIMIT = 60 * 1024 * 1024
+MAIN_LIMIT = 36 * 1024 * 1024
 SMALL_LIMIT = 24 * 1024 * 1024
 
 
@@ -38,18 +39,18 @@
     return (b // SUB) * (SUB * highs) + b % SUB
 
 
-def fill_weights(amp_ref, counts, scales):
-    bins, entries = amp_ref.shape[1], amp_ref.shape[2]
-    weight = amp_ref[0].T * counts.astype(F32)
+def fill_weights(amplitude, counts, scales):
+    bins, entries = amplitude.shape
+    weight = amplitude.T * counts.astype(F32)
     for b in range(bins):
         column = jnp.broadcast_to(weight[:, b : b + 1], (entries, LANES))
         scales[pl.ds(b * entries, entries), :] = column
 
 
-def sample_bin(source, first, highs, times_ref, b, scales, vals):
+def sample_bin(source, first, highs, times_ref, bin_at, b, scales, vals):
     entries = times_ref.shape[1]
     for part in range(0, entries, SUB):
-        times = times_ref[b, pl.ds(part, SUB), :]
+        times = times_ref[bin_at, pl.ds(part, SUB), :]
         high = jnp.right_shift(times, LANES.bit_length() - 1)
         low = jnp.bitwise_and(times, LANES - 1)
         acc = jnp.zeros(times.shape, F32)
@@ -62,13 +63,23 @@
         vals[at, :] = acc * scales[at, :]
 
 
-def spread_bins(vals, place_ref, s_ref, row, wide_y):
+def column_offset(entry, wide_y):
+    return entry + jnp.right_shift(entry * 241, 12) * (wide_y - SIDE)
+
+
+def place_row(aperture, wide_y, first_bin=0):
+    offset = column_offset(aperture, wide_y)
+    return jnp.concatenate(
+        [offset[b : b + 1, :] + (b + first_bin) for b in range(offset.shape[0])], axis=1
+    )
+
+
+def spread_bins(vals, place, s_ref, row, wide_y):
     span = SIDE * wide_y
     value = vals[...]
     upper = value.astype(BF16)
     lower = (value - upper.astype(F32)).astype(BF16)
     both = jnp.concatenate([upper, lower], axis=1)
-    place = place_ref[0]
     iota = lax.broadcasted_iota(jnp.int32, (span, place.shape[1]), 0)
     table = jnp.where(iota == place, 1.0, 0.0).astype(BF16)
     part = jnp.dot(table, both, preferred_element_type=F32)
@@ -76,22 +87,23 @@
 
 
 def first_kernel(
-    geo, row0, res_ref, times_ref, amp_ref, counts_ref, place_ref, prev_ref, s_ref, vals, scales
+    geo, row0, res_ref, times_ref, amp_ref, counts_ref, aper_ref, *refs
 ):
     bins_y, entries, highs, wide_y = geo
     step = pl.program_id(0)
+    s_ref, vals, scales = refs[-3:]
 
     @pl.when(step == 0)
     def _():
-        s_ref[...] = prev_ref[...]
-
-    fill_weights(amp_ref, counts_ref[pl.ds(step + row0, 1), :], scales)
+        s_ref[...] = refs[0][...] if len(refs) > 3 else jnp.zeros_like(s_ref)
+
+    fill_weights(amp_ref[0], counts_ref[pl.ds(step + row0, 1), :], scales)
     for b in range(bins_y):
-        sample_bin(res_ref, trace_row(b, highs), highs, times_ref, b, scales, vals)
-    spread_bins(vals, place_ref, s_ref, step + row0, wide_y)
-
-
-def scatter_bin(geo, b, image, col_ref, times_ref, scales, work):
+        sample_bin(res_ref, trace_row(b, highs), highs, times_ref, b, b, scales, vals)
+    spread_bins(vals, place_row(aper_ref[0], wide_y), s_ref, step + row0, wide_y)
+
+
+def scatter_bin(geo, row, b, image, entry_ref, times_ref, scales, work):
     bins_y, entries, highs, wide_y = geo
     half = LANES // 2
     half_bits = half.bit_length() - 1
@@ -101,12 +113,12 @@
     zero = jnp.zeros((), BF16)
     one = jnp.ones((), BF16)
     for e in range(entries):
-        column = col_ref[0, b, e]
+        column = column_offset(entry_ref[row, b, e], wide_y) + (row * wide_y + b)
         work[0, pl.ds(e, 1), :] = image[pl.ds(column, 1), :]
     value = work[0, pl.ds(0, entries), :]
-    value = value * scales[pl.ds(pl.multiple_of(b * entries, SUB), entries), :]
+    value = value * scales[pl.ds(b * entries, entries), :]
     upper = value.astype(BF16).astype(F32)
-    times = times_ref[b]
+    times = times_ref[row * bins_y + b]
     middle = jnp.bitwise_and(jnp.right_shift(times, half_bits), 1)
     rows = pl.ds(0, entries)
     work[0, rows, :] = upper
@@ -141,19 +153,13 @@
 
 def main_kernel(
     geo,
-    unroll,
     row0,
-    col_ref,
+    entry_ref,
     times_ref,
-    old_times_ref,
-    res_times_ref,
     amp_ref,
-    res_amp_ref,
     counts_ref,
-    res_counts_ref,
-    old_place_ref,
-    last_place_ref,
-    res_place_ref,
+    parts_ref,
+    aper_ref,
     res_ref,
     mid_ref,
     left_ref,
@@ -176,57 +182,65 @@
     *works,
 ):
     bins_y, entries, highs, wide_y = geo
-    step = pl.program_id(0)
+    bins_x = amp_ref.shape[0]
     wide_x = mid_ref.shape[0]
-    groups = bins_y // unroll
-    res_bins = res_times_ref.shape[0]
-    res_unroll = res_bins // groups
-
-    @pl.when(step == 0)
-    def _():
-        s1_ref[...] = s1_in_ref[...]
-        s2_ref[...] = jnp.zeros_like(s2_ref)
-        curv_ref[...] = jnp.zeros_like(curv_ref)
-        old_data[...] = jnp.zeros_like(old_data)
-        scales[...] = jnp.zeros_like(scales)
+    rows_per = bins_y * highs
+    cut = bins_x // (bins_x - row0)
+    res_bins = bins_y // cut
+
+    s1_ref[...] = s1_in_ref[...]
+    s2_ref[...] = jnp.zeros_like(s2_ref)
+    old_data[...] = jnp.zeros_like(old_data)
+    scales[...] = jnp.zeros_like(scales)
+    for x in range(wide_x):
+        image[pl.ds(x * wide_y, RADIUS), :] = left_ref[x]
+        image[pl.ds(x * wide_y + RADIUS, bins_y), :] = mid_ref[x]
+        image[pl.ds(x * wide_y + RADIUS + bins_y, RADIUS), :] = right_ref[x]
+
+    def one_row(step, total):
+        before = jnp.maximum(step - 1, 0)
+        res_row = row0 + step // cut
+        res_part = (step % cut) * res_bins
+        res_first = pl.multiple_of(res_row * rows_per + res_part * highs, SUB)
+        old_scales[...] = scales[...]
+        fill_weights(amp_ref[step], counts_ref[pl.ds(step, 1), :], scales)
+        fill_weights(
+            amp_ref[res_row, pl.ds(pl.multiple_of(res_part, SUB), res_bins), :],
+            parts_ref[pl.ds(row0 * cut + step, 1), :],
+            res_scales,
+        )
+        for b in range(bins_y):
+            trace = scatter_bin(
+                geo, step, b, image, entry_ref, times_ref, scales, works[b % len(works)]
+            )
+            first = trace_row(b, highs)
+            data_ref[pl.ds(step * rows_per + first, highs, stride=SUB), :] = trace
+            total = total + trace * trace
+            sample_bin(
+                old_data, first, highs, times_ref, before * bins_y + b, b, old_scales, vals
+            )
+            if b % cut == 0:
+                r = b // cut
+                first = res_first + trace_row(r, highs)
+                at = res_row * bins_y + res_part + r
+                sample_bin(res_ref, first, highs, times_ref, at, r, res_scales, res_vals)
+        spread_bins(vals, place_row(aper_ref[before], wide_y), s2_ref, before, wide_y)
+        entry = aper_ref[res_row, pl.ds(pl.multiple_of(res_part, SUB), res_bins), :]
+        spread_bins(res_vals, place_row(entry, wide_y, res_part), s1_ref, res_row, wide_y)
+        old_data[...] = data_ref[pl.ds(pl.multiple_of(step * rows_per, SUB), rows_per), :]
+        return total
+
+    curv_ref[...] = lax.fori_loop(0, bins_x, one_row, jnp.zeros((highs, LANES), F32))
+    last = bins_x - 1
+    for b in range(bins_y):
+        at = last * bins_y + b
+        sample_bin(old_data, trace_row(b, highs), highs, times_ref, at, b, scales, vals)
+    spread_bins(vals, place_row(aper_ref[last], wide_y), s2_ref, last, wide_y)
+    for k, ref in enumerate((s1_ref, s2_ref)):
         for x in range(wide_x):
-            image[pl.ds(x * wide_y, RADIUS), :] = left_ref[x]
-            image[pl.ds(x * wide_y + RADIUS, bins_y), :] = mid_ref[x]
-            image[pl.ds(x * wide_y + RADIUS + bins_y, RADIUS), :] = right_ref[x]
-
-    old_scales[...] = scales[...]
-    fill_weights(amp_ref, counts_ref[pl.ds(step, 1), :], scales)
-    fill_weights(res_amp_ref, res_counts_ref[0], res_scales)
-
-    def some_bins(k, total):
-        for u in range(unroll):
-            b = k * unroll + u
-            trace = scatter_bin(geo, b, image, col_ref, times_ref, scales, works[u])
-            data_ref[pl.ds(trace_row(b, highs), highs, stride=SUB), :] = trace
-            total = total + trace * trace
-            first = trace_row(b, highs)
-            sample_bin(old_data, first, highs, old_times_ref, b, old_scales, vals)
-            if u < res_unroll:
-                r = k * res_unroll + u
-                first = trace_row(r, highs)
-                sample_bin(res_ref, first, highs, res_times_ref, r, res_scales, res_vals)
-        return total
-
-    curv_ref[...] += lax.fori_loop(0, groups, some_bins, jnp.zeros((highs, LANES), F32))
-    spread_bins(vals, old_place_ref, s2_ref, jnp.maximum(step - 1, 0), wide_y)
-    spread_bins(res_vals, res_place_ref, s1_ref, row0 + (step * res_bins) // bins_y, wide_y)
-    old_data[...] = data_ref[...]
-
-    @pl.when(step == pl.num_programs(0) - 1)
-    def _():
-        for b in range(bins_y):
-            sample_bin(old_data, trace_row(b, highs), highs, times_ref, b, scales, vals)
-        spread_bins(vals, last_place_ref, s2_ref, step, wide_y)
-        for k, ref in enumerate((s1_ref, s2_ref)):
-            for x in range(wide_x):
-                out_left[k, x] = ref[pl.ds(x * wide_y, RADIUS), :]
-                out_mid[k, x] = ref[pl.ds(x * wide_y + RADIUS, bins_y), :]
-                out_right[k, x] = ref[pl.ds(x * wide_y + RADIUS + bins_y, RADIUS), :]
+            out_left[k, x] = ref[pl.ds(x * wide_y, RADIUS), :]
+            out_mid[k, x] = ref[pl.ds(x * wide_y + RADIUS, bins_y), :]
+            out_right[k, x] = ref[pl.ds(x * wide_y + RADIUS + bins_y, RADIUS), :]
 
 
 def fold_y_kernel(mid_ref, low_ref, high_ref, out_head, out_mid, out_tail):
@@ -320,12 +334,7 @@
 
     times = travel_times.reshape(bins_x * bins_y, entries, depths)
     res_rows = to_rows(data_residual)
-    off = (aperture // SIDE) * wide_y + aperture % SIDE
-    window = off + jnp.arange(bins_y, dtype=jnp.int32)[None, :, None]
-    column = window + wide_y * jnp.arange(bins_x, dtype=jnp.int32)[:, None, None]
-    place = window.reshape(bins_x, 1, bins_y * entries)
-
-    def first(row0, count, prev):
+    def first(row0, count, prev, limit):
         return pl.pallas_call(
             functools.partial(first_kernel, geo, row0),
             grid=(count,),
@@ -334,98 +343,63 @@
                 pl.BlockSpec((bins_y, entries, depths), lambda i: (i + row0, 0, 0)),
                 pl.BlockSpec((1, bins_y, entries), lambda i: (i + row0, 0, 0)),
                 pl.BlockSpec((bins_x, bins_y), lambda i: (0, 0)),
-                pl.BlockSpec((1, 1, bins_y * entries), lambda i: (i + row0, 0, 0)),
-                pl.BlockSpec((columns, depths), lambda i: (0, 0)),
-            ],
+                pl.BlockSpec((1, bins_y, entries), lambda i: (i + row0, 0, 0)),
+            ]
+            + [pl.BlockSpec((columns, depths), lambda i: (0, 0))] * len(prev),
             out_specs=pl.BlockSpec((columns, depths), lambda i: (0, 0)),
             out_shape=jax.ShapeDtypeStruct((columns, depths), F32),
             scratch_shapes=[pltpu.VMEM((bins_y * entries, depths), F32)] * 2,
-            compiler_params=params(),
+            compiler_params=params(limit),
             cost_estimate=pl.CostEstimate(
                 flops=4 * 10**9, bytes_accessed=4 * 10**6, transcendentals=0
             ),
             name="sample_residual",
-        )(res_rows, times, amplitude, trace_counts, place, prev)
+        )(res_rows, times, amplitude, trace_counts, aperture, *prev)
 
     early = bins_x // 4
     row0 = 2 * early
-    s1 = first(0, early, jnp.zeros((columns, depths), F32))
+    s1 = first(0, early, (), FIRST_LIMIT)
     ext = jnp.concatenate([from_prev, direction, from_next], axis=0)
     tail, head, s1 = lax.optimization_barrier((ext[:, bins_y - RADIUS :], ext[:, :RADIUS], s1))
     left = shift(tail, "gy", 1)
     right = shift(head, "gy", -1)
-    s1 = first(early, early, s1)
-
-    unroll = 8
+    s1 = first(early, early, (s1,), VMEM_LIMIT)
+
     cut = bins_x // (bins_x - row0)
     res_bins = bins_y // cut
-    counts_cut = trace_counts.reshape(bins_x * cut, 1, res_bins)
-    whole3 = lambda i: (0, 0, 0)
-    whole4 = lambda i: (0, 0, 0, 0)
-    before = lambda i: (jnp.maximum(i - 1, 0), 0, 0)
-    this = lambda i: (i, 0, 0)
-    late = lambda i: (row0 * cut + i, 0, 0)
-    strip = (2, wide_x, RADIUS, depths)
-    middle = (2, wide_x, bins_y, depths)
+    parts = trace_counts.reshape(bins_x * cut, res_bins)
+    strip = jax.ShapeDtypeStruct((2, wide_x, RADIUS, depths), F32)
     vals_shape = pltpu.VMEM((bins_y * entries, depths), F32)
     res_shape = pltpu.VMEM((res_bins * entries, depths), F32)
     columns_shape = pltpu.VMEM((columns, depths), F32)
+    in_vmem = pl.BlockSpec(memory_space=pltpu.VMEM)
     data_rows, curv, out_left, out_mid, out_right = pl.pallas_call(
-        functools.partial(main_kernel, geo, unroll, row0),
-        grid=(bins_x,),
-        in_specs=[
-            pl.BlockSpec((1, bins_y, entries), this, memory_space=pltpu.SMEM),
-            pl.BlockSpec((bins_y, entries, depths), this),
-            pl.BlockSpec((bins_y, entries, depths), before),
-            pl.BlockSpec((res_bins, entries, depths), late),
-            pl.BlockSpec((1, bins_y, entries), this),
-            pl.BlockSpec((1, res_bins, entries), late),
-            pl.BlockSpec((bins_x, bins_y), lambda i: (0, 0)),
-            pl.BlockSpec((1, 1, res_bins), late),
-            pl.BlockSpec((1, 1, bins_y * entries), before),
-            pl.BlockSpec((1, 1, bins_y * entries), lambda i: (bins_x - 1, 0, 0)),
-            pl.BlockSpec((1, 1, res_bins * entries), late),
-            pl.BlockSpec((res_bins * highs, LANES), lambda i: (row0 * cut + i, 0)),
-            pl.BlockSpec((wide_x, bins_y, depths), whole3),
-            pl.BlockSpec((wide_x, RADIUS, depths), whole3),
-            pl.BlockSpec((wide_x, RADIUS, depths), whole3),
-            pl.BlockSpec((columns, depths), lambda i: (0, 0)),
-        ],
-        out_specs=[
-            pl.BlockSpec((rows_per, LANES), lambda i: (i, 0)),
-            pl.BlockSpec((highs, LANES), lambda i: (0, 0)),
-            pl.BlockSpec(strip, whole4),
-            pl.BlockSpec(middle, whole4),
-            pl.BlockSpec(strip, whole4),
-        ],
+        functools.partial(main_kernel, geo, row0),
+        in_specs=[pl.BlockSpec(memory_space=pltpu.SMEM)] + [in_vmem] * 10,
+        out_specs=[in_vmem] * 5,
         out_shape=[
             jax.ShapeDtypeStruct((bins_x * rows_per, LANES), F32),
             jax.ShapeDtypeStruct((highs, LANES), F32),
-            jax.ShapeDtypeStruct(strip, F32),
-            jax.ShapeDtypeStruct(middle, F32),
-            jax.ShapeDtypeStruct(strip, F32),
+            strip,
+            jax.ShapeDtypeStruct((2, wide_x, bins_y, depths), F32),
+            strip,
         ],
         scratch_shapes=[columns_shape, columns_shape, columns_shape]
         + [vals_shape, res_shape, vals_shape, vals_shape, res_shape]
         + [pltpu.VMEM((rows_per, LANES), F32)]
-        + [pltpu.VMEM((4, entries + SUB, LANES), F32)] * unroll,
+        + [pltpu.VMEM((4, entries + SUB, LANES), F32)] * 8,
         compiler_params=params(MAIN_LIMIT),
         cost_estimate=pl.CostEstimate(
             flops=20 * 10**9, bytes_accessed=8 * 10**6, transcendentals=0
         ),
         name="demigrate_and_sample",
     )(
-        column,
-        times,
-        times,
+        aperture,
         times,
         amplitude,
-        amplitude.reshape(bins_x * cut, res_bins, entries),
         trace_counts,
-        counts_cut,
-        place,
-        place,
-        place.reshape(bins_x * cut, 1, res_bins * entries),
+        parts,
+        aperture,
         res_rows,
         ext,
         left,
@@ -456,7 +430,7 @@
     )(inner, from_low, from_high, old_gradient, curv)
     stats = lax.all_to_all(stats, ("gx", "gy"), 0, 0, tiled=True)
 
-    steps = 8
+    steps = 4
     rows_step = bins_x * rows_per // steps
     x_step = bins_x // steps
     cells = pl.BlockSpec((x_step, bins_y, depths), lambda i: (i, 0, 0))

time: 103 us -> 98.4 us (0.955)
  Pallas kernels: 53.4 us -> 50.4 us
  other arithmetic: 1.08 us -> 0.02 us
    pallas_call x1, Pallas kernels: 37.6 us -> 35.1 us  [body(): pl.pallas_call(functools.partial(main_kernel, geo, row0), in_specs=[pl.Bl...]
    pallas_call x1, Pallas kernels: 3.65 us -> 2.26 us  [body(): pl.pallas_call(last_kernel, grid=(steps,), in_specs=[pl.BlockSpec(stats.s...]
    add x1 -> x0, other arithmetic: 1.05 us -> none  [body(): window + wide_y * jnp.arange(bins_x, dtype=jnp.int32)[:, None, None]]
  transfers between devices with their start and end apart: 8 -> 8, of which waited for: 3 -> 3; matrix products, arithmetic and copies ran while one was open for 1% -> 0% of each run, Pallas kernels for 12% -> 13%
where the time goes in v5:
time: 98.4 us; the launch traced here: 98 us
  Pallas kernels  50.4 us (51%)
  starting transfers between devices  21.8 us (22%)
  blocking collectives  14.8 us (15%)
  waiting for transfers between devices  8.9 us (9%)
  local copies, waits for them, and re-layouts  1.18 us (1%)
    pallas_call x1, Pallas kernels, body(): pl.pallas_call(functools.partial(main_kernel, geo, row0), in_specs=[pl.Bl...  35.1 us
    ppermute x8, starting transfers between devices, shift(): return lax.ppermute(cells, axis, pairs)  21.8 us
    all_to_all x1, blocking collectives, body(): stats = lax.all_to_all(stats, ('gx', 'gy'), 0, 0, tiled=True)  14.8 us
    pallas_call x2, Pallas kernels, first(): pl.pallas_call(functools.partial(first_kernel, geo, row0), grid=(count,),...  12.7 us
    ppermute x8, waiting for transfers between devices, shift(): return lax.ppermute(cells, axis, pairs)  8.9 us
    pallas_call x1, Pallas kernels, body(): pl.pallas_call(last_kernel, grid=(steps,), in_specs=[pl.BlockSpec(stats.s...  2.26 us
  transfers between devices with their start and end apart: 8, of which 3 were waited for; matrix products, arithmetic and copies ran while one was open for 0% of the time, Pallas kernels for 13%

profile of v5, /device:TPU:0, one launch (start us, length us, event | category | flops | bytes accessed | tf_op | source)
XLA Modules:
  0.0 98.0 jit_solution(8894244595199321287)
XLA Ops:
  0.6 1.3 %collective-permute-start.1 = (f32[16,16,128]{2,1,0:T(8,128)}, f32[16,16,128]{2,1,0:T(8,128)S(1)}, u32[]{:S(2)}, u32[]{:S(2)}) collective-permute-start(f32[16,16,128]{2,1,0:T(8,128)} %dir_ref.1), channel_id=1, source_target_pairs={{4,0},{8,4},{12,8},{16,12},{20,16},{24,20},{28,24},{5,1},{9,5},{13... | collective-permute-start | bytes 393224 | tf_op jit(solution)/shard_map/ppermute | solution.py:310
  1.9 5.5 %collective-permute-start = (f32[16,16,128]{2,1,0:T(8,128)}, f32[16,16,128]{2,1,0:T(8,128)S(1)}, u32[]{:S(2)}, u32[]{:S(2)}) collective-permute-start(f32[16,16,128]{2,1,0:T(8,128)} %dir_ref.1), channel_id=1, source_target_pairs={{0,4},{4,8},{8,12},{12,16},{16,20},{20,24},{24,28},{1,5},{5,9},{9,... | collective-permute-start | bytes 393224 | tf_op jit(solution)/shard_map/ppermute | solution.py:310
  7.4 0.0 copy-start.4
  7.4 0.0 copy-start.1
  7.4 0.0 copy-start.6
  7.4 0.0 copy-start.7
  7.5 6.8 %sample_residual.2.refs_0_ = f32[1024,128]{1,0:T(8,128)} custom-call(f32[4096,128]{1,0:T(8,128)} %bitcast.11, s32[256,16,128]{2,1,0:T(8,128)} %bitcast.15, f32[16,16,16]{2,1,0:T(8,128)} %amp_ref.5, s32[16,16]{1,0:T(8,128)} %counts_ref.5, s32[16,16,16]{2,1,0:T(8,128)} %aper_ref.5), custom_call_target="tpu_custom_call" | custom-call | flops 4000000000 | bytes 4000000 | tf_op jit(solution)/shard_map/sample_residual/pallas_call | solution.py:338
  14.3 0.0 copy-done.4
  14.3 0.1 reshape.25.parts_ref
  14.3 0.0 collective-permute-done.1
  14.4 0.0 collective-permute-done
  14.4 0.0 copy-done.1
  14.4 0.0 copy-start
  14.5 0.0 copy-start.5
  14.5 1.9 %collective-permute-start.2 = (f32[32,8,128]{2,1,0:T(8,128)S(1)}, f32[32,8,128]{2,1,0:T(8,128)S(1)}, u32[]{:S(2)}, u32[]{:S(2)}) collective-permute-start(f32[32,8,128]{2,1,0:T(8,128)S(1)} %get-tuple-element.19), channel_id=1, source_target_pairs={{0,1},{1,2},{2,3},{4,5},{5,6},{6,7},{8,9},{9,10},{10,11},{12,13},{... | collective-permute-start | bytes 393224 | tf_op jit(solution)/shard_map/ppermute | solution.py:310
  16.3 1.3 %collective-permute-start.3 = (f32[32,8,128]{2,1,0:T(8,128)S(1)}, f32[32,8,128]{2,1,0:T(8,128)S(1)}, u32[]{:S(2)}, u32[]{:S(2)}) collective-permute-start(f32[32,8,128]{2,1,0:T(8,128)S(1)} %get-tuple-element.20), channel_id=1, source_target_pairs={{1,0},{2,1},{3,2},{5,4},{6,5},{7,6},{9,8},{10,9},{11,10},{13,12},{... | collective-permute-start | bytes 393224 | tf_op jit(solution)/shard_map/ppermute | solution.py:310
  17.6 0.0 copy-done.6
  17.6 0.0 copy-done.7
  17.7 0.0 copy-start.8
  17.7 1.0 %copy-done.8 = f32[1024,128]{1,0:T(8,128)S(1)} copy-done((f32[1024,128]{1,0:T(8,128)S(1)}, f32[1024,128]{1,0:T(8,128)}, u32[]{:S(2)}) %copy-start.8) | copy-done | bytes 524312
  18.7 5.9 %sample_residual.3.s1_in_ref = f32[1024,128]{1,0:T(8,128)S(1)} custom-call(f32[4096,128]{1,0:T(8,128)} %bitcast.12, s32[256,16,128]{2,1,0:T(8,128)} %bitcast.16, f32[16,16,16]{2,1,0:T(8,128)S(1)} %copy-done.7, s32[16,16]{1,0:T(8,128)S(1)} %copy-done.4, s32[16,16,16]{2,1,0:T(8,128)S(1)} %copy-done.6, f32[1024,128]{1,0:T(8,128)S(1)} %copy-done.8), custom_call_target="tpu_custom_call" | custom-call | flops 4000000000 | bytes 4000000 | tf_op jit(solution)/shard_map/sample_residual/pallas_call | solution.py:338
  24.6 0.0 copy-start.3
  24.7 0.0 copy-start.2
  24.7 0.0 collective-permute-done.2.left_ref
  24.7 0.0 collective-permute-done.3.right_ref
  24.7 0.0 copy-done
  24.7 0.0 copy-done.5
  24.7 35.1 %demigrate_and_sample.1 = (f32[4096,128]{1,0:T(8,128)S(1)}, f32[16,128]{1,0:T(8,128)S(1)}, f32[2,32,8,128]{3,2,1,0:T(8,128)S(1)}, f32[2,32,16,128]{3,2,1,0:T(8,128)S(1)}, f32[2,32,8,128]{3,2,1,0:T(8,128)S(1)}) custom-call(s32[16,16,16]{2,1,0:T(8,128)S(1)} %copy-done.6, s32[256,16,128]{2,1,0:T(8,128)S(1)} %bitcast.17, f32[16,16,16]{2,1,0:T(8,128)S(1)} %copy-done.7, ...), custom_call_target="tpu_custom_call" | custom-call | flops 20000000000 | bytes 8000000 | tf_op jit(solution)/shard_map/demigrate_and_sample/pallas_call | solution.py:376
  59.8 5.0 %collective-permute-start.4 = (f32[2,32,8,128]{3,2,1,0:T(8,128)S(1)}, f32[2,32,8,128]{3,2,1,0:T(8,128)S(1)}, u32[]{:S(2)}, u32[]{:S(2)}) collective-permute-start(f32[2,32,8,128]{3,2,1,0:T(8,128)S(1)} %get-tuple-element.23), channel_id=1, source_target_pairs={{0,1},{1,2},{2,3},{4,5},{5,6},{6,7},{8,9},{9,10},{10,11},{12,13},{... | collective-permute-start | bytes 786440 | tf_op jit(solution)/shard_map/ppermute | solution.py:310
  64.9 1.3 %collective-permute-start.5 = (f32[2,32,8,128]{3,2,1,0:T(8,128)S(1)}, f32[2,32,8,128]{3,2,1,0:T(8,128)S(1)}, u32[]{:S(2)}, u32[]{:S(2)}) collective-permute-start(f32[2,32,8,128]{3,2,1,0:T(8,128)S(1)} %get-tuple-element.24), channel_id=1, source_target_pairs={{1,0},{2,1},{3,2},{5,4},{6,5},{7,6},{9,8},{10,9},{11,10},{13,12},{... | collective-permute-start | bytes 786440 | tf_op jit(solution)/shard_map/ppermute | solution.py:310
  66.2 0.0 collective-permute-done.4.low_ref
  66.2 3.3 %collective-permute-done.5.high_ref = f32[2,32,8,128]{3,2,1,0:T(8,128)S(1)} collective-permute-done((f32[2,32,8,128]{3,2,1,0:T(8,128)S(1)}, f32[2,32,8,128]{3,2,1,0:T(8,128)S(1)}, u32[]{:S(2)}, u32[]{:S(2)}) %collective-permute-start.5) | collective-permute-done | bytes 262176 | tf_op jit(solution)/shard_map/ppermute | solution.py:310
  69.5 0.1 fold_y.1
  69.6 4.3 %collective-permute-start.6 = (f32[2,8,16,128]{3,2,1,0:T(8,128)S(1)}, f32[2,8,16,128]{3,2,1,0:T(8,128)S(1)}, u32[]{:S(2)}, u32[]{:S(2)}) collective-permute-start(f32[2,8,16,128]{3,2,1,0:T(8,128)S(1)} %get-tuple-element.26), channel_id=1, source_target_pairs={{0,4},{4,8},{8,12},{12,16},{16,20},{20,24},{24,28},{1,5},{5,9},{9,... | collective-permute-start | bytes 393224 | tf_op jit(solution)/shard_map/ppermute | solution.py:310
  73.9 1.3 %collective-permute-start.7 = (f32[2,8,16,128]{3,2,1,0:T(8,128)S(1)}, f32[2,8,16,128]{3,2,1,0:T(8,128)S(1)}, u32[]{:S(2)}, u32[]{:S(2)}) collective-permute-start(f32[2,8,16,128]{3,2,1,0:T(8,128)S(1)} %get-tuple-element.27), channel_id=1, source_target_pairs={{4,0},{8,4},{12,8},{16,12},{20,16},{24,20},{28,24},{5,1},{9,5},{13... | collective-permute-start | bytes 393224 | tf_op jit(solution)/shard_map/ppermute | solution.py:310
  75.2 1.2 %collective-permute-done.6.low_ref = f32[2,8,16,128]{3,2,1,0:T(8,128)S(1)} collective-permute-done((f32[2,8,16,128]{3,2,1,0:T(8,128)S(1)}, f32[2,8,16,128]{3,2,1,0:T(8,128)S(1)}, u32[]{:S(2)}, u32[]{:S(2)}) %collective-permute-start.6) | collective-permute-done | bytes 131104 | tf_op jit(solution)/shard_map/ppermute | solution.py:310
  76.4 4.4 %collective-permute-done.7.high_ref = f32[2,8,16,128]{3,2,1,0:T(8,128)S(1)} collective-permute-done((f32[2,8,16,128]{3,2,1,0:T(8,128)S(1)}, f32[2,8,16,128]{3,2,1,0:T(8,128)S(1)}, u32[]{:S(2)}, u32[]{:S(2)}) %collective-permute-start.7) | collective-permute-done | bytes 131104 | tf_op jit(solution)/shard_map/ppermute | solution.py:310
  80.8 0.0 copy-done.3
  80.8 0.2 fold_x.1
  80.9 14.8 %all_to_all.5.stats_ref = f32[32,1,128]{2,1,0:T(1,128)S(1)} all-to-all(f32[32,1,128]{2,1,0:T(1,128)S(1)} %get-tuple-element.29), channel_id=1, replica_groups=mesh['gx'=8,'gy'=4] {'gx','gy'}, dimensions={0} | all-to-all | bytes 32768 | tf_op jit(solution)/shard_map/all_to_all | solution.py:431
  95.7 0.0 copy-done.2
  95.8 2.3 %update.1 = (f32[16,16,128]{2,1,0:T(8,128)}, f32[4096,128]{1,0:T(8,128)}, f32[16,16,128]{2,1,0:T(8,128)}) custom-call(f32[32,1,128]{2,1,0:T(1,128)S(1)} %all_to_all.5.stats_ref, f32[4096,128]{1,0:T(8,128)S(1)} %bitcast.14, f32[4096,128]{1,0:T(8,128)S(1)} %get-tuple-element.30.data_ref, f32[16,16,128]{2,1,0:T(8,128)S(1)} %copy-done.2, ...), custom_call_target="tpu_custom_call" | custom-call | tf_op jit(solution)/shard_map/update/pallas_call | solution.py:439
  (4 shorter events, 0.1 us)
Async XLA Ops:
  0.6 13.7 %collective-permute-start.1 = (f32[16,16,128]{2,1,0:T(8,128)}, f32[16,16,128]{2,1,0:T(8,128)S(1)}, u32[]{:S(2)}, u32[]{:S(2)}) collective-permute-start(f32[16,16,128]{2,1,0:T(8,128)} %dir_ref.1), channel_id=1, source_target_pairs={{4,0},{8,4},{12,8},{16,12},{20,16},{24,20},{28,24},{5,1},{9,5},{13... | collective-permute-start | bytes 393224 | tf_op jit(solution)/shard_map/ppermute | solution.py:310
  1.9 12.4 %collective-permute-start = (f32[16,16,128]{2,1,0:T(8,128)}, f32[16,16,128]{2,1,0:T(8,128)S(1)}, u32[]{:S(2)}, u32[]{:S(2)}) collective-permute-start(f32[16,16,128]{2,1,0:T(8,128)} %dir_ref.1), channel_id=1, source_target_pairs={{0,4},{4,8},{8,12},{12,16},{16,20},{20,24},{24,28},{1,5},{5,9},{9,... | collective-permute-start | bytes 393224 | tf_op jit(solution)/shard_map/ppermute | solution.py:310
  7.4 6.9 %copy-start.4 = (s32[16,16]{1,0:T(8,128)S(1)}, s32[16,16]{1,0:T(8,128)}, u32[]{:S(2)}) copy-start(s32[16,16]{1,0:T(8,128)} %counts_ref.5) | copy-start | bytes 3076
  7.4 7.0 %copy-start.1 = (f32[16,16,128]{2,1,0:T(8,128)S(1)}, f32[16,16,128]{2,1,0:T(8,128)}, u32[]{:S(2)}) copy-start(f32[16,16,128]{2,1,0:T(8,128)} %dir_ref.1) | copy-start | bytes 393220
  7.4 10.2 %copy-start.6 = (s32[16,16,16]{2,1,0:T(8,128)S(1)}, s32[16,16,16]{2,1,0:T(8,128)}, u32[]{:S(2)}) copy-start(s32[16,16,16]{2,1,0:T(8,128)} %aper_ref.5) | copy-start | bytes 49156
  7.4 10.2 %copy-start.7 = (f32[16,16,16]{2,1,0:T(8,128)S(1)}, f32[16,16,16]{2,1,0:T(8,128)}, u32[]{:S(2)}) copy-start(f32[16,16,16]{2,1,0:T(8,128)} %amp_ref.5) | copy-start | bytes 49156
  14.4 10.2 %copy-start = (f32[16,16,2048]{2,1,0:T(8,128)S(1)}, f32[16,16,2048]{2,1,0:T(8,128)}, u32[]{:S(2)}) copy-start(f32[16,16,2048]{2,1,0:T(8,128)} %param.9) | copy-start | bytes 6291460
  14.5 10.2 %copy-start.5 = (s32[16,16,16,128]{3,2,1,0:T(8,128)S(1)}, s32[16,16,16,128]{3,2,1,0:T(8,128)}, u32[]{:S(2)}) copy-start(s32[16,16,16,128]{3,2,1,0:T(8,128)} %param.13) | copy-start | bytes 6291460
  14.5 10.2 %collective-permute-start.2 = (f32[32,8,128]{2,1,0:T(8,128)S(1)}, f32[32,8,128]{2,1,0:T(8,128)S(1)}, u32[]{:S(2)}, u32[]{:S(2)}) collective-permute-start(f32[32,8,128]{2,1,0:T(8,128)S(1)} %get-tuple-element.19), channel_id=1, source_target_pairs={{0,1},{1,2},{2,3},{4,5},{5,6},{6,7},{8,9},{9,10},{10,11},{12,13},{... | collective-permute-start | bytes 393224 | tf_op jit(solution)/shard_map/ppermute | solution.py:310
  16.3 8.3 %collective-permute-start.3 = (f32[32,8,128]{2,1,0:T(8,128)S(1)}, f32[32,8,128]{2,1,0:T(8,128)S(1)}, u32[]{:S(2)}, u32[]{:S(2)}) collective-permute-start(f32[32,8,128]{2,1,0:T(8,128)S(1)} %get-tuple-element.20), channel_id=1, source_target_pairs={{1,0},{2,1},{3,2},{5,4},{6,5},{7,6},{9,8},{10,9},{11,10},{13,12},{... | collective-permute-start | bytes 393224 | tf_op jit(solution)/shard_map/ppermute | solution.py:310
  17.7 1.0 %copy-start.8 = (f32[1024,128]{1,0:T(8,128)S(1)}, f32[1024,128]{1,0:T(8,128)}, u32[]{:S(2)}) copy-start(f32[1024,128]{1,0:T(8,128)} %sample_residual.2.refs_0_) | copy-start | bytes 1572868
  24.6 56.1 %copy-start.3 = (f32[16,16,128]{2,1,0:T(8,128)S(1)}, f32[16,16,128]{2,1,0:T(8,128)}, u32[]{:S(2)}) copy-start(f32[16,16,128]{2,1,0:T(8,128)} %grad_ref.1) | copy-start | bytes 393220
  24.7 71.1 %copy-start.2 = (f32[16,16,128]{2,1,0:T(8,128)S(1)}, f32[16,16,128]{2,1,0:T(8,128)}, u32[]{:S(2)}) copy-start(f32[16,16,128]{2,1,0:T(8,128)} %model_ref.1) | copy-start | bytes 393220
  59.8 6.3 %collective-permute-start.4 = (f32[2,32,8,128]{3,2,1,0:T(8,128)S(1)}, f32[2,32,8,128]{3,2,1,0:T(8,128)S(1)}, u32[]{:S(2)}, u32[]{:S(2)}) collective-permute-start(f32[2,32,8,128]{3,2,1,0:T(8,128)S(1)} %get-tuple-element.23), channel_id=1, source_target_pairs={{0,1},{1,2},{2,3},{4,5},{5,6},{6,7},{8,9},{9,10},{10,11},{12,13},{... | collective-permute-start | bytes 786440 | tf_op jit(solution)/shard_map/ppermute | solution.py:310
  64.9 4.6 %collective-permute-start.5 = (f32[2,32,8,128]{3,2,1,0:T(8,128)S(1)}, f32[2,32,8,128]{3,2,1,0:T(8,128)S(1)}, u32[]{:S(2)}, u32[]{:S(2)}) collective-permute-start(f32[2,32,8,128]{3,2,1,0:T(8,128)S(1)} %get-tuple-element.24), channel_id=1, source_target_pairs={{1,0},{2,1},{3,2},{5,4},{6,5},{7,6},{9,8},{10,9},{11,10},{13,12},{... | collective-permute-start | bytes 786440 | tf_op jit(solution)/shard_map/ppermute | solution.py:310
  69.6 6.8 %collective-permute-start.6 = (f32[2,8,16,128]{3,2,1,0:T(8,128)S(1)}, f32[2,8,16,128]{3,2,1,0:T(8,128)S(1)}, u32[]{:S(2)}, u32[]{:S(2)}) collective-permute-start(f32[2,8,16,128]{3,2,1,0:T(8,128)S(1)} %get-tuple-element.26), channel_id=1, source_target_pairs={{0,4},{4,8},{8,12},{12,16},{16,20},{20,24},{24,28},{1,5},{5,9},{9,... | collective-permute-start | bytes 393224 | tf_op jit(solution)/shard_map/ppermute | solution.py:310
  73.9 6.9 %collective-permute-start.7 = (f32[2,8,16,128]{3,2,1,0:T(8,128)S(1)}, f32[2,8,16,128]{3,2,1,0:T(8,128)S(1)}, u32[]{:S(2)}, u32[]{:S(2)}) collective-permute-start(f32[2,8,16,128]{3,2,1,0:T(8,128)S(1)} %get-tuple-element.27), channel_id=1, source_target_pairs={{4,0},{8,4},{12,8},{16,12},{20,16},{24,20},{28,24},{5,1},{9,5},{13... | collective-permute-start | bytes 393224 | tf_op jit(solution)/shard_map/ppermute | solution.py:310

commit v6 on v5

--- a/solution.py
+++ b/solution.py
@@ -14,7 +14,7 @@
 F32 = jnp.float32
 BF16 = jnp.bfloat16
 VMEM_LIMIT = 51 * 1024 * 1024
-FIRST_LIMIT = 60 * 1024 * 1024
+FIRST_LIMIT = 59 * 1024 * 1024
 MAIN_LIMIT = 36 * 1024 * 1024
 SMALL_LIMIT = 24 * 1024 * 1024
 
@@ -49,14 +49,14 @@
 
 def sample_bin(source, first, highs, times_ref, bin_at, b, scales, vals):
     entries = times_ref.shape[1]
+    tables = [source[pl.ds(first + SUB * h, SUB, stride=0), :] for h in range(highs)]
     for part in range(0, entries, SUB):
         times = times_ref[bin_at, pl.ds(part, SUB), :]
         high = jnp.right_shift(times, LANES.bit_length() - 1)
         low = jnp.bitwise_and(times, LANES - 1)
         acc = jnp.zeros(times.shape, F32)
         for h in range(highs):
-            table = source[pl.ds(first + SUB * h, SUB, stride=0), :]
-            got = jnp.take_along_axis(table, low, axis=1, mode="promise_in_bounds")
+            got = jnp.take_along_axis(tables[h], low, axis=1, mode="promise_in_bounds")
             acc = jnp.where(high == h, got, acc)
         at = b * entries + part
         at = pl.ds(at if isinstance(at, int) else pl.multiple_of(at, SUB), SUB)
@@ -74,12 +74,15 @@
     )
 
 
-def spread_bins(vals, place, s_ref, row, wide_y):
-    span = SIDE * wide_y
+def split_values(vals):
     value = vals[...]
     upper = value.astype(BF16)
     lower = (value - upper.astype(F32)).astype(BF16)
-    both = jnp.concatenate([upper, lower], axis=1)
+    return jnp.concatenate([upper, lower], axis=1)
+
+
+def spread_bins(both, place, s_ref, row, wide_y):
+    span = SIDE * wide_y
     iota = lax.broadcasted_iota(jnp.int32, (span, place.shape[1]), 0)
     table = jnp.where(iota == place, 1.0, 0.0).astype(BF16)
     part = jnp.dot(table, both, preferred_element_type=F32)
@@ -87,20 +90,20 @@
 
 
 def first_kernel(
-    geo, row0, res_ref, times_ref, amp_ref, counts_ref, aper_ref, *refs
+    geo, row0, res_ref, times_ref, amp_ref, counts_ref, aper_ref, s_ref, vals, scales
 ):
     bins_y, entries, highs, wide_y = geo
     step = pl.program_id(0)
-    s_ref, vals, scales = refs[-3:]
 
     @pl.when(step == 0)
     def _():
-        s_ref[...] = refs[0][...] if len(refs) > 3 else jnp.zeros_like(s_ref)
+        s_ref[...] = jnp.zeros_like(s_ref)
 
     fill_weights(amp_ref[0], counts_ref[pl.ds(step + row0, 1), :], scales)
     for b in range(bins_y):
         sample_bin(res_ref, trace_row(b, highs), highs, times_ref, b, b, scales, vals)
-    spread_bins(vals, place_row(aper_ref[0], wide_y), s_ref, step + row0, wide_y)
+    both = split_values(vals)
+    spread_bins(both, place_row(aper_ref[0], wide_y), s_ref, step + row0, wide_y)
 
 
 def scatter_bin(geo, row, b, image, entry_ref, times_ref, scales, work):
@@ -165,6 +168,7 @@
     left_ref,
     right_ref,
     s1_in_ref,
+    s1_more_ref,
     data_ref,
     curv_ref,
     out_left,
@@ -179,6 +183,8 @@
     old_scales,
     res_scales,
     old_data,
+    both,
+    res_both,
     *works,
 ):
     bins_y, entries, highs, wide_y = geo
@@ -188,19 +194,33 @@
     cut = bins_x // (bins_x - row0)
     res_bins = bins_y // cut
 
-    s1_ref[...] = s1_in_ref[...]
+    s1_ref[...] = s1_in_ref[...] + s1_more_ref[...]
     s2_ref[...] = jnp.zeros_like(s2_ref)
     old_data[...] = jnp.zeros_like(old_data)
     scales[...] = jnp.zeros_like(scales)
+    both[...] = jnp.zeros_like(both)
+    res_both[...] = jnp.zeros_like(res_both)
     for x in range(wide_x):
         image[pl.ds(x * wide_y, RADIUS), :] = left_ref[x]
         image[pl.ds(x * wide_y + RADIUS, bins_y), :] = mid_ref[x]
         image[pl.ds(x * wide_y + RADIUS + bins_y, RADIUS), :] = right_ref[x]
 
+    def residual_part(step):
+        return row0 + step // cut, (step % cut) * res_bins
+
+    def spread_image(row):
+        spread_bins(both[...], place_row(aper_ref[row], wide_y), s2_ref, row, wide_y)
+
+    def spread_residual(step):
+        row, part = residual_part(step)
+        entry = aper_ref[row, pl.ds(pl.multiple_of(part, SUB), res_bins), :]
+        spread_bins(res_both[...], place_row(entry, wide_y, part), s1_ref, row, wide_y)
+
     def one_row(step, total):
         before = jnp.maximum(step - 1, 0)
-        res_row = row0 + step // cut
-        res_part = (step % cut) * res_bins
+        spread_image(jnp.maximum(step - 2, 0))
+        spread_residual(before)
+        res_row, res_part = residual_part(step)
         res_first = pl.multiple_of(res_row * rows_per + res_part * highs, SUB)
         old_scales[...] = scales[...]
         fill_weights(amp_ref[step], counts_ref[pl.ds(step, 1), :], scales)
@@ -224,18 +244,20 @@
                 first = res_first + trace_row(r, highs)
                 at = res_row * bins_y + res_part + r
                 sample_bin(res_ref, first, highs, times_ref, at, r, res_scales, res_vals)
-        spread_bins(vals, place_row(aper_ref[before], wide_y), s2_ref, before, wide_y)
-        entry = aper_ref[res_row, pl.ds(pl.multiple_of(res_part, SUB), res_bins), :]
-        spread_bins(res_vals, place_row(entry, wide_y, res_part), s1_ref, res_row, wide_y)
+        both[...] = split_values(vals)
+        res_both[...] = split_values(res_vals)
         old_data[...] = data_ref[pl.ds(pl.multiple_of(step * rows_per, SUB), rows_per), :]
         return total
 
     curv_ref[...] = lax.fori_loop(0, bins_x, one_row, jnp.zeros((highs, LANES), F32))
     last = bins_x - 1
+    spread_image(last - 1)
+    spread_residual(last)
     for b in range(bins_y):
         at = last * bins_y + b
         sample_bin(old_data, trace_row(b, highs), highs, times_ref, at, b, scales, vals)
-    spread_bins(vals, place_row(aper_ref[last], wide_y), s2_ref, last, wide_y)
+    both[...] = split_values(vals)
+    spread_image(last)
     for k, ref in enumerate((s1_ref, s2_ref)):
         for x in range(wide_x):
             out_left[k, x] = ref[pl.ds(x * wide_y, RADIUS), :]
@@ -334,7 +356,7 @@
 
     times = travel_times.reshape(bins_x * bins_y, entries, depths)
     res_rows = to_rows(data_residual)
-    def first(row0, count, prev, limit):
+    def first(row0, count, counts, limit):
         return pl.pallas_call(
             functools.partial(first_kernel, geo, row0),
             grid=(count,),
@@ -344,8 +366,7 @@
                 pl.BlockSpec((1, bins_y, entries), lambda i: (i + row0, 0, 0)),
                 pl.BlockSpec((bins_x, bins_y), lambda i: (0, 0)),
                 pl.BlockSpec((1, bins_y, entries), lambda i: (i + row0, 0, 0)),
-            ]
-            + [pl.BlockSpec((columns, depths), lambda i: (0, 0))] * len(prev),
+            ],
             out_specs=pl.BlockSpec((columns, depths), lambda i: (0, 0)),
             out_shape=jax.ShapeDtypeStruct((columns, depths), F32),
             scratch_shapes=[pltpu.VMEM((bins_y * entries, depths), F32)] * 2,
@@ -354,16 +375,18 @@
                 flops=4 * 10**9, bytes_accessed=4 * 10**6, transcendentals=0
             ),
             name="sample_residual",
-        )(res_rows, times, amplitude, trace_counts, aperture, *prev)
+        )(res_rows, times, amplitude, counts, aperture)
 
     early = bins_x // 4
     row0 = 2 * early
-    s1 = first(0, early, (), FIRST_LIMIT)
+    s1 = first(0, early, trace_counts, FIRST_LIMIT)
     ext = jnp.concatenate([from_prev, direction, from_next], axis=0)
-    tail, head, s1 = lax.optimization_barrier((ext[:, bins_y - RADIUS :], ext[:, :RADIUS], s1))
+    tail, head, s1, counts = lax.optimization_barrier(
+        (ext[:, bins_y - RADIUS :], ext[:, :RADIUS], s1, trace_counts)
+    )
     left = shift(tail, "gy", 1)
     right = shift(head, "gy", -1)
-    s1 = first(early, early, (s1,), VMEM_LIMIT)
+    s1_more = first(early, early, counts, VMEM_LIMIT)
 
     cut = bins_x // (bins_x - row0)
     res_bins = bins_y // cut
@@ -375,7 +398,7 @@
     in_vmem = pl.BlockSpec(memory_space=pltpu.VMEM)
     data_rows, curv, out_left, out_mid, out_right = pl.pallas_call(
         functools.partial(main_kernel, geo, row0),
-        in_specs=[pl.BlockSpec(memory_space=pltpu.SMEM)] + [in_vmem] * 10,
+        in_specs=[pl.BlockSpec(memory_space=pltpu.SMEM)] + [in_vmem] * 11,
         out_specs=[in_vmem] * 5,
         out_shape=[
             jax.ShapeDtypeStruct((bins_x * rows_per, LANES), F32),
@@ -387,6 +410,8 @@
         scratch_shapes=[columns_shape, columns_shape, columns_shape]
         + [vals_shape, res_shape, vals_shape, vals_shape, res_shape]
         + [pltpu.VMEM((rows_per, LANES), F32)]
+        + [pltpu.VMEM((bins_y * entries, 2 * depths), BF16)]
+        + [pltpu.VMEM((res_bins * entries, 2 * depths), BF16)]
         + [pltpu.VMEM((4, entries + SUB, LANES), F32)] * 8,
         compiler_params=params(MAIN_LIMIT),
         cost_estimate=pl.CostEstimate(
@@ -405,6 +430,7 @@
         left,
         right,
         s1,
+        s1_more,
     )
 
     from_low = shift(out_right, "gy", 1)

time: 98.4 us -> 94.2 us (0.957)
  Pallas kernels: 50.4 us -> 47.4 us
  local copies, waits for them, and re-layouts: 1.18 us -> 0.15 us
    pallas_call x1, Pallas kernels: 35.1 us -> 32.1 us  [body(): pl.pallas_call(functools.partial(main_kernel, geo, row0), in_specs=[pl.Bl...]
    unnamed x18, local copies, waits for them, and re-layouts: 1.08 us -> 0.05 us
  transfers between devices with their start and end apart: 8 -> 8, of which waited for: 3 -> 3; matrix products, arithmetic and copies ran while one was open for 0% -> 0% of each run, Pallas kernels for 13% -> 14%
where the time goes in v6:
time: 94.2 us; the launch traced here: 93.9 us
  Pallas kernels  47.4 us (50%)
  starting transfers between devices  21.7 us (23%)
  blocking collectives  14.8 us (16%)
  waiting for transfers between devices  8.92 us (9%)
    pallas_call x1, Pallas kernels, body(): pl.pallas_call(functools.partial(main_kernel, geo, row0), in_specs=[pl.Bl...  32.1 us
    ppermute x8, starting transfers between devices, shift(): return lax.ppermute(cells, axis, pairs)  21.7 us
    all_to_all x1, blocking collectives, body(): stats = lax.all_to_all(stats, ('gx', 'gy'), 0, 0, tiled=True)  14.8 us
    pallas_call x2, Pallas kernels, first(): pl.pallas_call(functools.partial(first_kernel, geo, row0), grid=(count,),...  12.8 us
    ppermute x8, waiting for transfers between devices, shift(): return lax.ppermute(cells, axis, pairs)  8.92 us
    pallas_call x1, Pallas kernels, body(): pl.pallas_call(last_kernel, grid=(steps,), in_specs=[pl.BlockSpec(stats.s...  2.24 us
  transfers between devices with their start and end apart: 8, of which 3 were waited for; matrix products, arithmetic and copies ran while one was open for 0% of the time, Pallas kernels for 14%

profile of v6, /device:TPU:0, one launch (start us, length us, event | category | flops | bytes accessed | tf_op | source)
XLA Modules:
  0.0 93.9 jit_solution(17130410968995811518)
XLA Ops:
  0.6 1.3 %collective-permute-start.1 = (f32[16,16,128]{2,1,0:T(8,128)}, f32[16,16,128]{2,1,0:T(8,128)S(1)}, u32[]{:S(2)}, u32[]{:S(2)}) collective-permute-start(f32[16,16,128]{2,1,0:T(8,128)} %dir_ref.1), channel_id=1, source_target_pairs={{4,0},{8,4},{12,8},{16,12},{20,16},{24,20},{28,24},{5,1},{9,5},{13... | collective-permute-start | bytes 393224 | tf_op jit(solution)/shard_map/ppermute | solution.py:332
  1.9 5.5 %collective-permute-start = (f32[16,16,128]{2,1,0:T(8,128)}, f32[16,16,128]{2,1,0:T(8,128)S(1)}, u32[]{:S(2)}, u32[]{:S(2)}) collective-permute-start(f32[16,16,128]{2,1,0:T(8,128)} %dir_ref.1), channel_id=1, source_target_pairs={{0,4},{4,8},{8,12},{12,16},{16,20},{20,24},{24,28},{1,5},{5,9},{9,... | collective-permute-start | bytes 393224 | tf_op jit(solution)/shard_map/ppermute | solution.py:332
  7.4 0.0 copy-start.4
  7.4 0.0 copy-start.1
  7.4 0.0 copy-start
  7.4 0.0 copy-start.6
  7.5 0.0 copy-start.7
  7.5 6.9 %sample_residual.2.s1_in_ref = f32[1024,128]{1,0:T(8,128)} custom-call(f32[4096,128]{1,0:T(8,128)} %bitcast.11, s32[256,16,128]{2,1,0:T(8,128)} %bitcast.15, f32[16,16,16]{2,1,0:T(8,128)} %amp_ref.5, s32[16,16]{1,0:T(8,128)} %counts_ref.4, s32[16,16,16]{2,1,0:T(8,128)} %aper_ref.5), custom_call_target="tpu_custom_call" | custom-call | flops 4000000000 | bytes 4000000 | tf_op jit(solution)/shard_map/sample_residual/pallas_call | solution.py:360
  14.4 0.0 copy-done.4
  14.4 0.1 reshape.25.parts_ref
  14.4 0.0 collective-permute-done.1
  14.4 0.0 collective-permute-done
  14.5 0.0 copy-done.1
  14.5 0.0 copy-start.5
  14.6 0.0 copy-start.8
  14.6 1.6 %collective-permute-start.2 = (f32[32,8,128]{2,1,0:T(8,128)S(1)}, f32[32,8,128]{2,1,0:T(8,128)S(1)}, u32[]{:S(2)}, u32[]{:S(2)}) collective-permute-start(f32[32,8,128]{2,1,0:T(8,128)S(1)} %get-tuple-element.20), channel_id=1, source_target_pairs={{0,1},{1,2},{2,3},{4,5},{5,6},{6,7},{8,9},{9,10},{10,11},{12,13},{... | collective-permute-start | bytes 393224 | tf_op jit(solution)/shard_map/ppermute | solution.py:332
  16.2 1.3 %collective-permute-start.3 = (f32[32,8,128]{2,1,0:T(8,128)S(1)}, f32[32,8,128]{2,1,0:T(8,128)S(1)}, u32[]{:S(2)}, u32[]{:S(2)}) collective-permute-start(f32[32,8,128]{2,1,0:T(8,128)S(1)} %get-tuple-element.21), channel_id=1, source_target_pairs={{1,0},{2,1},{3,2},{5,4},{6,5},{7,6},{9,8},{10,9},{11,10},{13,12},{... | collective-permute-start | bytes 393224 | tf_op jit(solution)/shard_map/ppermute | solution.py:332
  17.5 0.0 copy-done
  17.5 0.0 copy-done.6
  17.5 0.0 copy-done.7
  17.5 5.9 %sample_residual.3.s1_more_ref = f32[1024,128]{1,0:T(8,128)S(1)} custom-call(f32[4096,128]{1,0:T(8,128)S(1)} %bitcast.12, s32[256,16,128]{2,1,0:T(8,128)} %bitcast.16, f32[16,16,16]{2,1,0:T(8,128)S(1)} %copy-done.7, s32[16,16]{1,0:T(8,128)S(1)} %copy-done.4, s32[16,16,16]{2,1,0:T(8,128)S(1)} %copy-done.6), custom_call_target="tpu_custom_call" | custom-call | flops 4000000000 | bytes 4000000 | tf_op jit(solution)/shard_map/sample_residual/pallas_call | solution.py:360
  23.4 0.0 copy-start.3
  23.4 0.0 copy-start.2
  23.4 0.0 collective-permute-done.2.left_ref
  23.4 0.0 collective-permute-done.3.right_ref
  23.4 0.0 copy-done.5
  23.4 0.0 copy-done.8
  23.4 32.1 %demigrate_and_sample.1 = (f32[4096,128]{1,0:T(8,128)S(1)}, f32[16,128]{1,0:T(8,128)S(1)}, f32[2,32,8,128]{3,2,1,0:T(8,128)S(1)}, f32[2,32,16,128]{3,2,1,0:T(8,128)S(1)}, f32[2,32,8,128]{3,2,1,0:T(8,128)S(1)}) custom-call(s32[16,16,16]{2,1,0:T(8,128)S(1)} %copy-done.6, s32[256,16,128]{2,1,0:T(8,128)S(1)} %bitcast.17, f32[16,16,16]{2,1,0:T(8,128)S(1)} %copy-done.7, ...), custom_call_target="tpu_custom_call" | custom-call | flops 20000000000 | bytes 8000000 | tf_op jit(solution)/shard_map/demigrate_and_sample/pallas_call | solution.py:399
  55.6 5.2 %collective-permute-start.4 = (f32[2,32,8,128]{3,2,1,0:T(8,128)S(1)}, f32[2,32,8,128]{3,2,1,0:T(8,128)S(1)}, u32[]{:S(2)}, u32[]{:S(2)}) collective-permute-start(f32[2,32,8,128]{3,2,1,0:T(8,128)S(1)} %get-tuple-element.25), channel_id=1, source_target_pairs={{0,1},{1,2},{2,3},{4,5},{5,6},{6,7},{8,9},{9,10},{10,11},{12,13},{... | collective-permute-start | bytes 786440 | tf_op jit(solution)/shard_map/ppermute | solution.py:332
  60.7 1.3 %collective-permute-start.5 = (f32[2,32,8,128]{3,2,1,0:T(8,128)S(1)}, f32[2,32,8,128]{3,2,1,0:T(8,128)S(1)}, u32[]{:S(2)}, u32[]{:S(2)}) collective-permute-start(f32[2,32,8,128]{3,2,1,0:T(8,128)S(1)} %get-tuple-element.26), channel_id=1, source_target_pairs={{1,0},{2,1},{3,2},{5,4},{6,5},{7,6},{9,8},{10,9},{11,10},{13,12},{... | collective-permute-start | bytes 786440 | tf_op jit(solution)/shard_map/ppermute | solution.py:332
  62.0 0.0 collective-permute-done.4.low_ref
  62.0 3.3 %collective-permute-done.5.high_ref = f32[2,32,8,128]{3,2,1,0:T(8,128)S(1)} collective-permute-done((f32[2,32,8,128]{3,2,1,0:T(8,128)S(1)}, f32[2,32,8,128]{3,2,1,0:T(8,128)S(1)}, u32[]{:S(2)}, u32[]{:S(2)}) %collective-permute-start.5) | collective-permute-done | bytes 262176 | tf_op jit(solution)/shard_map/ppermute | solution.py:332
  65.4 0.1 fold_y.1
  65.4 4.3 %collective-permute-start.6 = (f32[2,8,16,128]{3,2,1,0:T(8,128)S(1)}, f32[2,8,16,128]{3,2,1,0:T(8,128)S(1)}, u32[]{:S(2)}, u32[]{:S(2)}) collective-permute-start(f32[2,8,16,128]{3,2,1,0:T(8,128)S(1)} %get-tuple-element.28), channel_id=1, source_target_pairs={{0,4},{4,8},{8,12},{12,16},{16,20},{20,24},{24,28},{1,5},{5,9},{9,... | collective-permute-start | bytes 393224 | tf_op jit(solution)/shard_map/ppermute | solution.py:332
  69.7 1.3 %collective-permute-start.7 = (f32[2,8,16,128]{3,2,1,0:T(8,128)S(1)}, f32[2,8,16,128]{3,2,1,0:T(8,128)S(1)}, u32[]{:S(2)}, u32[]{:S(2)}) collective-permute-start(f32[2,8,16,128]{3,2,1,0:T(8,128)S(1)} %get-tuple-element.29), channel_id=1, source_target_pairs={{4,0},{8,4},{12,8},{16,12},{20,16},{24,20},{28,24},{5,1},{9,5},{13... | collective-permute-start | bytes 393224 | tf_op jit(solution)/shard_map/ppermute | solution.py:332
  71.0 1.2 %collective-permute-done.6.low_ref = f32[2,8,16,128]{3,2,1,0:T(8,128)S(1)} collective-permute-done((f32[2,8,16,128]{3,2,1,0:T(8,128)S(1)}, f32[2,8,16,128]{3,2,1,0:T(8,128)S(1)}, u32[]{:S(2)}, u32[]{:S(2)}) %collective-permute-start.6) | collective-permute-done | bytes 131104 | tf_op jit(solution)/shard_map/ppermute | solution.py:332
  72.2 4.4 %collective-permute-done.7.high_ref = f32[2,8,16,128]{3,2,1,0:T(8,128)S(1)} collective-permute-done((f32[2,8,16,128]{3,2,1,0:T(8,128)S(1)}, f32[2,8,16,128]{3,2,1,0:T(8,128)S(1)}, u32[]{:S(2)}, u32[]{:S(2)}) %collective-permute-start.7) | collective-permute-done | bytes 131104 | tf_op jit(solution)/shard_map/ppermute | solution.py:332
  76.6 0.0 copy-done.3
  76.6 0.2 fold_x.1
  76.8 14.8 %all_to_all.5.stats_ref = f32[32,1,128]{2,1,0:T(1,128)S(1)} all-to-all(f32[32,1,128]{2,1,0:T(1,128)S(1)} %get-tuple-element.31), channel_id=1, replica_groups=mesh['gx'=8,'gy'=4] {'gx','gy'}, dimensions={0} | all-to-all | bytes 32768 | tf_op jit(solution)/shard_map/all_to_all | solution.py:457
  91.6 0.0 copy-done.2
  91.6 2.2 %update.1 = (f32[16,16,128]{2,1,0:T(8,128)}, f32[4096,128]{1,0:T(8,128)}, f32[16,16,128]{2,1,0:T(8,128)}) custom-call(f32[32,1,128]{2,1,0:T(1,128)S(1)} %all_to_all.5.stats_ref, f32[4096,128]{1,0:T(8,128)S(1)} %bitcast.14, f32[4096,128]{1,0:T(8,128)S(1)} %get-tuple-element.32.data_ref, f32[16,16,128]{2,1,0:T(8,128)S(1)} %copy-done.2, ...), custom_call_target="tpu_custom_call" | custom-call | tf_op jit(solution)/shard_map/update/pallas_call | solution.py:465
  (4 shorter events, 0.1 us)
Async XLA Ops:
  0.6 13.8 %collective-permute-start.1 = (f32[16,16,128]{2,1,0:T(8,128)}, f32[16,16,128]{2,1,0:T(8,128)S(1)}, u32[]{:S(2)}, u32[]{:S(2)}) collective-permute-start(f32[16,16,128]{2,1,0:T(8,128)} %dir_ref.1), channel_id=1, source_target_pairs={{4,0},{8,4},{12,8},{16,12},{20,16},{24,20},{28,24},{5,1},{9,5},{13... | collective-permute-start | bytes 393224 | tf_op jit(solution)/shard_map/ppermute | solution.py:332
  1.9 12.5 %collective-permute-start = (f32[16,16,128]{2,1,0:T(8,128)}, f32[16,16,128]{2,1,0:T(8,128)S(1)}, u32[]{:S(2)}, u32[]{:S(2)}) collective-permute-start(f32[16,16,128]{2,1,0:T(8,128)} %dir_ref.1), channel_id=1, source_target_pairs={{0,4},{4,8},{8,12},{12,16},{16,20},{20,24},{24,28},{1,5},{5,9},{9,... | collective-permute-start | bytes 393224 | tf_op jit(solution)/shard_map/ppermute | solution.py:332
  7.4 6.9 %copy-start.4 = (s32[16,16]{1,0:T(8,128)S(1)}, s32[16,16]{1,0:T(8,128)}, u32[]{:S(2)}) copy-start(s32[16,16]{1,0:T(8,128)} %counts_ref.4) | copy-start | bytes 3076
  7.4 7.0 %copy-start.1 = (f32[16,16,128]{2,1,0:T(8,128)S(1)}, f32[16,16,128]{2,1,0:T(8,128)}, u32[]{:S(2)}) copy-start(f32[16,16,128]{2,1,0:T(8,128)} %dir_ref.1) | copy-start | bytes 393220
  7.4 10.0 %copy-start = (f32[16,16,2048]{2,1,0:T(8,128)S(1)}, f32[16,16,2048]{2,1,0:T(8,128)}, u32[]{:S(2)}) copy-start(f32[16,16,2048]{2,1,0:T(8,128)} %param.9) | copy-start | bytes 6291460
  7.4 10.0 %copy-start.6 = (s32[16,16,16]{2,1,0:T(8,128)S(1)}, s32[16,16,16]{2,1,0:T(8,128)}, u32[]{:S(2)}) copy-start(s32[16,16,16]{2,1,0:T(8,128)} %aper_ref.5) | copy-start | bytes 49156
  7.5 10.0 %copy-start.7 = (f32[16,16,16]{2,1,0:T(8,128)S(1)}, f32[16,16,16]{2,1,0:T(8,128)}, u32[]{:S(2)}) copy-start(f32[16,16,16]{2,1,0:T(8,128)} %amp_ref.5) | copy-start | bytes 49156
  14.5 8.9 %copy-start.5 = (s32[16,16,16,128]{3,2,1,0:T(8,128)S(1)}, s32[16,16,16,128]{3,2,1,0:T(8,128)}, u32[]{:S(2)}) copy-start(s32[16,16,16,128]{3,2,1,0:T(8,128)} %param.13) | copy-start | bytes 6291460
  14.6 8.9 %copy-start.8 = (f32[1024,128]{1,0:T(8,128)S(1)}, f32[1024,128]{1,0:T(8,128)}, u32[]{:S(2)}) copy-start(f32[1024,128]{1,0:T(8,128)} %sample_residual.2.s1_in_ref) | copy-start | bytes 1572868
  14.6 8.8 %collective-permute-start.2 = (f32[32,8,128]{2,1,0:T(8,128)S(1)}, f32[32,8,128]{2,1,0:T(8,128)S(1)}, u32[]{:S(2)}, u32[]{:S(2)}) collective-permute-start(f32[32,8,128]{2,1,0:T(8,128)S(1)} %get-tuple-element.20), channel_id=1, source_target_pairs={{0,1},{1,2},{2,3},{4,5},{5,6},{6,7},{8,9},{9,10},{10,11},{12,13},{... | collective-permute-start | bytes 393224 | tf_op jit(solution)/shard_map/ppermute | solution.py:332
  16.2 7.3 %collective-permute-start.3 = (f32[32,8,128]{2,1,0:T(8,128)S(1)}, f32[32,8,128]{2,1,0:T(8,128)S(1)}, u32[]{:S(2)}, u32[]{:S(2)}) collective-permute-start(f32[32,8,128]{2,1,0:T(8,128)S(1)} %get-tuple-element.21), channel_id=1, source_target_pairs={{1,0},{2,1},{3,2},{5,4},{6,5},{7,6},{9,8},{10,9},{11,10},{13,12},{... | collective-permute-start | bytes 393224 | tf_op jit(solution)/shard_map/ppermute | solution.py:332
  23.4 53.2 %copy-start.3 = (f32[16,16,128]{2,1,0:T(8,128)S(1)}, f32[16,16,128]{2,1,0:T(8,128)}, u32[]{:S(2)}) copy-start(f32[16,16,128]{2,1,0:T(8,128)} %grad_ref.1) | copy-start | bytes 393220
  23.4 68.2 %copy-start.2 = (f32[16,16,128]{2,1,0:T(8,128)S(1)}, f32[16,16,128]{2,1,0:T(8,128)}, u32[]{:S(2)}) copy-start(f32[16,16,128]{2,1,0:T(8,128)} %model_ref.1) | copy-start | bytes 393220
  55.6 6.5 %collective-permute-start.4 = (f32[2,32,8,128]{3,2,1,0:T(8,128)S(1)}, f32[2,32,8,128]{3,2,1,0:T(8,128)S(1)}, u32[]{:S(2)}, u32[]{:S(2)}) collective-permute-start(f32[2,32,8,128]{3,2,1,0:T(8,128)S(1)} %get-tuple-element.25), channel_id=1, source_target_pairs={{0,1},{1,2},{2,3},{4,5},{5,6},{6,7},{8,9},{9,10},{10,11},{12,13},{... | collective-permute-start | bytes 786440 | tf_op jit(solution)/shard_map/ppermute | solution.py:332
  60.7 4.7 %collective-permute-start.5 = (f32[2,32,8,128]{3,2,1,0:T(8,128)S(1)}, f32[2,32,8,128]{3,2,1,0:T(8,128)S(1)}, u32[]{:S(2)}, u32[]{:S(2)}) collective-permute-start(f32[2,32,8,128]{3,2,1,0:T(8,128)S(1)} %get-tuple-element.26), channel_id=1, source_target_pairs={{1,0},{2,1},{3,2},{5,4},{6,5},{7,6},{9,8},{10,9},{11,10},{13,12},{... | collective-permute-start | bytes 786440 | tf_op jit(solution)/shard_map/ppermute | solution.py:332
  65.4 6.8 %collective-permute-start.6 = (f32[2,8,16,128]{3,2,1,0:T(8,128)S(1)}, f32[2,8,16,128]{3,2,1,0:T(8,128)S(1)}, u32[]{:S(2)}, u32[]{:S(2)}) collective-permute-start(f32[2,8,16,128]{3,2,1,0:T(8,128)S(1)} %get-tuple-element.28), channel_id=1, source_target_pairs={{0,4},{4,8},{8,12},{12,16},{16,20},{20,24},{24,28},{1,5},{5,9},{9,... | collective-permute-start | bytes 393224 | tf_op jit(solution)/shard_map/ppermute | solution.py:332
  69.7 6.9 %collective-permute-start.7 = (f32[2,8,16,128]{3,2,1,0:T(8,128)S(1)}, f32[2,8,16,128]{3,2,1,0:T(8,128)S(1)}, u32[]{:S(2)}, u32[]{:S(2)}) collective-permute-start(f32[2,8,16,128]{3,2,1,0:T(8,128)S(1)} %get-tuple-element.29), channel_id=1, source_target_pairs={{4,0},{8,4},{12,8},{16,12},{20,16},{24,20},{28,24},{5,1},{9,5},{13... | collective-permute-start | bytes 393224 | tf_op jit(solution)/shard_map/ppermute | solution.py:332

commit v7 on v6

--- a/solution.py
+++ b/solution.py
@@ -106,7 +106,7 @@
     spread_bins(both, place_row(aper_ref[0], wide_y), s_ref, step + row0, wide_y)
 
 
-def scatter_bin(geo, row, b, image, entry_ref, times_ref, scales, work):
+def scatter_bin(geo, row, b, image, entry_ref, times_ref, scales, work, late=None):
     bins_y, entries, highs, wide_y = geo
     half = LANES // 2
     half_bits = half.bit_length() - 1
@@ -144,13 +144,30 @@
         rights.append(
             jnp.concatenate([jnp.where(low == iota, one, zero) for iota in iota_lo], axis=0)
         )
+    right = jnp.concatenate(rights, axis=1)
     out = lax.dot_general(
         jnp.concatenate(lefts, axis=1),
-        jnp.concatenate(rights, axis=1),
+        right,
         (((1,), (1,)), ((), ())),
         preferred_element_type=F32,
     )
     out = out[: 2 * highs] + out[2 * highs :]
+    if late is not None:
+        upper = out.astype(BF16)
+        lower = (out - upper.astype(F32)).astype(BF16)
+        halves = jnp.concatenate([upper, lower], axis=0)
+        iota8 = lax.broadcasted_iota(jnp.int32, (SUB, LANES), 0)
+        for e in range(0, entries, 2):
+            tables = jnp.concatenate(rights[e : e + 2], axis=1)
+            picked = jnp.dot(halves, tables, preferred_element_type=F32)
+            picked = picked[: 2 * highs] + picked[2 * highs :]
+            for u in range(2):
+                place = work[3, pl.ds(e + u, SUB, stride=0), :]
+                kept = jnp.zeros((SUB, LANES), F32)
+                for k in range(0, 2 * highs, SUB):
+                    part = picked[k : k + SUB, u * LANES : (u + 1) * LANES]
+                    kept = kept + jnp.where(place == (iota8 + k).astype(F32), part, 0.0)
+                late[pl.ds(b * entries + e + u, 1), :] = jnp.sum(kept, axis=0, keepdims=True)
     return jnp.concatenate([out[:highs], out[highs:]], axis=1)
 
 
@@ -185,6 +202,7 @@
     old_data,
     both,
     res_both,
+    late,
     *works,
 ):
     bins_y, entries, highs, wide_y = geo
@@ -199,6 +217,7 @@
     old_data[...] = jnp.zeros_like(old_data)
     scales[...] = jnp.zeros_like(scales)
     both[...] = jnp.zeros_like(both)
+    late[...] = jnp.zeros_like(late)
     res_both[...] = jnp.zeros_like(res_both)
     for x in range(wide_x):
         image[pl.ds(x * wide_y, RADIUS), :] = left_ref[x]
@@ -215,6 +234,15 @@
         row, part = residual_part(step)
         entry = aper_ref[row, pl.ds(pl.multiple_of(part, SUB), res_bins), :]
         spread_bins(res_both[...], place_row(entry, wide_y, part), s1_ref, row, wide_y)
+
+    def by_tables(b):
+        return b % cut == cut - 1
+
+    def take_late(weights):
+        for b in range(bins_y):
+            if by_tables(b):
+                at = pl.ds(b * entries, entries)
+                vals[at, :] = late[at, :] * weights[at, :]
 
     def one_row(step, total):
         before = jnp.maximum(step - 1, 0)
@@ -223,6 +251,7 @@
         res_row, res_part = residual_part(step)
         res_first = pl.multiple_of(res_row * rows_per + res_part * highs, SUB)
         old_scales[...] = scales[...]
+        take_late(old_scales)
         fill_weights(amp_ref[step], counts_ref[pl.ds(step, 1), :], scales)
         fill_weights(
             amp_ref[res_row, pl.ds(pl.multiple_of(res_part, SUB), res_bins), :],
@@ -231,15 +260,23 @@
         )
         for b in range(bins_y):
             trace = scatter_bin(
-                geo, step, b, image, entry_ref, times_ref, scales, works[b % len(works)]
+                geo,
+                step,
+                b,
+                image,
+                entry_ref,
+                times_ref,
+                scales,
+                works[b % len(works)],
+                late if by_tables(b) else None,
             )
             first = trace_row(b, highs)
             data_ref[pl.ds(step * rows_per + first, highs, stride=SUB), :] = trace
             total = total + trace * trace
-            sample_bin(
-                old_data, first, highs, times_ref, before * bins_y + b, b, old_scales, vals
-            )
-            if b % cut == 0:
+            if not by_tables(b):
+                at = before * bins_y + b
+                sample_bin(old_data, first, highs, times_ref, at, b, old_scales, vals)
+            else:
                 r = b // cut
                 first = res_first + trace_row(r, highs)
                 at = res_row * bins_y + res_part + r
@@ -253,9 +290,11 @@
     last = bins_x - 1
     spread_image(last - 1)
     spread_residual(last)
+    take_late(scales)
     for b in range(bins_y):
         at = last * bins_y + b
-        sample_bin(old_data, trace_row(b, highs), highs, times_ref, at, b, scales, vals)
+        if not by_tables(b):
+            sample_bin(old_data, trace_row(b, highs), highs, times_ref, at, b, scales, vals)
     both[...] = split_values(vals)
     spread_image(last)
     for k, ref in enumerate((s1_ref, s2_ref)):
@@ -412,6 +451,7 @@
         + [pltpu.VMEM((rows_per, LANES), F32)]
         + [pltpu.VMEM((bins_y * entries, 2 * depths), BF16)]
         + [pltpu.VMEM((res_bins * entries, 2 * depths), BF16)]
+        + [vals_shape]
         + [pltpu.VMEM((4, entries + SUB, LANES), F32)] * 8,
         compiler_params=params(MAIN_LIMIT),
         cost_estimate=pl.CostEstimate(

time: 94.2 us -> 118 us (1.25)
  Pallas kernels: 47.4 us -> 71.6 us
    pallas_call x1, Pallas kernels: 32.1 us -> 56.3 us  [body(): pl.pallas_call(functools.partial(main_kernel, geo, row0), in_specs=[pl.Bl...]
  transfers between devices with their start and end apart: 8 -> 8, of which waited for: 3 -> 3; matrix products, arithmetic and copies ran while one was open for 0% -> 0% of each run, Pallas kernels for 14% -> 11%
where the time goes in v7:
time: 118 us
  Pallas kernels  71.6 us (61%)
  starting transfers between devices  21.8 us (18%)
  blocking collectives  14.7 us (12%)
  waiting for transfers between devices  8.85 us (8%)
    pallas_call x1, Pallas kernels, body(): pl.pallas_call(functools.partial(main_kernel, geo, row0), in_specs=[pl.Bl...  56.3 us
    ppermute x8, starting transfers between devices, shift(): return lax.ppermute(cells, axis, pairs)  21.8 us
    all_to_all x1, blocking collectives, body(): stats = lax.all_to_all(stats, ('gx', 'gy'), 0, 0, tiled=True)  14.7 us
    pallas_call x2, Pallas kernels, first(): pl.pallas_call(functools.partial(first_kernel, geo, row0), grid=(count,),...  12.8 us
    ppermute x8, waiting for transfers between devices, shift(): return lax.ppermute(cells, axis, pairs)  8.85 us
  transfers between devices with their start and end apart: 8, of which 3 were waited for; matrix products, arithmetic and copies ran while one was open for 0% of the time, Pallas kernels for 11%

profile of v7, /device:TPU:0, one launch (start us, length us, event | category | flops | bytes accessed | tf_op | source)
XLA Modules:
  0.0 118.0 jit_solution(12021181806298987800)
XLA Ops:
  0.6 1.3 %collective-permute-start.1 = (f32[16,16,128]{2,1,0:T(8,128)}, f32[16,16,128]{2,1,0:T(8,128)S(1)}, u32[]{:S(2)}, u32[]{:S(2)}) collective-permute-start(f32[16,16,128]{2,1,0:T(8,128)} %dir_ref.1), channel_id=1, source_target_pairs={{4,0},{8,4},{12,8},{16,12},{20,16},{24,20},{28,24},{5,1},{9,5},{13... | collective-permute-start | bytes 393224 | tf_op jit(solution)/shard_map/ppermute | solution.py:371
  1.9 5.5 %collective-permute-start = (f32[16,16,128]{2,1,0:T(8,128)}, f32[16,16,128]{2,1,0:T(8,128)S(1)}, u32[]{:S(2)}, u32[]{:S(2)}) collective-permute-start(f32[16,16,128]{2,1,0:T(8,128)} %dir_ref.1), channel_id=1, source_target_pairs={{0,4},{4,8},{8,12},{12,16},{16,20},{20,24},{24,28},{1,5},{5,9},{9,... | collective-permute-start | bytes 393224 | tf_op jit(solution)/shard_map/ppermute | solution.py:371
  7.4 0.0 copy-start.4
  7.4 0.0 copy-start.1
  7.4 0.0 copy-start
  7.4 0.0 copy-start.6
  7.5 0.0 copy-start.7
  7.5 6.9 %sample_residual.2.s1_in_ref = f32[1024,128]{1,0:T(8,128)} custom-call(f32[4096,128]{1,0:T(8,128)} %bitcast.11, s32[256,16,128]{2,1,0:T(8,128)} %bitcast.15, f32[16,16,16]{2,1,0:T(8,128)} %amp_ref.5, s32[16,16]{1,0:T(8,128)} %counts_ref.4, s32[16,16,16]{2,1,0:T(8,128)} %aper_ref.5), custom_call_target="tpu_custom_call" | custom-call | flops 4000000000 | bytes 4000000 | tf_op jit(solution)/shard_map/sample_residual/pallas_call | solution.py:399
  14.4 0.0 copy-done.4
  14.4 0.1 reshape.25.parts_ref
  14.4 0.0 collective-permute-done.1
  14.4 0.0 collective-permute-done
  14.5 0.0 copy-done.1
  14.5 0.0 copy-start.5
  14.6 0.0 copy-start.8
  14.6 1.6 %collective-permute-start.2 = (f32[32,8,128]{2,1,0:T(8,128)S(1)}, f32[32,8,128]{2,1,0:T(8,128)S(1)}, u32[]{:S(2)}, u32[]{:S(2)}) collective-permute-start(f32[32,8,128]{2,1,0:T(8,128)S(1)} %get-tuple-element.20), channel_id=1, source_target_pairs={{0,1},{1,2},{2,3},{4,5},{5,6},{6,7},{8,9},{9,10},{10,11},{12,13},{... | collective-permute-start | bytes 393224 | tf_op jit(solution)/shard_map/ppermute | solution.py:371
  16.2 1.3 %collective-permute-start.3 = (f32[32,8,128]{2,1,0:T(8,128)S(1)}, f32[32,8,128]{2,1,0:T(8,128)S(1)}, u32[]{:S(2)}, u32[]{:S(2)}) collective-permute-start(f32[32,8,128]{2,1,0:T(8,128)S(1)} %get-tuple-element.21), channel_id=1, source_target_pairs={{1,0},{2,1},{3,2},{5,4},{6,5},{7,6},{9,8},{10,9},{11,10},{13,12},{... | collective-permute-start | bytes 393224 | tf_op jit(solution)/shard_map/ppermute | solution.py:371
  17.5 0.0 copy-done
  17.5 0.0 copy-done.6
  17.5 0.0 copy-done.7
  17.5 5.9 %sample_residual.3.s1_more_ref = f32[1024,128]{1,0:T(8,128)S(1)} custom-call(f32[4096,128]{1,0:T(8,128)S(1)} %bitcast.12, s32[256,16,128]{2,1,0:T(8,128)} %bitcast.16, f32[16,16,16]{2,1,0:T(8,128)S(1)} %copy-done.7, s32[16,16]{1,0:T(8,128)S(1)} %copy-done.4, s32[16,16,16]{2,1,0:T(8,128)S(1)} %copy-done.6), custom_call_target="tpu_custom_call" | custom-call | flops 4000000000 | bytes 4000000 | tf_op jit(solution)/shard_map/sample_residual/pallas_call | solution.py:399
  23.4 0.0 copy-start.3
  23.4 0.0 copy-start.2
  23.4 0.0 collective-permute-done.2.left_ref
  23.4 0.0 collective-permute-done.3.right_ref
  23.4 0.0 copy-done.5
  23.4 0.0 copy-done.8
  23.4 56.3 %demigrate_and_sample.1 = (f32[4096,128]{1,0:T(8,128)S(1)}, f32[16,128]{1,0:T(8,128)S(1)}, f32[2,32,8,128]{3,2,1,0:T(8,128)S(1)}, f32[2,32,16,128]{3,2,1,0:T(8,128)S(1)}, f32[2,32,8,128]{3,2,1,0:T(8,128)S(1)}) custom-call(s32[16,16,16]{2,1,0:T(8,128)S(1)} %copy-done.6, s32[256,16,128]{2,1,0:T(8,128)S(1)} %bitcast.17, f32[16,16,16]{2,1,0:T(8,128)S(1)} %copy-done.7, ...), custom_call_target="tpu_custom_call" | custom-call | flops 20000000000 | bytes 8000000 | tf_op jit(solution)/shard_map/demigrate_and_sample/pallas_call | solution.py:438
  79.8 5.2 %collective-permute-start.4 = (f32[2,32,8,128]{3,2,1,0:T(8,128)S(1)}, f32[2,32,8,128]{3,2,1,0:T(8,128)S(1)}, u32[]{:S(2)}, u32[]{:S(2)}) collective-permute-start(f32[2,32,8,128]{3,2,1,0:T(8,128)S(1)} %get-tuple-element.25), channel_id=1, source_target_pairs={{0,1},{1,2},{2,3},{4,5},{5,6},{6,7},{8,9},{9,10},{10,11},{12,13},{... | collective-permute-start | bytes 786440 | tf_op jit(solution)/shard_map/ppermute | solution.py:371
  84.9 1.3 %collective-permute-start.5 = (f32[2,32,8,128]{3,2,1,0:T(8,128)S(1)}, f32[2,32,8,128]{3,2,1,0:T(8,128)S(1)}, u32[]{:S(2)}, u32[]{:S(2)}) collective-permute-start(f32[2,32,8,128]{3,2,1,0:T(8,128)S(1)} %get-tuple-element.26), channel_id=1, source_target_pairs={{1,0},{2,1},{3,2},{5,4},{6,5},{7,6},{9,8},{10,9},{11,10},{13,12},{... | collective-permute-start | bytes 786440 | tf_op jit(solution)/shard_map/ppermute | solution.py:371
  86.2 0.0 collective-permute-done.4.low_ref
  86.2 3.3 %collective-permute-done.5.high_ref = f32[2,32,8,128]{3,2,1,0:T(8,128)S(1)} collective-permute-done((f32[2,32,8,128]{3,2,1,0:T(8,128)S(1)}, f32[2,32,8,128]{3,2,1,0:T(8,128)S(1)}, u32[]{:S(2)}, u32[]{:S(2)}) %collective-permute-start.5) | collective-permute-done | bytes 262176 | tf_op jit(solution)/shard_map/ppermute | solution.py:371
  89.5 0.1 fold_y.1
  89.6 4.4 %collective-permute-start.6 = (f32[2,8,16,128]{3,2,1,0:T(8,128)S(1)}, f32[2,8,16,128]{3,2,1,0:T(8,128)S(1)}, u32[]{:S(2)}, u32[]{:S(2)}) collective-permute-start(f32[2,8,16,128]{3,2,1,0:T(8,128)S(1)} %get-tuple-element.28), channel_id=1, source_target_pairs={{0,4},{4,8},{8,12},{12,16},{16,20},{20,24},{24,28},{1,5},{5,9},{9,... | collective-permute-start | bytes 393224 | tf_op jit(solution)/shard_map/ppermute | solution.py:371
  93.9 1.3 %collective-permute-start.7 = (f32[2,8,16,128]{3,2,1,0:T(8,128)S(1)}, f32[2,8,16,128]{3,2,1,0:T(8,128)S(1)}, u32[]{:S(2)}, u32[]{:S(2)}) collective-permute-start(f32[2,8,16,128]{3,2,1,0:T(8,128)S(1)} %get-tuple-element.29), channel_id=1, source_target_pairs={{4,0},{8,4},{12,8},{16,12},{20,16},{24,20},{28,24},{5,1},{9,5},{13... | collective-permute-start | bytes 393224 | tf_op jit(solution)/shard_map/ppermute | solution.py:371
  95.2 1.2 %collective-permute-done.6.low_ref = f32[2,8,16,128]{3,2,1,0:T(8,128)S(1)} collective-permute-done((f32[2,8,16,128]{3,2,1,0:T(8,128)S(1)}, f32[2,8,16,128]{3,2,1,0:T(8,128)S(1)}, u32[]{:S(2)}, u32[]{:S(2)}) %collective-permute-start.6) | collective-permute-done | bytes 131104 | tf_op jit(solution)/shard_map/ppermute | solution.py:371
  96.4 4.4 %collective-permute-done.7.high_ref = f32[2,8,16,128]{3,2,1,0:T(8,128)S(1)} collective-permute-done((f32[2,8,16,128]{3,2,1,0:T(8,128)S(1)}, f32[2,8,16,128]{3,2,1,0:T(8,128)S(1)}, u32[]{:S(2)}, u32[]{:S(2)}) %collective-permute-start.7) | collective-permute-done | bytes 131104 | tf_op jit(solution)/shard_map/ppermute | solution.py:371
  100.8 0.0 copy-done.3
  100.8 0.2 fold_x.1
  101.0 14.7 %all_to_all.5.stats_ref = f32[32,1,128]{2,1,0:T(1,128)S(1)} all-to-all(f32[32,1,128]{2,1,0:T(1,128)S(1)} %get-tuple-element.31), channel_id=1, replica_groups=mesh['gx'=8,'gy'=4] {'gx','gy'}, dimensions={0} | all-to-all | bytes 32768 | tf_op jit(solution)/shard_map/all_to_all | solution.py:497
  115.7 0.0 copy-done.2
  115.7 2.2 %update.1 = (f32[16,16,128]{2,1,0:T(8,128)}, f32[4096,128]{1,0:T(8,128)}, f32[16,16,128]{2,1,0:T(8,128)}) custom-call(f32[32,1,128]{2,1,0:T(1,128)S(1)} %all_to_all.5.stats_ref, f32[4096,128]{1,0:T(8,128)S(1)} %bitcast.14, f32[4096,128]{1,0:T(8,128)S(1)} %get-tuple-element.32.data_ref, f32[16,16,128]{2,1,0:T(8,128)S(1)} %copy-done.2, ...), custom_call_target="tpu_custom_call" | custom-call | tf_op jit(solution)/shard_map/update/pallas_call | solution.py:505
  (4 shorter events, 0.1 us)
Async XLA Ops:
  0.6 13.8 %collective-permute-start.1 = (f32[16,16,128]{2,1,0:T(8,128)}, f32[16,16,128]{2,1,0:T(8,128)S(1)}, u32[]{:S(2)}, u32[]{:S(2)}) collective-permute-start(f32[16,16,128]{2,1,0:T(8,128)} %dir_ref.1), channel_id=1, source_target_pairs={{4,0},{8,4},{12,8},{16,12},{20,16},{24,20},{28,24},{5,1},{9,5},{13... | collective-permute-start | bytes 393224 | tf_op jit(solution)/shard_map/ppermute | solution.py:371
  1.9 12.5 %collective-permute-start = (f32[16,16,128]{2,1,0:T(8,128)}, f32[16,16,128]{2,1,0:T(8,128)S(1)}, u32[]{:S(2)}, u32[]{:S(2)}) collective-permute-start(f32[16,16,128]{2,1,0:T(8,128)} %dir_ref.1), channel_id=1, source_target_pairs={{0,4},{4,8},{8,12},{12,16},{16,20},{20,24},{24,28},{1,5},{5,9},{9,... | collective-permute-start | bytes 393224 | tf_op jit(solution)/shard_map/ppermute | solution.py:371
  7.4 6.9 %copy-start.4 = (s32[16,16]{1,0:T(8,128)S(1)}, s32[16,16]{1,0:T(8,128)}, u32[]{:S(2)}) copy-start(s32[16,16]{1,0:T(8,128)} %counts_ref.4) | copy-start | bytes 3076
  7.4 7.0 %copy-start.1 = (f32[16,16,128]{2,1,0:T(8,128)S(1)}, f32[16,16,128]{2,1,0:T(8,128)}, u32[]{:S(2)}) copy-start(f32[16,16,128]{2,1,0:T(8,128)} %dir_ref.1) | copy-start | bytes 393220
  7.4 10.0 %copy-start = (f32[16,16,2048]{2,1,0:T(8,128)S(1)}, f32[16,16,2048]{2,1,0:T(8,128)}, u32[]{:S(2)}) copy-start(f32[16,16,2048]{2,1,0:T(8,128)} %param.9) | copy-start | bytes 6291460
  7.4 10.0 %copy-start.6 = (s32[16,16,16]{2,1,0:T(8,128)S(1)}, s32[16,16,16]{2,1,0:T(8,128)}, u32[]{:S(2)}) copy-start(s32[16,16,16]{2,1,0:T(8,128)} %aper_ref.5) | copy-start | bytes 49156
  7.5 10.0 %copy-start.7 = (f32[16,16,16]{2,1,0:T(8,128)S(1)}, f32[16,16,16]{2,1,0:T(8,128)}, u32[]{:S(2)}) copy-start(f32[16,16,16]{2,1,0:T(8,128)} %amp_ref.5) | copy-start | bytes 49156
  14.5 8.9 %copy-start.5 = (s32[16,16,16,128]{3,2,1,0:T(8,128)S(1)}, s32[16,16,16,128]{3,2,1,0:T(8,128)}, u32[]{:S(2)}) copy-start(s32[16,16,16,128]{3,2,1,0:T(8,128)} %param.13) | copy-start | bytes 6291460
  14.6 8.9 %copy-start.8 = (f32[1024,128]{1,0:T(8,128)S(1)}, f32[1024,128]{1,0:T(8,128)}, u32[]{:S(2)}) copy-start(f32[1024,128]{1,0:T(8,128)} %sample_residual.2.s1_in_ref) | copy-start | bytes 1572868
  14.6 8.8 %collective-permute-start.2 = (f32[32,8,128]{2,1,0:T(8,128)S(1)}, f32[32,8,128]{2,1,0:T(8,128)S(1)}, u32[]{:S(2)}, u32[]{:S(2)}) collective-permute-start(f32[32,8,128]{2,1,0:T(8,128)S(1)} %get-tuple-element.20), channel_id=1, source_target_pairs={{0,1},{1,2},{2,3},{4,5},{5,6},{6,7},{8,9},{9,10},{10,11},{12,13},{... | collective-permute-start | bytes 393224 | tf_op jit(solution)/shard_map/ppermute | solution.py:371
  16.2 7.3 %collective-permute-start.3 = (f32[32,8,128]{2,1,0:T(8,128)S(1)}, f32[32,8,128]{2,1,0:T(8,128)S(1)}, u32[]{:S(2)}, u32[]{:S(2)}) collective-permute-start(f32[32,8,128]{2,1,0:T(8,128)S(1)} %get-tuple-element.21), channel_id=1, source_target_pairs={{1,0},{2,1},{3,2},{5,4},{6,5},{7,6},{9,8},{10,9},{11,10},{13,12},{... | collective-permute-start | bytes 393224 | tf_op jit(solution)/shard_map/ppermute | solution.py:371
  23.4 77.4 %copy-start.3 = (f32[16,16,128]{2,1,0:T(8,128)S(1)}, f32[16,16,128]{2,1,0:T(8,128)}, u32[]{:S(2)}) copy-start(f32[16,16,128]{2,1,0:T(8,128)} %grad_ref.1) | copy-start | bytes 393220
  23.4 92.3 %copy-start.2 = (f32[16,16,128]{2,1,0:T(8,128)S(1)}, f32[16,16,128]{2,1,0:T(8,128)}, u32[]{:S(2)}) copy-start(f32[16,16,128]{2,1,0:T(8,128)} %model_ref.1) | copy-start | bytes 393220
  79.8 6.5 %collective-permute-start.4 = (f32[2,32,8,128]{3,2,1,0:T(8,128)S(1)}, f32[2,32,8,128]{3,2,1,0:T(8,128)S(1)}, u32[]{:S(2)}, u32[]{:S(2)}) collective-permute-start(f32[2,32,8,128]{3,2,1,0:T(8,128)S(1)} %get-tuple-element.25), channel_id=1, source_target_pairs={{0,1},{1,2},{2,3},{4,5},{5,6},{6,7},{8,9},{9,10},{10,11},{12,13},{... | collective-permute-start | bytes 786440 | tf_op jit(solution)/shard_map/ppermute | solution.py:371
  84.9 4.6 %collective-permute-start.5 = (f32[2,32,8,128]{3,2,1,0:T(8,128)S(1)}, f32[2,32,8,128]{3,2,1,0:T(8,128)S(1)}, u32[]{:S(2)}, u32[]{:S(2)}) collective-permute-start(f32[2,32,8,128]{3,2,1,0:T(8,128)S(1)} %get-tuple-element.26), channel_id=1, source_target_pairs={{1,0},{2,1},{3,2},{5,4},{6,5},{7,6},{9,8},{10,9},{11,10},{13,12},{... | collective-permute-start | bytes 786440 | tf_op jit(solution)/shard_map/ppermute | solution.py:371
  89.6 6.9 %collective-permute-start.6 = (f32[2,8,16,128]{3,2,1,0:T(8,128)S(1)}, f32[2,8,16,128]{3,2,1,0:T(8,128)S(1)}, u32[]{:S(2)}, u32[]{:S(2)}) collective-permute-start(f32[2,8,16,128]{3,2,1,0:T(8,128)S(1)} %get-tuple-element.28), channel_id=1, source_target_pairs={{0,4},{4,8},{8,12},{12,16},{16,20},{20,24},{24,28},{1,5},{5,9},{9,... | collective-permute-start | bytes 393224 | tf_op jit(solution)/shard_map/ppermute | solution.py:371
  93.9 6.9 %collective-permute-start.7 = (f32[2,8,16,128]{3,2,1,0:T(8,128)S(1)}, f32[2,8,16,128]{3,2,1,0:T(8,128)S(1)}, u32[]{:S(2)}, u32[]{:S(2)}) collective-permute-start(f32[2,8,16,128]{3,2,1,0:T(8,128)S(1)} %get-tuple-element.29), channel_id=1, source_target_pairs={{4,0},{8,4},{12,8},{16,12},{20,16},{24,20},{28,24},{5,1},{9,5},{13... | collective-permute-start | bytes 393224 | tf_op jit(solution)/shard_map/ppermute | solution.py:371

commit v8 on v6

--- a/solution.py
+++ b/solution.py
@@ -444,17 +444,19 @@
     )(out_mid, from_low, from_high)
     from_low = shift(out_tail, "gx", 1)
     from_high = shift(out_head, "gx", -1)
-    devices = lax.axis_size("gx") * lax.axis_size("gy")
+    devices_x, devices_y = lax.axis_size("gx"), lax.axis_size("gy")
     grads, stats = pl.pallas_call(
         fold_x_kernel,
         out_shape=[
             jax.ShapeDtypeStruct((2, bins_x, bins_y, depths), F32),
-            jax.ShapeDtypeStruct((devices, 1, LANES), F32),
+            jax.ShapeDtypeStruct((devices_y, 1, LANES), F32),
         ],
         compiler_params=params(SMALL_LIMIT),
         name="fold_x",
     )(inner, from_low, from_high, old_gradient, curv)
-    stats = lax.all_to_all(stats, ("gx", "gy"), 0, 0, tiled=True)
+    stats = lax.all_to_all(stats, "gy", 0, 0, tiled=True)
+    stats = jnp.broadcast_to(jnp.sum(stats, axis=0, keepdims=True), (devices_x, 1, LANES))
+    stats = lax.all_to_all(stats, "gx", 0, 0, tiled=True)
 
     steps = 4
     rows_step = bins_x * rows_per // steps

time: 94.2 us -> 103 us (1.093)
  blocking collectives: 14.8 us -> 20.4 us
  local copies, waits for them, and re-layouts: 0.15 us -> 3.06 us
    all_to_all x1 -> x2, blocking collectives: 14.8 us -> 20.4 us  [the longest x1 11.1 us: body(): stats = lax.all_to_all(stats, 'gx', 0, 0, tiled=True)]
    unnamed x18 -> x22, local copies, waits for them, and re-layouts: 0.05 us -> 2.95 us
  transfers between devices with their start and end apart: 8 -> 8, of which waited for: 3 -> 3; matrix products, arithmetic and copies ran while one was open for 0% -> 0% of each run, Pallas kernels for 14% -> 12%
where the time goes in v8:
time: 103 us; the launch traced here: 102 us
  Pallas kernels  47.3 us (46%)
  starting transfers between devices  21.6 us (21%)
  blocking collectives  20.4 us (20%)
  waiting for transfers between devices  8.93 us (9%)
  local copies, waits for them, and re-layouts  3.06 us (3%)
    pallas_call x1, Pallas kernels, body(): pl.pallas_call(functools.partial(main_kernel, geo, row0), in_specs=[pl.Bl...  32.1 us
    ppermute x8, starting transfers between devices, shift(): return lax.ppermute(cells, axis, pairs)  21.6 us
    pallas_call x2, Pallas kernels, first(): pl.pallas_call(functools.partial(first_kernel, geo, row0), grid=(count,),...  12.8 us
    all_to_all x1, blocking collectives, body(): stats = lax.all_to_all(stats, 'gx', 0, 0, tiled=True)  11.1 us
    all_to_all x1, blocking collectives, body(): stats = lax.all_to_all(stats, 'gy', 0, 0, tiled=True)  9.29 us
    ppermute x8, waiting for transfers between devices, shift(): return lax.ppermute(cells, axis, pairs)  8.93 us
    unnamed x22, local copies, waits for them, and re-layouts  2.95 us
    pallas_call x1, Pallas kernels, body(): pl.pallas_call(last_kernel, grid=(steps,), in_specs=[pl.BlockSpec(stats.s...  2.14 us
  transfers between devices with their start and end apart: 8, of which 3 were waited for; matrix products, arithmetic and copies ran while one was open for 0% of the time, Pallas kernels for 12%

profile of v8, /device:TPU:0, one launch (start us, length us, event | category | flops | bytes accessed | tf_op | source)
XLA Modules:
  0.0 102.3 jit_solution(4734894142865504062)
XLA Ops:
  0.6 1.3 %collective-permute-start.1 = (f32[16,16,128]{2,1,0:T(8,128)}, f32[16,16,128]{2,1,0:T(8,128)S(1)}, u32[]{:S(2)}, u32[]{:S(2)}) collective-permute-start(f32[16,16,128]{2,1,0:T(8,128)} %dir_ref.1), channel_id=1, source_target_pairs={{4,0},{8,4},{12,8},{16,12},{20,16},{24,20},{28,24},{5,1},{9,5},{13... | collective-permute-start | bytes 393224 | tf_op jit(solution)/shard_map/ppermute | solution.py:332
  1.9 5.5 %collective-permute-start = (f32[16,16,128]{2,1,0:T(8,128)}, f32[16,16,128]{2,1,0:T(8,128)S(1)}, u32[]{:S(2)}, u32[]{:S(2)}) collective-permute-start(f32[16,16,128]{2,1,0:T(8,128)} %dir_ref.1), channel_id=1, source_target_pairs={{0,4},{4,8},{8,12},{12,16},{16,20},{20,24},{24,28},{1,5},{5,9},{9,... | collective-permute-start | bytes 393224 | tf_op jit(solution)/shard_map/ppermute | solution.py:332
  7.4 0.0 copy-start.6
  7.4 0.0 copy-start.3
  7.4 0.0 copy-start
  7.4 0.0 copy-start.8
  7.5 0.0 copy-start.9
  7.5 6.9 %sample_residual.2.s1_in_ref = f32[1024,128]{1,0:T(8,128)} custom-call(f32[4096,128]{1,0:T(8,128)} %bitcast.11, s32[256,16,128]{2,1,0:T(8,128)} %bitcast.15, f32[16,16,16]{2,1,0:T(8,128)} %amp_ref.5, s32[16,16]{1,0:T(8,128)} %counts_ref.4, s32[16,16,16]{2,1,0:T(8,128)} %aper_ref.5), custom_call_target="tpu_custom_call" | custom-call | flops 4000000000 | bytes 4000000 | tf_op jit(solution)/shard_map/sample_residual/pallas_call | solution.py:360
  14.4 0.0 copy-done.6
  14.4 0.1 reshape.30.parts_ref
  14.4 0.0 collective-permute-done.1
  14.4 0.0 collective-permute-done
  14.5 0.0 copy-done.3
  14.5 0.0 copy-start.7
  14.6 0.0 copy-start.10
  14.6 1.6 %collective-permute-start.2 = (f32[32,8,128]{2,1,0:T(8,128)S(1)}, f32[32,8,128]{2,1,0:T(8,128)S(1)}, u32[]{:S(2)}, u32[]{:S(2)}) collective-permute-start(f32[32,8,128]{2,1,0:T(8,128)S(1)} %get-tuple-element.20), channel_id=1, source_target_pairs={{0,1},{1,2},{2,3},{4,5},{5,6},{6,7},{8,9},{9,10},{10,11},{12,13},{... | collective-permute-start | bytes 393224 | tf_op jit(solution)/shard_map/ppermute | solution.py:332
  16.2 1.3 %collective-permute-start.3 = (f32[32,8,128]{2,1,0:T(8,128)S(1)}, f32[32,8,128]{2,1,0:T(8,128)S(1)}, u32[]{:S(2)}, u32[]{:S(2)}) collective-permute-start(f32[32,8,128]{2,1,0:T(8,128)S(1)} %get-tuple-element.21), channel_id=1, source_target_pairs={{1,0},{2,1},{3,2},{5,4},{6,5},{7,6},{9,8},{10,9},{11,10},{13,12},{... | collective-permute-start | bytes 393224 | tf_op jit(solution)/shard_map/ppermute | solution.py:332
  17.5 0.0 copy-done
  17.5 0.0 copy-done.8
  17.5 0.0 copy-done.9
  17.5 5.9 %sample_residual.3.s1_more_ref = f32[1024,128]{1,0:T(8,128)S(1)} custom-call(f32[4096,128]{1,0:T(8,128)S(1)} %bitcast.12, s32[256,16,128]{2,1,0:T(8,128)} %bitcast.16, f32[16,16,16]{2,1,0:T(8,128)S(1)} %copy-done.9, s32[16,16]{1,0:T(8,128)S(1)} %copy-done.6, s32[16,16,16]{2,1,0:T(8,128)S(1)} %copy-done.8), custom_call_target="tpu_custom_call" | custom-call | flops 4000000000 | bytes 4000000 | tf_op jit(solution)/shard_map/sample_residual/pallas_call | solution.py:360
  23.4 0.0 copy-start.5
  23.4 0.0 copy-start.4
  23.4 0.0 collective-permute-done.2.left_ref
  23.4 0.0 collective-permute-done.3.right_ref
  23.4 0.0 copy-done.7
  23.4 0.0 copy-done.10
  23.4 32.1 %demigrate_and_sample.1 = (f32[4096,128]{1,0:T(8,128)S(1)}, f32[16,128]{1,0:T(8,128)S(1)}, f32[2,32,8,128]{3,2,1,0:T(8,128)S(1)}, f32[2,32,16,128]{3,2,1,0:T(8,128)S(1)}, f32[2,32,8,128]{3,2,1,0:T(8,128)S(1)}) custom-call(s32[16,16,16]{2,1,0:T(8,128)S(1)} %copy-done.8, s32[256,16,128]{2,1,0:T(8,128)S(1)} %bitcast.17, f32[16,16,16]{2,1,0:T(8,128)S(1)} %copy-done.9, ...), custom_call_target="tpu_custom_call" | custom-call | flops 20000000000 | bytes 8000000 | tf_op jit(solution)/shard_map/demigrate_and_sample/pallas_call | solution.py:399
  55.6 0.0 copy-start.1
  55.6 1.3 %copy-done.1 = f32[4096,128]{1,0:T(8,128)} copy-done((f32[4096,128]{1,0:T(8,128)}, f32[4096,128]{1,0:T(8,128)S(1)}, u32[]{:S(2)}) %copy-start.1) | copy-done | bytes 2097176
  56.9 5.1 %collective-permute-start.4 = (f32[2,32,8,128]{3,2,1,0:T(8,128)S(1)}, f32[2,32,8,128]{3,2,1,0:T(8,128)S(1)}, u32[]{:S(2)}, u32[]{:S(2)}) collective-permute-start(f32[2,32,8,128]{3,2,1,0:T(8,128)S(1)} %get-tuple-element.25), channel_id=1, source_target_pairs={{0,1},{1,2},{2,3},{4,5},{5,6},{6,7},{8,9},{9,10},{10,11},{12,13},{... | collective-permute-start | bytes 786440 | tf_op jit(solution)/shard_map/ppermute | solution.py:332
  62.0 1.3 %collective-permute-start.5 = (f32[2,32,8,128]{3,2,1,0:T(8,128)S(1)}, f32[2,32,8,128]{3,2,1,0:T(8,128)S(1)}, u32[]{:S(2)}, u32[]{:S(2)}) collective-permute-start(f32[2,32,8,128]{3,2,1,0:T(8,128)S(1)} %get-tuple-element.26), channel_id=1, source_target_pairs={{1,0},{2,1},{3,2},{5,4},{6,5},{7,6},{9,8},{10,9},{11,10},{13,12},{... | collective-permute-start | bytes 786440 | tf_op jit(solution)/shard_map/ppermute | solution.py:332
  63.3 0.0 collective-permute-done.4.low_ref
  63.3 3.4 %collective-permute-done.5.high_ref = f32[2,32,8,128]{3,2,1,0:T(8,128)S(1)} collective-permute-done((f32[2,32,8,128]{3,2,1,0:T(8,128)S(1)}, f32[2,32,8,128]{3,2,1,0:T(8,128)S(1)}, u32[]{:S(2)}, u32[]{:S(2)}) %collective-permute-start.5) | collective-permute-done | bytes 262176 | tf_op jit(solution)/shard_map/ppermute | solution.py:332
  66.7 0.1 fold_y.1
  66.8 4.3 %collective-permute-start.6 = (f32[2,8,16,128]{3,2,1,0:T(8,128)S(1)}, f32[2,8,16,128]{3,2,1,0:T(8,128)S(1)}, u32[]{:S(2)}, u32[]{:S(2)}) collective-permute-start(f32[2,8,16,128]{3,2,1,0:T(8,128)S(1)} %get-tuple-element.28), channel_id=1, source_target_pairs={{0,4},{4,8},{8,12},{12,16},{16,20},{20,24},{24,28},{1,5},{5,9},{9,... | collective-permute-start | bytes 393224 | tf_op jit(solution)/shard_map/ppermute | solution.py:332
  71.0 1.3 %collective-permute-start.7 = (f32[2,8,16,128]{3,2,1,0:T(8,128)S(1)}, f32[2,8,16,128]{3,2,1,0:T(8,128)S(1)}, u32[]{:S(2)}, u32[]{:S(2)}) collective-permute-start(f32[2,8,16,128]{3,2,1,0:T(8,128)S(1)} %get-tuple-element.29), channel_id=1, source_target_pairs={{4,0},{8,4},{12,8},{16,12},{20,16},{24,20},{28,24},{5,1},{9,5},{13... | collective-permute-start | bytes 393224 | tf_op jit(solution)/shard_map/ppermute | solution.py:332
  72.3 1.2 %collective-permute-done.6.low_ref = f32[2,8,16,128]{3,2,1,0:T(8,128)S(1)} collective-permute-done((f32[2,8,16,128]{3,2,1,0:T(8,128)S(1)}, f32[2,8,16,128]{3,2,1,0:T(8,128)S(1)}, u32[]{:S(2)}, u32[]{:S(2)}) %collective-permute-start.6) | collective-permute-done | bytes 131104 | tf_op jit(solution)/shard_map/ppermute | solution.py:332
  73.5 4.4 %collective-permute-done.7.high_ref = f32[2,8,16,128]{3,2,1,0:T(8,128)S(1)} collective-permute-done((f32[2,8,16,128]{3,2,1,0:T(8,128)S(1)}, f32[2,8,16,128]{3,2,1,0:T(8,128)S(1)}, u32[]{:S(2)}, u32[]{:S(2)}) %collective-permute-start.7) | collective-permute-done | bytes 131104 | tf_op jit(solution)/shard_map/ppermute | solution.py:332
  77.9 0.0 copy-done.5
  77.9 0.2 fold_x.1
  78.1 9.3 %all_to_all.10 = f32[4,1,128]{2,1,0:T(1,128)S(1)} all-to-all(f32[4,1,128]{2,1,0:T(1,128)S(1)} %get-tuple-element.31), channel_id=1, replica_groups=mesh['gx'=8,'gy'=4] {'gy'}, dimensions={0} | all-to-all | bytes 4096 | tf_op jit(solution)/shard_map/all_to_all | solution.py:457
  87.4 11.1 %all_to_all.11.stats_ref = f32[8,1,128]{2,1,0:T(1,128)S(1)} all-to-all(f32[8,1,128]{2,1,0:T(1,128)S(1)} %broadcast_in_dim.2), channel_id=1, replica_groups=mesh['gx'=8,'gy'=4] {'gx'}, dimensions={0} | all-to-all | bytes 8192 | tf_op jit(solution)/shard_map/all_to_all | solution.py:459
  98.5 0.0 copy-done.4
  98.5 0.0 copy-start.2
  98.5 1.6 %copy-done.2 = f32[4096,128]{1,0:T(8,128)S(1)} copy-done((f32[4096,128]{1,0:T(8,128)S(1)}, f32[4096,128]{1,0:T(8,128)}, u32[]{:S(2)}) %copy-start.2) | copy-done | bytes 2097176
  100.1 2.1 %update.1 = (f32[16,16,128]{2,1,0:T(8,128)}, f32[4096,128]{1,0:T(8,128)}, f32[16,16,128]{2,1,0:T(8,128)}) custom-call(f32[8,1,128]{2,1,0:T(1,128)S(1)} %all_to_all.11.stats_ref, f32[4096,128]{1,0:T(8,128)S(1)} %bitcast.14, f32[4096,128]{1,0:T(8,128)S(1)} %copy-done.2, f32[16,16,128]{2,1,0:T(8,128)S(1)} %copy-done.4, f32[16,16,128]{2,1,0:T(8,128)S(1)} %copy-done.3, ...), custom_call_target="tpu_custom_call" | custom-call | tf_op jit(solution)/shard_map/update/pallas_call | solution.py:467
  (6 shorter events, 0.1 us)
Async XLA Ops:
  0.6 13.8 %collective-permute-start.1 = (f32[16,16,128]{2,1,0:T(8,128)}, f32[16,16,128]{2,1,0:T(8,128)S(1)}, u32[]{:S(2)}, u32[]{:S(2)}) collective-permute-start(f32[16,16,128]{2,1,0:T(8,128)} %dir_ref.1), channel_id=1, source_target_pairs={{4,0},{8,4},{12,8},{16,12},{20,16},{24,20},{28,24},{5,1},{9,5},{13... | collective-permute-start | bytes 393224 | tf_op jit(solution)/shard_map/ppermute | solution.py:332
  1.9 12.5 %collective-permute-start = (f32[16,16,128]{2,1,0:T(8,128)}, f32[16,16,128]{2,1,0:T(8,128)S(1)}, u32[]{:S(2)}, u32[]{:S(2)}) collective-permute-start(f32[16,16,128]{2,1,0:T(8,128)} %dir_ref.1), channel_id=1, source_target_pairs={{0,4},{4,8},{8,12},{12,16},{16,20},{20,24},{24,28},{1,5},{5,9},{9,... | collective-permute-start | bytes 393224 | tf_op jit(solution)/shard_map/ppermute | solution.py:332
  7.4 6.9 %copy-start.6 = (s32[16,16]{1,0:T(8,128)S(1)}, s32[16,16]{1,0:T(8,128)}, u32[]{:S(2)}) copy-start(s32[16,16]{1,0:T(8,128)} %counts_ref.4) | copy-start | bytes 3076
  7.4 7.0 %copy-start.3 = (f32[16,16,128]{2,1,0:T(8,128)S(1)}, f32[16,16,128]{2,1,0:T(8,128)}, u32[]{:S(2)}) copy-start(f32[16,16,128]{2,1,0:T(8,128)} %dir_ref.1) | copy-start | bytes 393220
  7.4 10.0 %copy-start = (f32[16,16,2048]{2,1,0:T(8,128)S(1)}, f32[16,16,2048]{2,1,0:T(8,128)}, u32[]{:S(2)}) copy-start(f32[16,16,2048]{2,1,0:T(8,128)} %param.9) | copy-start | bytes 6291460
  7.4 10.0 %copy-start.8 = (s32[16,16,16]{2,1,0:T(8,128)S(1)}, s32[16,16,16]{2,1,0:T(8,128)}, u32[]{:S(2)}) copy-start(s32[16,16,16]{2,1,0:T(8,128)} %aper_ref.5) | copy-start | bytes 49156
  7.5 10.0 %copy-start.9 = (f32[16,16,16]{2,1,0:T(8,128)S(1)}, f32[16,16,16]{2,1,0:T(8,128)}, u32[]{:S(2)}) copy-start(f32[16,16,16]{2,1,0:T(8,128)} %amp_ref.5) | copy-start | bytes 49156
  14.5 8.9 %copy-start.7 = (s32[16,16,16,128]{3,2,1,0:T(8,128)S(1)}, s32[16,16,16,128]{3,2,1,0:T(8,128)}, u32[]{:S(2)}) copy-start(s32[16,16,16,128]{3,2,1,0:T(8,128)} %param.13) | copy-start | bytes 6291460
  14.6 8.9 %copy-start.10 = (f32[1024,128]{1,0:T(8,128)S(1)}, f32[1024,128]{1,0:T(8,128)}, u32[]{:S(2)}) copy-start(f32[1024,128]{1,0:T(8,128)} %sample_residual.2.s1_in_ref) | copy-start | bytes 1572868
  14.6 8.8 %collective-permute-start.2 = (f32[32,8,128]{2,1,0:T(8,128)S(1)}, f32[32,8,128]{2,1,0:T(8,128)S(1)}, u32[]{:S(2)}, u32[]{:S(2)}) collective-permute-start(f32[32,8,128]{2,1,0:T(8,128)S(1)} %get-tuple-element.20), channel_id=1, source_target_pairs={{0,1},{1,2},{2,3},{4,5},{5,6},{6,7},{8,9},{9,10},{10,11},{12,13},{... | collective-permute-start | bytes 393224 | tf_op jit(solution)/shard_map/ppermute | solution.py:332
  16.2 7.3 %collective-permute-start.3 = (f32[32,8,128]{2,1,0:T(8,128)S(1)}, f32[32,8,128]{2,1,0:T(8,128)S(1)}, u32[]{:S(2)}, u32[]{:S(2)}) collective-permute-start(f32[32,8,128]{2,1,0:T(8,128)S(1)} %get-tuple-element.21), channel_id=1, source_target_pairs={{1,0},{2,1},{3,2},{5,4},{6,5},{7,6},{9,8},{10,9},{11,10},{13,12},{... | collective-permute-start | bytes 393224 | tf_op jit(solution)/shard_map/ppermute | solution.py:332
  23.4 54.5 %copy-start.5 = (f32[16,16,128]{2,1,0:T(8,128)S(1)}, f32[16,16,128]{2,1,0:T(8,128)}, u32[]{:S(2)}) copy-start(f32[16,16,128]{2,1,0:T(8,128)} %grad_ref.1) | copy-start | bytes 393220
  23.4 75.1 %copy-start.4 = (f32[16,16,128]{2,1,0:T(8,128)S(1)}, f32[16,16,128]{2,1,0:T(8,128)}, u32[]{:S(2)}) copy-start(f32[16,16,128]{2,1,0:T(8,128)} %model_ref.1) | copy-start | bytes 393220
  55.6 1.3 %copy-start.1 = (f32[4096,128]{1,0:T(8,128)}, f32[4096,128]{1,0:T(8,128)S(1)}, u32[]{:S(2)}) copy-start(f32[4096,128]{1,0:T(8,128)S(1)} %get-tuple-element.32.data_ref) | copy-start | bytes 6291460
  56.9 6.4 %collective-permute-start.4 = (f32[2,32,8,128]{3,2,1,0:T(8,128)S(1)}, f32[2,32,8,128]{3,2,1,0:T(8,128)S(1)}, u32[]{:S(2)}, u32[]{:S(2)}) collective-permute-start(f32[2,32,8,128]{3,2,1,0:T(8,128)S(1)} %get-tuple-element.25), channel_id=1, source_target_pairs={{0,1},{1,2},{2,3},{4,5},{5,6},{6,7},{8,9},{9,10},{10,11},{12,13},{... | collective-permute-start | bytes 786440 | tf_op jit(solution)/shard_map/ppermute | solution.py:332
  62.0 4.7 %collective-permute-start.5 = (f32[2,32,8,128]{3,2,1,0:T(8,128)S(1)}, f32[2,32,8,128]{3,2,1,0:T(8,128)S(1)}, u32[]{:S(2)}, u32[]{:S(2)}) collective-permute-start(f32[2,32,8,128]{3,2,1,0:T(8,128)S(1)} %get-tuple-element.26), channel_id=1, source_target_pairs={{1,0},{2,1},{3,2},{5,4},{6,5},{7,6},{9,8},{10,9},{11,10},{13,12},{... | collective-permute-start | bytes 786440 | tf_op jit(solution)/shard_map/ppermute | solution.py:332
  66.8 6.8 %collective-permute-start.6 = (f32[2,8,16,128]{3,2,1,0:T(8,128)S(1)}, f32[2,8,16,128]{3,2,1,0:T(8,128)S(1)}, u32[]{:S(2)}, u32[]{:S(2)}) collective-permute-start(f32[2,8,16,128]{3,2,1,0:T(8,128)S(1)} %get-tuple-element.28), channel_id=1, source_target_pairs={{0,4},{4,8},{8,12},{12,16},{16,20},{20,24},{24,28},{1,5},{5,9},{9,... | collective-permute-start | bytes 393224 | tf_op jit(solution)/shard_map/ppermute | solution.py:332
  71.0 6.9 %collective-permute-start.7 = (f32[2,8,16,128]{3,2,1,0:T(8,128)S(1)}, f32[2,8,16,128]{3,2,1,0:T(8,128)S(1)}, u32[]{:S(2)}, u32[]{:S(2)}) collective-permute-start(f32[2,8,16,128]{3,2,1,0:T(8,128)S(1)} %get-tuple-element.29), channel_id=1, source_target_pairs={{4,0},{8,4},{12,8},{16,12},{20,16},{24,20},{28,24},{5,1},{9,5},{13... | collective-permute-start | bytes 393224 | tf_op jit(solution)/shard_map/ppermute | solution.py:332
  98.5 1.6 %copy-start.2 = (f32[4096,128]{1,0:T(8,128)S(1)}, f32[4096,128]{1,0:T(8,128)}, u32[]{:S(2)}) copy-start(f32[4096,128]{1,0:T(8,128)} %copy-done.1) | copy-start | bytes 6291460

commit v9 on v6

--- a/solution.py
+++ b/solution.py
@@ -90,7 +90,7 @@
 
 
 def first_kernel(
-    geo, row0, res_ref, times_ref, amp_ref, counts_ref, aper_ref, s_ref, vals, scales
+    geo, row0, res_ref, times_ref, amp_ref, counts_ref, aper_ref, s_ref, vals, scales, traces
 ):
     bins_y, entries, highs, wide_y = geo
     step = pl.program_id(0)
@@ -99,9 +99,10 @@
     def _():
         s_ref[...] = jnp.zeros_like(s_ref)
 
+    traces[pl.ds(0, bins_y * highs), :] = res_ref[...]
     fill_weights(amp_ref[0], counts_ref[pl.ds(step + row0, 1), :], scales)
     for b in range(bins_y):
-        sample_bin(res_ref, trace_row(b, highs), highs, times_ref, b, b, scales, vals)
+        sample_bin(traces, trace_row(b, highs), highs, times_ref, b, b, scales, vals)
     both = split_values(vals)
     spread_bins(both, place_row(aper_ref[0], wide_y), s_ref, step + row0, wide_y)
 
@@ -175,8 +176,7 @@
     out_mid,
     out_right,
     image,
-    s1_ref,
-    s2_ref,
+    s_ref,
     vals,
     res_vals,
     scales,
@@ -185,6 +185,7 @@
     old_data,
     both,
     res_both,
+    traces,
     *works,
 ):
     bins_y, entries, highs, wide_y = geo
@@ -194,10 +195,13 @@
     cut = bins_x // (bins_x - row0)
     res_bins = bins_y // cut
 
-    s1_ref[...] = s1_in_ref[...] + s1_more_ref[...]
-    s2_ref[...] = jnp.zeros_like(s2_ref)
-    old_data[...] = jnp.zeros_like(old_data)
-    scales[...] = jnp.zeros_like(scales)
+    columns = wide_x * wide_y
+    current = pl.ds(0, rows_per)
+    s_ref[pl.ds(0, columns), :] = s1_in_ref[...] + s1_more_ref[...]
+    s_ref[pl.ds(columns, columns), :] = jnp.zeros((columns, LANES), F32)
+    odd_row = row0 - 1
+    old_data[current, :] = res_ref[pl.ds(odd_row * rows_per, rows_per), :]
+    fill_weights(amp_ref[odd_row], counts_ref[pl.ds(odd_row, 1), :], scales)
     both[...] = jnp.zeros_like(both)
     res_both[...] = jnp.zeros_like(res_both)
     for x in range(wide_x):
@@ -208,21 +212,25 @@
     def residual_part(step):
         return row0 + step // cut, (step % cut) * res_bins
 
-    def spread_image(row):
-        spread_bins(both[...], place_row(aper_ref[row], wide_y), s2_ref, row, wide_y)
+    def spread_image(step):
+        row = jnp.where(step < 1, odd_row, step - 1)
+        at = jnp.where(step < 1, odd_row, step - 1 + wide_x)
+        spread_bins(both[...], place_row(aper_ref[row], wide_y), s_ref, at, wide_y)
 
     def spread_residual(step):
         row, part = residual_part(step)
         entry = aper_ref[row, pl.ds(pl.multiple_of(part, SUB), res_bins), :]
-        spread_bins(res_both[...], place_row(entry, wide_y, part), s1_ref, row, wide_y)
+        spread_bins(res_both[...], place_row(entry, wide_y, part), s_ref, row, wide_y)
 
     def one_row(step, total):
-        before = jnp.maximum(step - 1, 0)
-        spread_image(jnp.maximum(step - 2, 0))
-        spread_residual(before)
+        before = jnp.where(step < 1, odd_row, step - 1)
+        spread_image(step - 1)
+        spread_residual(jnp.maximum(step - 1, 0))
         res_row, res_part = residual_part(step)
         res_first = pl.multiple_of(res_row * rows_per + res_part * highs, SUB)
         old_scales[...] = scales[...]
+        part = res_bins * highs
+        traces[pl.ds(0, part), :] = res_ref[pl.ds(res_first, part), :]
         fill_weights(amp_ref[step], counts_ref[pl.ds(step, 1), :], scales)
         fill_weights(
             amp_ref[res_row, pl.ds(pl.multiple_of(res_part, SUB), res_bins), :],
@@ -241,28 +249,29 @@
             )
             if b % cut == 0:
                 r = b // cut
-                first = res_first + trace_row(r, highs)
+                first = trace_row(r, highs)
                 at = res_row * bins_y + res_part + r
-                sample_bin(res_ref, first, highs, times_ref, at, r, res_scales, res_vals)
+                sample_bin(traces, first, highs, times_ref, at, r, res_scales, res_vals)
         both[...] = split_values(vals)
         res_both[...] = split_values(res_vals)
-        old_data[...] = data_ref[pl.ds(pl.multiple_of(step * rows_per, SUB), rows_per), :]
+        old_data[current, :] = data_ref[pl.ds(pl.multiple_of(step * rows_per, SUB), rows_per), :]
         return total
 
     curv_ref[...] = lax.fori_loop(0, bins_x, one_row, jnp.zeros((highs, LANES), F32))
     last = bins_x - 1
-    spread_image(last - 1)
+    spread_image(last)
     spread_residual(last)
     for b in range(bins_y):
         at = last * bins_y + b
         sample_bin(old_data, trace_row(b, highs), highs, times_ref, at, b, scales, vals)
     both[...] = split_values(vals)
-    spread_image(last)
-    for k, ref in enumerate((s1_ref, s2_ref)):
+    spread_image(bins_x)
+    for k in range(2):
         for x in range(wide_x):
-            out_left[k, x] = ref[pl.ds(x * wide_y, RADIUS), :]
-            out_mid[k, x] = ref[pl.ds(x * wide_y + RADIUS, bins_y), :]
-            out_right[k, x] = ref[pl.ds(x * wide_y + RADIUS + bins_y, RADIUS), :]
+            at = k * columns + x * wide_y
+            out_left[k, x] = s_ref[pl.ds(at, RADIUS), :]
+            out_mid[k, x] = s_ref[pl.ds(at + RADIUS, bins_y), :]
+            out_right[k, x] = s_ref[pl.ds(at + RADIUS + bins_y, RADIUS), :]
 
 
 def fold_y_kernel(mid_ref, low_ref, high_ref, out_head, out_mid, out_tail):
@@ -369,7 +378,8 @@
             ],
             out_specs=pl.BlockSpec((columns, depths), lambda i: (0, 0)),
             out_shape=jax.ShapeDtypeStruct((columns, depths), F32),
-            scratch_shapes=[pltpu.VMEM((bins_y * entries, depths), F32)] * 2,
+            scratch_shapes=[pltpu.VMEM((bins_y * entries, depths), F32)] * 2
+            + [pltpu.VMEM((rows_per + SUB, LANES), F32)],
             compiler_params=params(limit),
             cost_estimate=pl.CostEstimate(
                 flops=4 * 10**9, bytes_accessed=4 * 10**6, transcendentals=0
@@ -386,7 +396,7 @@
     )
     left = shift(tail, "gy", 1)
     right = shift(head, "gy", -1)
-    s1_more = first(early, early, counts, VMEM_LIMIT)
+    s1_more = first(early, early - 1, counts, VMEM_LIMIT)
 
     cut = bins_x // (bins_x - row0)
     res_bins = bins_y // cut
@@ -407,11 +417,12 @@
             jax.ShapeDtypeStruct((2, wide_x, bins_y, depths), F32),
             strip,
         ],
-        scratch_shapes=[columns_shape, columns_shape, columns_shape]
+        scratch_shapes=[columns_shape, pltpu.VMEM((2 * columns, depths), F32)]
         + [vals_shape, res_shape, vals_shape, vals_shape, res_shape]
-        + [pltpu.VMEM((rows_per, LANES), F32)]
+        + [pltpu.VMEM((rows_per + SUB, LANES), F32)]
         + [pltpu.VMEM((bins_y * entries, 2 * depths), BF16)]
         + [pltpu.VMEM((res_bins * entries, 2 * depths), BF16)]
+        + [pltpu.VMEM((res_bins * highs + SUB, LANES), F32)]
         + [pltpu.VMEM((4, entries + SUB, LANES), F32)] * 8,
         compiler_params=params(MAIN_LIMIT),
         cost_estimate=pl.CostEstimate(

time: 94.2 us -> 93.8 us (level)
    pallas_call x2, Pallas kernels: 12.8 us -> 11.6 us  [first(): pl.pallas_call(functools.partial(first_kernel, geo, row0), grid=(count,),...]
  transfers between devices with their start and end apart: 8 -> 8, of which waited for: 3 -> 3; matrix products, arithmetic and copies ran while one was open for 0% -> 0% of each run, Pallas kernels for 14% -> 12%
where the time goes in v9:
time: 93.8 us; the launch traced here: 93.4 us
  Pallas kernels  46.9 us (50%)
  starting transfers between devices  21.7 us (23%)
  blocking collectives  14.8 us (16%)
  waiting for transfers between devices  8.91 us (9%)
    pallas_call x1, Pallas kernels, body(): pl.pallas_call(functools.partial(main_kernel, geo, row0), in_specs=[pl.Bl...  32.9 us
    ppermute x8, starting transfers between devices, shift(): return lax.ppermute(cells, axis, pairs)  21.7 us
    all_to_all x1, blocking collectives, body(): stats = lax.all_to_all(stats, ('gx', 'gy'), 0, 0, tiled=True)  14.8 us
    pallas_call x2, Pallas kernels, first(): pl.pallas_call(functools.partial(first_kernel, geo, row0), grid=(count,),...  11.6 us
    ppermute x8, waiting for transfers between devices, shift(): return lax.ppermute(cells, axis, pairs)  8.91 us
    pallas_call x1, Pallas kernels, body(): pl.pallas_call(last_kernel, grid=(steps,), in_specs=[pl.BlockSpec(stats.s...  2.24 us
  transfers between devices with their start and end apart: 8, of which 3 were waited for; matrix products, arithmetic and copies ran while one was open for 0% of the time, Pallas kernels for 12%

profile of v9, /device:TPU:0, one launch (start us, length us, event | category | flops | bytes accessed | tf_op | source)
XLA Modules:
  0.0 93.4 jit_solution(16036113691943534227)
XLA Ops:
  0.6 1.3 %collective-permute-start.1 = (f32[16,16,128]{2,1,0:T(8,128)}, f32[16,16,128]{2,1,0:T(8,128)S(1)}, u32[]{:S(2)}, u32[]{:S(2)}) collective-permute-start(f32[16,16,128]{2,1,0:T(8,128)} %dir_ref.1), channel_id=1, source_target_pairs={{4,0},{8,4},{12,8},{16,12},{20,16},{24,20},{28,24},{5,1},{9,5},{13... | collective-permute-start | bytes 393224 | tf_op jit(solution)/shard_map/ppermute | solution.py:341
  1.9 5.5 %collective-permute-start = (f32[16,16,128]{2,1,0:T(8,128)}, f32[16,16,128]{2,1,0:T(8,128)S(1)}, u32[]{:S(2)}, u32[]{:S(2)}) collective-permute-start(f32[16,16,128]{2,1,0:T(8,128)} %dir_ref.1), channel_id=1, source_target_pairs={{0,4},{4,8},{8,12},{12,16},{16,20},{20,24},{24,28},{1,5},{5,9},{9,... | collective-permute-start | bytes 393224 | tf_op jit(solution)/shard_map/ppermute | solution.py:341
  7.4 0.0 copy-start.4
  7.4 0.0 copy-start.1
  7.4 0.0 copy-start
  7.4 0.0 copy-start.6
  7.5 0.0 copy-start.7
  7.5 6.9 %sample_residual.2.s1_in_ref = f32[1024,128]{1,0:T(8,128)} custom-call(f32[4096,128]{1,0:T(8,128)} %bitcast.11, s32[256,16,128]{2,1,0:T(8,128)} %bitcast.15, f32[16,16,16]{2,1,0:T(8,128)} %amp_ref.5, s32[16,16]{1,0:T(8,128)} %counts_ref.4, s32[16,16,16]{2,1,0:T(8,128)} %aper_ref.5), custom_call_target="tpu_custom_call" | custom-call | flops 4000000000 | bytes 4000000 | tf_op jit(solution)/shard_map/sample_residual/pallas_call | solution.py:369
  14.4 0.0 copy-done.4
  14.4 0.1 reshape.25.parts_ref
  14.5 0.0 collective-permute-done.1
  14.5 0.0 collective-permute-done
  14.5 0.0 copy-done.1
  14.6 0.0 copy-start.5
  14.6 0.0 copy-start.8
  14.6 1.6 %collective-permute-start.2 = (f32[32,8,128]{2,1,0:T(8,128)S(1)}, f32[32,8,128]{2,1,0:T(8,128)S(1)}, u32[]{:S(2)}, u32[]{:S(2)}) collective-permute-start(f32[32,8,128]{2,1,0:T(8,128)S(1)} %get-tuple-element.20), channel_id=1, source_target_pairs={{0,1},{1,2},{2,3},{4,5},{5,6},{6,7},{8,9},{9,10},{10,11},{12,13},{... | collective-permute-start | bytes 393224 | tf_op jit(solution)/shard_map/ppermute | solution.py:341
  16.2 1.3 %collective-permute-start.3 = (f32[32,8,128]{2,1,0:T(8,128)S(1)}, f32[32,8,128]{2,1,0:T(8,128)S(1)}, u32[]{:S(2)}, u32[]{:S(2)}) collective-permute-start(f32[32,8,128]{2,1,0:T(8,128)S(1)} %get-tuple-element.21), channel_id=1, source_target_pairs={{1,0},{2,1},{3,2},{5,4},{6,5},{7,6},{9,8},{10,9},{11,10},{13,12},{... | collective-permute-start | bytes 393224 | tf_op jit(solution)/shard_map/ppermute | solution.py:341
  17.5 0.0 copy-done
  17.5 0.0 copy-done.6
  17.5 0.0 copy-done.7
  17.5 4.7 %sample_residual.3.s1_more_ref = f32[1024,128]{1,0:T(8,128)S(1)} custom-call(f32[4096,128]{1,0:T(8,128)S(1)} %bitcast.12, s32[256,16,128]{2,1,0:T(8,128)} %bitcast.16, f32[16,16,16]{2,1,0:T(8,128)S(1)} %copy-done.7, s32[16,16]{1,0:T(8,128)S(1)} %copy-done.4, s32[16,16,16]{2,1,0:T(8,128)S(1)} %copy-done.6), custom_call_target="tpu_custom_call" | custom-call | flops 4000000000 | bytes 4000000 | tf_op jit(solution)/shard_map/sample_residual/pallas_call | solution.py:369
  22.2 0.0 copy-start.3
  22.2 0.0 copy-start.2
  22.2 0.0 collective-permute-done.2.left_ref
  22.2 0.0 collective-permute-done.3.right_ref
  22.2 0.0 copy-done.5
  22.2 0.0 copy-done.8
  22.3 32.9 %demigrate_and_sample.1 = (f32[4096,128]{1,0:T(8,128)S(1)}, f32[16,128]{1,0:T(8,128)S(1)}, f32[2,32,8,128]{3,2,1,0:T(8,128)S(1)}, f32[2,32,16,128]{3,2,1,0:T(8,128)S(1)}, f32[2,32,8,128]{3,2,1,0:T(8,128)S(1)}) custom-call(s32[16,16,16]{2,1,0:T(8,128)S(1)} %copy-done.6, s32[256,16,128]{2,1,0:T(8,128)S(1)} %bitcast.17, f32[16,16,16]{2,1,0:T(8,128)S(1)} %copy-done.7, ...), custom_call_target="tpu_custom_call" | custom-call | flops 20000000000 | bytes 8000000 | tf_op jit(solution)/shard_map/demigrate_and_sample/pallas_call | solution.py:409
  55.1 5.1 %collective-permute-start.4 = (f32[2,32,8,128]{3,2,1,0:T(8,128)S(1)}, f32[2,32,8,128]{3,2,1,0:T(8,128)S(1)}, u32[]{:S(2)}, u32[]{:S(2)}) collective-permute-start(f32[2,32,8,128]{3,2,1,0:T(8,128)S(1)} %get-tuple-element.25), channel_id=1, source_target_pairs={{0,1},{1,2},{2,3},{4,5},{5,6},{6,7},{8,9},{9,10},{10,11},{12,13},{... | collective-permute-start | bytes 786440 | tf_op jit(solution)/shard_map/ppermute | solution.py:341
  60.3 1.3 %collective-permute-start.5 = (f32[2,32,8,128]{3,2,1,0:T(8,128)S(1)}, f32[2,32,8,128]{3,2,1,0:T(8,128)S(1)}, u32[]{:S(2)}, u32[]{:S(2)}) collective-permute-start(f32[2,32,8,128]{3,2,1,0:T(8,128)S(1)} %get-tuple-element.26), channel_id=1, source_target_pairs={{1,0},{2,1},{3,2},{5,4},{6,5},{7,6},{9,8},{10,9},{11,10},{13,12},{... | collective-permute-start | bytes 786440 | tf_op jit(solution)/shard_map/ppermute | solution.py:341
  61.6 0.0 collective-permute-done.4.low_ref
  61.6 3.3 %collective-permute-done.5.high_ref = f32[2,32,8,128]{3,2,1,0:T(8,128)S(1)} collective-permute-done((f32[2,32,8,128]{3,2,1,0:T(8,128)S(1)}, f32[2,32,8,128]{3,2,1,0:T(8,128)S(1)}, u32[]{:S(2)}, u32[]{:S(2)}) %collective-permute-start.5) | collective-permute-done | bytes 262176 | tf_op jit(solution)/shard_map/ppermute | solution.py:341
  64.9 0.1 fold_y.1
  65.0 4.3 %collective-permute-start.6 = (f32[2,8,16,128]{3,2,1,0:T(8,128)S(1)}, f32[2,8,16,128]{3,2,1,0:T(8,128)S(1)}, u32[]{:S(2)}, u32[]{:S(2)}) collective-permute-start(f32[2,8,16,128]{3,2,1,0:T(8,128)S(1)} %get-tuple-element.28), channel_id=1, source_target_pairs={{0,4},{4,8},{8,12},{12,16},{16,20},{20,24},{24,28},{1,5},{5,9},{9,... | collective-permute-start | bytes 393224 | tf_op jit(solution)/shard_map/ppermute | solution.py:341
  69.3 1.3 %collective-permute-start.7 = (f32[2,8,16,128]{3,2,1,0:T(8,128)S(1)}, f32[2,8,16,128]{3,2,1,0:T(8,128)S(1)}, u32[]{:S(2)}, u32[]{:S(2)}) collective-permute-start(f32[2,8,16,128]{3,2,1,0:T(8,128)S(1)} %get-tuple-element.29), channel_id=1, source_target_pairs={{4,0},{8,4},{12,8},{16,12},{20,16},{24,20},{28,24},{5,1},{9,5},{13... | collective-permute-start | bytes 393224 | tf_op jit(solution)/shard_map/ppermute | solution.py:341
  70.6 1.2 %collective-permute-done.6.low_ref = f32[2,8,16,128]{3,2,1,0:T(8,128)S(1)} collective-permute-done((f32[2,8,16,128]{3,2,1,0:T(8,128)S(1)}, f32[2,8,16,128]{3,2,1,0:T(8,128)S(1)}, u32[]{:S(2)}, u32[]{:S(2)}) %collective-permute-start.6) | collective-permute-done | bytes 131104 | tf_op jit(solution)/shard_map/ppermute | solution.py:341
  71.8 4.4 %collective-permute-done.7.high_ref = f32[2,8,16,128]{3,2,1,0:T(8,128)S(1)} collective-permute-done((f32[2,8,16,128]{3,2,1,0:T(8,128)S(1)}, f32[2,8,16,128]{3,2,1,0:T(8,128)S(1)}, u32[]{:S(2)}, u32[]{:S(2)}) %collective-permute-start.7) | collective-permute-done | bytes 131104 | tf_op jit(solution)/shard_map/ppermute | solution.py:341
  76.2 0.0 copy-done.3
  76.2 0.2 fold_x.1
  76.4 14.8 %all_to_all.5.stats_ref = f32[32,1,128]{2,1,0:T(1,128)S(1)} all-to-all(f32[32,1,128]{2,1,0:T(1,128)S(1)} %get-tuple-element.31), channel_id=1, replica_groups=mesh['gx'=8,'gy'=4] {'gx','gy'}, dimensions={0} | all-to-all | bytes 32768 | tf_op jit(solution)/shard_map/all_to_all | solution.py:468
  91.2 0.0 copy-done.2
  91.2 2.2 %update.1 = (f32[16,16,128]{2,1,0:T(8,128)}, f32[4096,128]{1,0:T(8,128)}, f32[16,16,128]{2,1,0:T(8,128)}) custom-call(f32[32,1,128]{2,1,0:T(1,128)S(1)} %all_to_all.5.stats_ref, f32[4096,128]{1,0:T(8,128)S(1)} %bitcast.14, f32[4096,128]{1,0:T(8,128)S(1)} %get-tuple-element.32.data_ref, f32[16,16,128]{2,1,0:T(8,128)S(1)} %copy-done.2, ...), custom_call_target="tpu_custom_call" | custom-call | tf_op jit(solution)/shard_map/update/pallas_call | solution.py:476
  (4 shorter events, 0.1 us)
Async XLA Ops:
  0.6 13.8 %collective-permute-start.1 = (f32[16,16,128]{2,1,0:T(8,128)}, f32[16,16,128]{2,1,0:T(8,128)S(1)}, u32[]{:S(2)}, u32[]{:S(2)}) collective-permute-start(f32[16,16,128]{2,1,0:T(8,128)} %dir_ref.1), channel_id=1, source_target_pairs={{4,0},{8,4},{12,8},{16,12},{20,16},{24,20},{28,24},{5,1},{9,5},{13... | collective-permute-start | bytes 393224 | tf_op jit(solution)/shard_map/ppermute | solution.py:341
  1.9 12.5 %collective-permute-start = (f32[16,16,128]{2,1,0:T(8,128)}, f32[16,16,128]{2,1,0:T(8,128)S(1)}, u32[]{:S(2)}, u32[]{:S(2)}) collective-permute-start(f32[16,16,128]{2,1,0:T(8,128)} %dir_ref.1), channel_id=1, source_target_pairs={{0,4},{4,8},{8,12},{12,16},{16,20},{20,24},{24,28},{1,5},{5,9},{9,... | collective-permute-start | bytes 393224 | tf_op jit(solution)/shard_map/ppermute | solution.py:341
  7.4 7.0 %copy-start.4 = (s32[16,16]{1,0:T(8,128)S(1)}, s32[16,16]{1,0:T(8,128)}, u32[]{:S(2)}) copy-start(s32[16,16]{1,0:T(8,128)} %counts_ref.4) | copy-start | bytes 3076
  7.4 7.1 %copy-start.1 = (f32[16,16,128]{2,1,0:T(8,128)S(1)}, f32[16,16,128]{2,1,0:T(8,128)}, u32[]{:S(2)}) copy-start(f32[16,16,128]{2,1,0:T(8,128)} %dir_ref.1) | copy-start | bytes 393220
  7.4 10.1 %copy-start = (f32[16,16,2048]{2,1,0:T(8,128)S(1)}, f32[16,16,2048]{2,1,0:T(8,128)}, u32[]{:S(2)}) copy-start(f32[16,16,2048]{2,1,0:T(8,128)} %param.9) | copy-start | bytes 6291460
  7.4 10.1 %copy-start.6 = (s32[16,16,16]{2,1,0:T(8,128)S(1)}, s32[16,16,16]{2,1,0:T(8,128)}, u32[]{:S(2)}) copy-start(s32[16,16,16]{2,1,0:T(8,128)} %aper_ref.5) | copy-start | bytes 49156
  7.5 10.1 %copy-start.7 = (f32[16,16,16]{2,1,0:T(8,128)S(1)}, f32[16,16,16]{2,1,0:T(8,128)}, u32[]{:S(2)}) copy-start(f32[16,16,16]{2,1,0:T(8,128)} %amp_ref.5) | copy-start | bytes 49156
  14.6 7.7 %copy-start.5 = (s32[16,16,16,128]{3,2,1,0:T(8,128)S(1)}, s32[16,16,16,128]{3,2,1,0:T(8,128)}, u32[]{:S(2)}) copy-start(s32[16,16,16,128]{3,2,1,0:T(8,128)} %param.13) | copy-start | bytes 6291460
  14.6 7.7 %copy-start.8 = (f32[1024,128]{1,0:T(8,128)S(1)}, f32[1024,128]{1,0:T(8,128)}, u32[]{:S(2)}) copy-start(f32[1024,128]{1,0:T(8,128)} %sample_residual.2.s1_in_ref) | copy-start | bytes 1572868
  14.6 7.6 %collective-permute-start.2 = (f32[32,8,128]{2,1,0:T(8,128)S(1)}, f32[32,8,128]{2,1,0:T(8,128)S(1)}, u32[]{:S(2)}, u32[]{:S(2)}) collective-permute-start(f32[32,8,128]{2,1,0:T(8,128)S(1)} %get-tuple-element.20), channel_id=1, source_target_pairs={{0,1},{1,2},{2,3},{4,5},{5,6},{6,7},{8,9},{9,10},{10,11},{12,13},{... | collective-permute-start | bytes 393224 | tf_op jit(solution)/shard_map/ppermute | solution.py:341
  16.2 6.0 %collective-permute-start.3 = (f32[32,8,128]{2,1,0:T(8,128)S(1)}, f32[32,8,128]{2,1,0:T(8,128)S(1)}, u32[]{:S(2)}, u32[]{:S(2)}) collective-permute-start(f32[32,8,128]{2,1,0:T(8,128)S(1)} %get-tuple-element.21), channel_id=1, source_target_pairs={{1,0},{2,1},{3,2},{5,4},{6,5},{7,6},{9,8},{10,9},{11,10},{13,12},{... | collective-permute-start | bytes 393224 | tf_op jit(solution)/shard_map/ppermute | solution.py:341
  22.2 54.0 %copy-start.3 = (f32[16,16,128]{2,1,0:T(8,128)S(1)}, f32[16,16,128]{2,1,0:T(8,128)}, u32[]{:S(2)}) copy-start(f32[16,16,128]{2,1,0:T(8,128)} %grad_ref.1) | copy-start | bytes 393220
  22.2 69.0 %copy-start.2 = (f32[16,16,128]{2,1,0:T(8,128)S(1)}, f32[16,16,128]{2,1,0:T(8,128)}, u32[]{:S(2)}) copy-start(f32[16,16,128]{2,1,0:T(8,128)} %model_ref.1) | copy-start | bytes 393220
  55.1 6.5 %collective-permute-start.4 = (f32[2,32,8,128]{3,2,1,0:T(8,128)S(1)}, f32[2,32,8,128]{3,2,1,0:T(8,128)S(1)}, u32[]{:S(2)}, u32[]{:S(2)}) collective-permute-start(f32[2,32,8,128]{3,2,1,0:T(8,128)S(1)} %get-tuple-element.25), channel_id=1, source_target_pairs={{0,1},{1,2},{2,3},{4,5},{5,6},{6,7},{8,9},{9,10},{10,11},{12,13},{... | collective-permute-start | bytes 786440 | tf_op jit(solution)/shard_map/ppermute | solution.py:341
  60.3 4.6 %collective-permute-start.5 = (f32[2,32,8,128]{3,2,1,0:T(8,128)S(1)}, f32[2,32,8,128]{3,2,1,0:T(8,128)S(1)}, u32[]{:S(2)}, u32[]{:S(2)}) collective-permute-start(f32[2,32,8,128]{3,2,1,0:T(8,128)S(1)} %get-tuple-element.26), channel_id=1, source_target_pairs={{1,0},{2,1},{3,2},{5,4},{6,5},{7,6},{9,8},{10,9},{11,10},{13,12},{... | collective-permute-start | bytes 786440 | tf_op jit(solution)/shard_map/ppermute | solution.py:341
  65.0 6.8 %collective-permute-start.6 = (f32[2,8,16,128]{3,2,1,0:T(8,128)S(1)}, f32[2,8,16,128]{3,2,1,0:T(8,128)S(1)}, u32[]{:S(2)}, u32[]{:S(2)}) collective-permute-start(f32[2,8,16,128]{3,2,1,0:T(8,128)S(1)} %get-tuple-element.28), channel_id=1, source_target_pairs={{0,4},{4,8},{8,12},{12,16},{16,20},{20,24},{24,28},{1,5},{5,9},{9,... | collective-permute-start | bytes 393224 | tf_op jit(solution)/shard_map/ppermute | solution.py:341
  69.3 6.9 %collective-permute-start.7 = (f32[2,8,16,128]{3,2,1,0:T(8,128)S(1)}, f32[2,8,16,128]{3,2,1,0:T(8,128)S(1)}, u32[]{:S(2)}, u32[]{:S(2)}) collective-permute-start(f32[2,8,16,128]{3,2,1,0:T(8,128)S(1)} %get-tuple-element.29), channel_id=1, source_target_pairs={{4,0},{8,4},{12,8},{16,12},{20,16},{24,20},{28,24},{5,1},{9,5},{13... | collective-permute-start | bytes 393224 | tf_op jit(solution)/shard_map/ppermute | solution.py:341

commit v10 on v9

--- a/solution.py
+++ b/solution.py
@@ -90,7 +90,19 @@
 
 
 def first_kernel(
-    geo, row0, res_ref, times_ref, amp_ref, counts_ref, aper_ref, s_ref, vals, scales, traces
+    geo,
+    row0,
+    res_ref,
+    times_ref,
+    amp_ref,
+    counts_ref,
+    old_aper_ref,
+    aper_ref,
+    s_ref,
+    vals,
+    scales,
+    traces,
+    both,
 ):
     bins_y, entries, highs, wide_y = geo
     step = pl.program_id(0)
@@ -98,13 +110,19 @@
     @pl.when(step == 0)
     def _():
         s_ref[...] = jnp.zeros_like(s_ref)
-
+        both[...] = jnp.zeros_like(both)
+
+    before = jnp.maximum(step - 1, 0) + row0
+    spread_bins(both[...], place_row(old_aper_ref[0], wide_y), s_ref, before, wide_y)
     traces[pl.ds(0, bins_y * highs), :] = res_ref[...]
     fill_weights(amp_ref[0], counts_ref[pl.ds(step + row0, 1), :], scales)
     for b in range(bins_y):
         sample_bin(traces, trace_row(b, highs), highs, times_ref, b, b, scales, vals)
-    both = split_values(vals)
-    spread_bins(both, place_row(aper_ref[0], wide_y), s_ref, step + row0, wide_y)
+    both[...] = split_values(vals)
+
+    @pl.when(step == pl.num_programs(0) - 1)
+    def _():
+        spread_bins(both[...], place_row(aper_ref[0], wide_y), s_ref, step + row0, wide_y)
 
 
 def scatter_bin(geo, row, b, image, entry_ref, times_ref, scales, work):
@@ -292,7 +310,7 @@
 
 def fold_x_kernel(mid_ref, low_ref, high_ref, grad_ref, curv_ref, out_ref, stats_ref):
     bins_x = mid_ref.shape[1]
-    sums = [jnp.zeros((1, LANES), F32) for _ in range(5)]
+    sums = [jnp.zeros(mid_ref.shape[2:], F32) for _ in range(5)]
     for x in range(bins_x):
         pair = []
         for k in range(2):
@@ -307,8 +325,9 @@
         terms = (old * old, None, pair[0] * pair[0], pair[0] * pair[1], pair[1] * pair[1])
         for n, term in enumerate(terms):
             if term is not None:
-                sums[n] = sums[n] + jnp.sum(term, axis=0, keepdims=True)
-    sums[1] = jnp.sum(curv_ref[...], axis=0, keepdims=True)
+                sums[n] = sums[n] + term
+    sums[1] = curv_ref[...]
+    sums = [jnp.sum(term, axis=0, keepdims=True) for term in sums]
     lane = lax.broadcasted_iota(jnp.int32, (1, LANES), 1)
     stats = jnp.zeros((1, LANES), F32)
     for n, term in enumerate(sums):
@@ -374,18 +393,20 @@
                 pl.BlockSpec((bins_y, entries, depths), lambda i: (i + row0, 0, 0)),
                 pl.BlockSpec((1, bins_y, entries), lambda i: (i + row0, 0, 0)),
                 pl.BlockSpec((bins_x, bins_y), lambda i: (0, 0)),
+                pl.BlockSpec((1, bins_y, entries), lambda i: (jnp.maximum(i - 1, 0) + row0, 0, 0)),
                 pl.BlockSpec((1, bins_y, entries), lambda i: (i + row0, 0, 0)),
             ],
             out_specs=pl.BlockSpec((columns, depths), lambda i: (0, 0)),
             out_shape=jax.ShapeDtypeStruct((columns, depths), F32),
             scratch_shapes=[pltpu.VMEM((bins_y * entries, depths), F32)] * 2
-            + [pltpu.VMEM((rows_per + SUB, LANES), F32)],
+            + [pltpu.VMEM((rows_per + SUB, LANES), F32)]
+            + [pltpu.VMEM((bins_y * entries, 2 * depths), BF16)],
             compiler_params=params(limit),
             cost_estimate=pl.CostEstimate(
                 flops=4 * 10**9, bytes_accessed=4 * 10**6, transcendentals=0
             ),
             name="sample_residual",
-        )(res_rows, times, amplitude, counts, aperture)
+        )(res_rows, times, amplitude, counts, aperture, aperture)
 
     early = bins_x // 4
     row0 = 2 * early

time: 93.8 us -> 92.2 us (0.983)
  Pallas kernels: 46.9 us -> 45.3 us
    pallas_call x2, Pallas kernels: 11.6 us -> 9.99 us  [first(): pl.pallas_call(functools.partial(first_kernel, geo, row0), grid=(count,),...]
  transfers between devices with their start and end apart: 8 -> 8, of which waited for: 3 -> 3; matrix products, arithmetic and copies ran while one was open for 0% -> 0% of each run, Pallas kernels for 12% -> 11%
where the time goes in v10:
time: 92.2 us; the launch traced here: 91.8 us
  Pallas kernels  45.3 us (49%)
  starting transfers between devices  21.9 us (24%)
  blocking collectives  14.8 us (16%)
  waiting for transfers between devices  8.64 us (9%)
    pallas_call x1, Pallas kernels, body(): pl.pallas_call(functools.partial(main_kernel, geo, row0), in_specs=[pl.Bl...  32.9 us
    ppermute x8, starting transfers between devices, shift(): return lax.ppermute(cells, axis, pairs)  21.9 us
    all_to_all x1, blocking collectives, body(): stats = lax.all_to_all(stats, ('gx', 'gy'), 0, 0, tiled=True)  14.8 us
    pallas_call x2, Pallas kernels, first(): pl.pallas_call(functools.partial(first_kernel, geo, row0), grid=(count,),...  9.99 us
    ppermute x8, waiting for transfers between devices, shift(): return lax.ppermute(cells, axis, pairs)  8.64 us
    pallas_call x1, Pallas kernels, body(): pl.pallas_call(last_kernel, grid=(steps,), in_specs=[pl.BlockSpec(stats.s...  2.24 us
  transfers between devices with their start and end apart: 8, of which 3 were waited for; matrix products, arithmetic and copies ran while one was open for 0% of the time, Pallas kernels for 11%

profile of v10, /device:TPU:0, one launch (start us, length us, event | category | flops | bytes accessed | tf_op | source)
XLA Modules:
  0.0 91.8 jit_solution(5919441134315750436)
XLA Ops:
  0.6 1.3 %collective-permute-start.1 = (f32[16,16,128]{2,1,0:T(8,128)}, f32[16,16,128]{2,1,0:T(8,128)S(1)}, u32[]{:S(2)}, u32[]{:S(2)}) collective-permute-start(f32[16,16,128]{2,1,0:T(8,128)} %dir_ref.1), channel_id=1, source_target_pairs={{4,0},{8,4},{12,8},{16,12},{20,16},{24,20},{28,24},{5,1},{9,5},{13... | collective-permute-start | bytes 393224 | tf_op jit(solution)/shard_map/ppermute | solution.py:360
  1.9 5.5 %collective-permute-start = (f32[16,16,128]{2,1,0:T(8,128)}, f32[16,16,128]{2,1,0:T(8,128)S(1)}, u32[]{:S(2)}, u32[]{:S(2)}) collective-permute-start(f32[16,16,128]{2,1,0:T(8,128)} %dir_ref.1), channel_id=1, source_target_pairs={{0,4},{4,8},{8,12},{12,16},{16,20},{20,24},{24,28},{1,5},{5,9},{9,... | collective-permute-start | bytes 393224 | tf_op jit(solution)/shard_map/ppermute | solution.py:360
  7.4 0.0 copy-start.4
  7.4 0.0 copy-start.1
  7.4 0.0 copy-start
  7.4 0.0 copy-start.6
  7.5 0.0 copy-start.7
  7.5 6.0 %sample_residual.2.s1_in_ref = f32[1024,128]{1,0:T(8,128)} custom-call(f32[4096,128]{1,0:T(8,128)} %bitcast.11, s32[256,16,128]{2,1,0:T(8,128)} %bitcast.15, f32[16,16,16]{2,1,0:T(8,128)} %amp_ref.5, s32[16,16]{1,0:T(8,128)} %counts_ref.4, s32[16,16,16]{2,1,0:T(8,128)} %aper_ref.5, s32[16,16,16]{2,1,0:T(8,128)} %aper_ref.5), custom_call_target="tpu_custom_call" | custom-call | flops 4000000000 | bytes 4000000 | tf_op jit(solution)/shard_map/sample_residual/pallas_call | solution.py:388
  13.5 0.0 copy-done.4
  13.5 0.1 reshape.25.parts_ref
  13.6 0.0 collective-permute-done.1
  13.6 0.0 collective-permute-done
  13.6 0.0 copy-done.1
  13.7 0.0 copy-start.5
  13.7 0.0 copy-start.8
  13.7 1.6 %collective-permute-start.2 = (f32[32,8,128]{2,1,0:T(8,128)S(1)}, f32[32,8,128]{2,1,0:T(8,128)S(1)}, u32[]{:S(2)}, u32[]{:S(2)}) collective-permute-start(f32[32,8,128]{2,1,0:T(8,128)S(1)} %get-tuple-element.20), channel_id=1, source_target_pairs={{0,1},{1,2},{2,3},{4,5},{5,6},{6,7},{8,9},{9,10},{10,11},{12,13},{... | collective-permute-start | bytes 393224 | tf_op jit(solution)/shard_map/ppermute | solution.py:360
  15.3 1.3 %collective-permute-start.3 = (f32[32,8,128]{2,1,0:T(8,128)S(1)}, f32[32,8,128]{2,1,0:T(8,128)S(1)}, u32[]{:S(2)}, u32[]{:S(2)}) collective-permute-start(f32[32,8,128]{2,1,0:T(8,128)S(1)} %get-tuple-element.21), channel_id=1, source_target_pairs={{1,0},{2,1},{3,2},{5,4},{6,5},{7,6},{9,8},{10,9},{11,10},{13,12},{... | collective-permute-start | bytes 393224 | tf_op jit(solution)/shard_map/ppermute | solution.py:360
  16.6 0.0 copy-done
  16.6 0.0 copy-done.6
  16.6 0.0 copy-done.7
  16.6 4.0 %sample_residual.3.s1_more_ref = f32[1024,128]{1,0:T(8,128)S(1)} custom-call(f32[4096,128]{1,0:T(8,128)S(1)} %bitcast.12, s32[256,16,128]{2,1,0:T(8,128)} %bitcast.16, f32[16,16,16]{2,1,0:T(8,128)S(1)} %copy-done.7, s32[16,16]{1,0:T(8,128)S(1)} %copy-done.4, s32[16,16,16]{2,1,0:T(8,128)S(1)} %copy-done.6, s32[16,16,16]{2,1,0:T(8,128)S(1)} %copy-done.6), custom_call_target="tpu_custom_call" | custom-call | flops 4000000000 | bytes 4000000 | tf_op jit(solution)/shard_map/sample_residual/pallas_call | solution.py:388
  20.6 0.0 copy-start.3
  20.6 0.0 copy-start.2
  20.6 0.0 collective-permute-done.2.left_ref
  20.6 0.0 collective-permute-done.3.right_ref
  20.6 0.0 copy-done.5
  20.6 0.0 copy-done.8
  20.7 32.9 %demigrate_and_sample.1 = (f32[4096,128]{1,0:T(8,128)S(1)}, f32[16,128]{1,0:T(8,128)S(1)}, f32[2,32,8,128]{3,2,1,0:T(8,128)S(1)}, f32[2,32,16,128]{3,2,1,0:T(8,128)S(1)}, f32[2,32,8,128]{3,2,1,0:T(8,128)S(1)}) custom-call(s32[16,16,16]{2,1,0:T(8,128)S(1)} %copy-done.6, s32[256,16,128]{2,1,0:T(8,128)S(1)} %bitcast.17, f32[16,16,16]{2,1,0:T(8,128)S(1)} %copy-done.7, ...), custom_call_target="tpu_custom_call" | custom-call | flops 20000000000 | bytes 8000000 | tf_op jit(solution)/shard_map/demigrate_and_sample/pallas_call | solution.py:430
  53.5 5.4 %collective-permute-start.4 = (f32[2,32,8,128]{3,2,1,0:T(8,128)S(1)}, f32[2,32,8,128]{3,2,1,0:T(8,128)S(1)}, u32[]{:S(2)}, u32[]{:S(2)}) collective-permute-start(f32[2,32,8,128]{3,2,1,0:T(8,128)S(1)} %get-tuple-element.25), channel_id=1, source_target_pairs={{0,1},{1,2},{2,3},{4,5},{5,6},{6,7},{8,9},{9,10},{10,11},{12,13},{... | collective-permute-start | bytes 786440 | tf_op jit(solution)/shard_map/ppermute | solution.py:360
  59.0 1.3 %collective-permute-start.5 = (f32[2,32,8,128]{3,2,1,0:T(8,128)S(1)}, f32[2,32,8,128]{3,2,1,0:T(8,128)S(1)}, u32[]{:S(2)}, u32[]{:S(2)}) collective-permute-start(f32[2,32,8,128]{3,2,1,0:T(8,128)S(1)} %get-tuple-element.26), channel_id=1, source_target_pairs={{1,0},{2,1},{3,2},{5,4},{6,5},{7,6},{9,8},{10,9},{11,10},{13,12},{... | collective-permute-start | bytes 786440 | tf_op jit(solution)/shard_map/ppermute | solution.py:360
  60.3 0.0 collective-permute-done.4.low_ref
  60.3 3.1 %collective-permute-done.5.high_ref = f32[2,32,8,128]{3,2,1,0:T(8,128)S(1)} collective-permute-done((f32[2,32,8,128]{3,2,1,0:T(8,128)S(1)}, f32[2,32,8,128]{3,2,1,0:T(8,128)S(1)}, u32[]{:S(2)}, u32[]{:S(2)}) %collective-permute-start.5) | collective-permute-done | bytes 262176 | tf_op jit(solution)/shard_map/ppermute | solution.py:360
  63.3 0.1 fold_y.1
  63.4 4.3 %collective-permute-start.6 = (f32[2,8,16,128]{3,2,1,0:T(8,128)S(1)}, f32[2,8,16,128]{3,2,1,0:T(8,128)S(1)}, u32[]{:S(2)}, u32[]{:S(2)}) collective-permute-start(f32[2,8,16,128]{3,2,1,0:T(8,128)S(1)} %get-tuple-element.28), channel_id=1, source_target_pairs={{0,4},{4,8},{8,12},{12,16},{16,20},{20,24},{24,28},{1,5},{5,9},{9,... | collective-permute-start | bytes 393224 | tf_op jit(solution)/shard_map/ppermute | solution.py:360
  67.7 1.3 %collective-permute-start.7 = (f32[2,8,16,128]{3,2,1,0:T(8,128)S(1)}, f32[2,8,16,128]{3,2,1,0:T(8,128)S(1)}, u32[]{:S(2)}, u32[]{:S(2)}) collective-permute-start(f32[2,8,16,128]{3,2,1,0:T(8,128)S(1)} %get-tuple-element.29), channel_id=1, source_target_pairs={{4,0},{8,4},{12,8},{16,12},{20,16},{24,20},{28,24},{5,1},{9,5},{13... | collective-permute-start | bytes 393224 | tf_op jit(solution)/shard_map/ppermute | solution.py:360
  69.0 1.2 %collective-permute-done.6.low_ref = f32[2,8,16,128]{3,2,1,0:T(8,128)S(1)} collective-permute-done((f32[2,8,16,128]{3,2,1,0:T(8,128)S(1)}, f32[2,8,16,128]{3,2,1,0:T(8,128)S(1)}, u32[]{:S(2)}, u32[]{:S(2)}) %collective-permute-start.6) | collective-permute-done | bytes 131104 | tf_op jit(solution)/shard_map/ppermute | solution.py:360
  70.2 4.4 %collective-permute-done.7.high_ref = f32[2,8,16,128]{3,2,1,0:T(8,128)S(1)} collective-permute-done((f32[2,8,16,128]{3,2,1,0:T(8,128)S(1)}, f32[2,8,16,128]{3,2,1,0:T(8,128)S(1)}, u32[]{:S(2)}, u32[]{:S(2)}) %collective-permute-start.7) | collective-permute-done | bytes 131104 | tf_op jit(solution)/shard_map/ppermute | solution.py:360
  74.6 0.0 copy-done.3
  74.6 0.1 fold_x.1
  74.7 14.8 %all_to_all.5.stats_ref = f32[32,1,128]{2,1,0:T(1,128)S(1)} all-to-all(f32[32,1,128]{2,1,0:T(1,128)S(1)} %get-tuple-element.31), channel_id=1, replica_groups=mesh['gx'=8,'gy'=4] {'gx','gy'}, dimensions={0} | all-to-all | bytes 32768 | tf_op jit(solution)/shard_map/all_to_all | solution.py:489
  89.5 0.0 copy-done.2
  89.5 2.2 %update.1 = (f32[16,16,128]{2,1,0:T(8,128)}, f32[4096,128]{1,0:T(8,128)}, f32[16,16,128]{2,1,0:T(8,128)}) custom-call(f32[32,1,128]{2,1,0:T(1,128)S(1)} %all_to_all.5.stats_ref, f32[4096,128]{1,0:T(8,128)S(1)} %bitcast.14, f32[4096,128]{1,0:T(8,128)S(1)} %get-tuple-element.32.data_ref, f32[16,16,128]{2,1,0:T(8,128)S(1)} %copy-done.2, ...), custom_call_target="tpu_custom_call" | custom-call | tf_op jit(solution)/shard_map/update/pallas_call | solution.py:497
  (4 shorter events, 0.1 us)
Async XLA Ops:
  0.6 12.9 %collective-permute-start.1 = (f32[16,16,128]{2,1,0:T(8,128)}, f32[16,16,128]{2,1,0:T(8,128)S(1)}, u32[]{:S(2)}, u32[]{:S(2)}) collective-permute-start(f32[16,16,128]{2,1,0:T(8,128)} %dir_ref.1), channel_id=1, source_target_pairs={{4,0},{8,4},{12,8},{16,12},{20,16},{24,20},{28,24},{5,1},{9,5},{13... | collective-permute-start | bytes 393224 | tf_op jit(solution)/shard_map/ppermute | solution.py:360
  1.9 11.6 %collective-permute-start = (f32[16,16,128]{2,1,0:T(8,128)}, f32[16,16,128]{2,1,0:T(8,128)S(1)}, u32[]{:S(2)}, u32[]{:S(2)}) collective-permute-start(f32[16,16,128]{2,1,0:T(8,128)} %dir_ref.1), channel_id=1, source_target_pairs={{0,4},{4,8},{8,12},{12,16},{16,20},{20,24},{24,28},{1,5},{5,9},{9,... | collective-permute-start | bytes 393224 | tf_op jit(solution)/shard_map/ppermute | solution.py:360
  7.4 6.1 %copy-start.4 = (s32[16,16]{1,0:T(8,128)S(1)}, s32[16,16]{1,0:T(8,128)}, u32[]{:S(2)}) copy-start(s32[16,16]{1,0:T(8,128)} %counts_ref.4) | copy-start | bytes 3076
  7.4 6.2 %copy-start.1 = (f32[16,16,128]{2,1,0:T(8,128)S(1)}, f32[16,16,128]{2,1,0:T(8,128)}, u32[]{:S(2)}) copy-start(f32[16,16,128]{2,1,0:T(8,128)} %dir_ref.1) | copy-start | bytes 393220
  7.4 9.1 %copy-start = (f32[16,16,2048]{2,1,0:T(8,128)S(1)}, f32[16,16,2048]{2,1,0:T(8,128)}, u32[]{:S(2)}) copy-start(f32[16,16,2048]{2,1,0:T(8,128)} %param.9) | copy-start | bytes 6291460
  7.4 9.1 %copy-start.6 = (s32[16,16,16]{2,1,0:T(8,128)S(1)}, s32[16,16,16]{2,1,0:T(8,128)}, u32[]{:S(2)}) copy-start(s32[16,16,16]{2,1,0:T(8,128)} %aper_ref.5) | copy-start | bytes 49156
  7.5 9.1 %copy-start.7 = (f32[16,16,16]{2,1,0:T(8,128)S(1)}, f32[16,16,16]{2,1,0:T(8,128)}, u32[]{:S(2)}) copy-start(f32[16,16,16]{2,1,0:T(8,128)} %amp_ref.5) | copy-start | bytes 49156
  13.7 7.0 %copy-start.5 = (s32[16,16,16,128]{3,2,1,0:T(8,128)S(1)}, s32[16,16,16,128]{3,2,1,0:T(8,128)}, u32[]{:S(2)}) copy-start(s32[16,16,16,128]{3,2,1,0:T(8,128)} %param.13) | copy-start | bytes 6291460
  13.7 7.0 %copy-start.8 = (f32[1024,128]{1,0:T(8,128)S(1)}, f32[1024,128]{1,0:T(8,128)}, u32[]{:S(2)}) copy-start(f32[1024,128]{1,0:T(8,128)} %sample_residual.2.s1_in_ref) | copy-start | bytes 1572868
  13.7 6.9 %collective-permute-start.2 = (f32[32,8,128]{2,1,0:T(8,128)S(1)}, f32[32,8,128]{2,1,0:T(8,128)S(1)}, u32[]{:S(2)}, u32[]{:S(2)}) collective-permute-start(f32[32,8,128]{2,1,0:T(8,128)S(1)} %get-tuple-element.20), channel_id=1, source_target_pairs={{0,1},{1,2},{2,3},{4,5},{5,6},{6,7},{8,9},{9,10},{10,11},{12,13},{... | collective-permute-start | bytes 393224 | tf_op jit(solution)/shard_map/ppermute | solution.py:360
  15.3 5.3 %collective-permute-start.3 = (f32[32,8,128]{2,1,0:T(8,128)S(1)}, f32[32,8,128]{2,1,0:T(8,128)S(1)}, u32[]{:S(2)}, u32[]{:S(2)}) collective-permute-start(f32[32,8,128]{2,1,0:T(8,128)S(1)} %get-tuple-element.21), channel_id=1, source_target_pairs={{1,0},{2,1},{3,2},{5,4},{6,5},{7,6},{9,8},{10,9},{11,10},{13,12},{... | collective-permute-start | bytes 393224 | tf_op jit(solution)/shard_map/ppermute | solution.py:360
  20.6 54.0 %copy-start.3 = (f32[16,16,128]{2,1,0:T(8,128)S(1)}, f32[16,16,128]{2,1,0:T(8,128)}, u32[]{:S(2)}) copy-start(f32[16,16,128]{2,1,0:T(8,128)} %grad_ref.1) | copy-start | bytes 393220
  20.6 68.9 %copy-start.2 = (f32[16,16,128]{2,1,0:T(8,128)S(1)}, f32[16,16,128]{2,1,0:T(8,128)}, u32[]{:S(2)}) copy-start(f32[16,16,128]{2,1,0:T(8,128)} %model_ref.1) | copy-start | bytes 393220
  53.5 6.7 %collective-permute-start.4 = (f32[2,32,8,128]{3,2,1,0:T(8,128)S(1)}, f32[2,32,8,128]{3,2,1,0:T(8,128)S(1)}, u32[]{:S(2)}, u32[]{:S(2)}) collective-permute-start(f32[2,32,8,128]{3,2,1,0:T(8,128)S(1)} %get-tuple-element.25), channel_id=1, source_target_pairs={{0,1},{1,2},{2,3},{4,5},{5,6},{6,7},{8,9},{9,10},{10,11},{12,13},{... | collective-permute-start | bytes 786440 | tf_op jit(solution)/shard_map/ppermute | solution.py:360
  59.0 4.4 %collective-permute-start.5 = (f32[2,32,8,128]{3,2,1,0:T(8,128)S(1)}, f32[2,32,8,128]{3,2,1,0:T(8,128)S(1)}, u32[]{:S(2)}, u32[]{:S(2)}) collective-permute-start(f32[2,32,8,128]{3,2,1,0:T(8,128)S(1)} %get-tuple-element.26), channel_id=1, source_target_pairs={{1,0},{2,1},{3,2},{5,4},{6,5},{7,6},{9,8},{10,9},{11,10},{13,12},{... | collective-permute-start | bytes 786440 | tf_op jit(solution)/shard_map/ppermute | solution.py:360
  63.4 6.8 %collective-permute-start.6 = (f32[2,8,16,128]{3,2,1,0:T(8,128)S(1)}, f32[2,8,16,128]{3,2,1,0:T(8,128)S(1)}, u32[]{:S(2)}, u32[]{:S(2)}) collective-permute-start(f32[2,8,16,128]{3,2,1,0:T(8,128)S(1)} %get-tuple-element.28), channel_id=1, source_target_pairs={{0,4},{4,8},{8,12},{12,16},{16,20},{20,24},{24,28},{1,5},{5,9},{9,... | collective-permute-start | bytes 393224 | tf_op jit(solution)/shard_map/ppermute | solution.py:360
  67.7 6.9 %collective-permute-start.7 = (f32[2,8,16,128]{3,2,1,0:T(8,128)S(1)}, f32[2,8,16,128]{3,2,1,0:T(8,128)S(1)}, u32[]{:S(2)}, u32[]{:S(2)}) collective-permute-start(f32[2,8,16,128]{3,2,1,0:T(8,128)S(1)} %get-tuple-element.29), channel_id=1, source_target_pairs={{4,0},{8,4},{12,8},{16,12},{20,16},{24,20},{28,24},{5,1},{9,5},{13... | collective-permute-start | bytes 393224 | tf_op jit(solution)/shard_map/ppermute | solution.py:360

commit v11 on v10

--- a/solution.py
+++ b/solution.py
@@ -444,7 +444,7 @@
         + [pltpu.VMEM((bins_y * entries, 2 * depths), BF16)]
         + [pltpu.VMEM((res_bins * entries, 2 * depths), BF16)]
         + [pltpu.VMEM((res_bins * highs + SUB, LANES), F32)]
-        + [pltpu.VMEM((4, entries + SUB, LANES), F32)] * 8,
+        + [pltpu.VMEM((4, entries + SUB, LANES), F32)] * bins_y,
         compiler_params=params(MAIN_LIMIT),
         cost_estimate=pl.CostEstimate(
             flops=20 * 10**9, bytes_accessed=8 * 10**6, transcendentals=0
@@ -488,7 +488,7 @@
     )(inner, from_low, from_high, old_gradient, curv)
     stats = lax.all_to_all(stats, ("gx", "gy"), 0, 0, tiled=True)
 
-    steps = 4
+    steps = 2
     rows_step = bins_x * rows_per // steps
     x_step = bins_x // steps
     cells = pl.BlockSpec((x_step, bins_y, depths), lambda i: (i, 0, 0))

time: 92.2 us -> 94.8 us (1.028)
  Pallas kernels: 45.3 us -> 47.9 us
    pallas_call x1, Pallas kernels: 32.9 us -> 36.1 us  [body(): pl.pallas_call(functools.partial(main_kernel, geo, row0), in_specs=[pl.Bl...]
where the time goes in v11:
time: 94.8 us; the launch traced here: 94.4 us
  Pallas kernels  47.9 us (51%)
  starting transfers between devices  22 us (23%)
  blocking collectives  14.8 us (16%)
  waiting for transfers between devices  8.64 us (9%)
    pallas_call x1, Pallas kernels, body(): pl.pallas_call(functools.partial(main_kernel, geo, row0), in_specs=[pl.Bl...  36.1 us
    ppermute x8, starting transfers between devices, shift(): return lax.ppermute(cells, axis, pairs)  22 us
    all_to_all x1, blocking collectives, body(): stats = lax.all_to_all(stats, ('gx', 'gy'), 0, 0, tiled=True)  14.8 us
    pallas_call x2, Pallas kernels, first(): pl.pallas_call(functools.partial(first_kernel, geo, row0), grid=(count,),...  9.99 us
    ppermute x8, waiting for transfers between devices, shift(): return lax.ppermute(cells, axis, pairs)  8.64 us
  transfers between devices with their start and end apart: 8, of which 3 were waited for; matrix products, arithmetic and copies ran while one was open for 0% of the time, Pallas kernels for 11%

profile of v11, /device:TPU:0, one launch (start us, length us, event | category | flops | bytes accessed | tf_op | source)
XLA Modules:
  0.0 94.4 jit_solution(493479918629206051)
XLA Ops:
  0.6 1.3 %collective-permute-start.1 = (f32[16,16,128]{2,1,0:T(8,128)}, f32[16,16,128]{2,1,0:T(8,128)S(1)}, u32[]{:S(2)}, u32[]{:S(2)}) collective-permute-start(f32[16,16,128]{2,1,0:T(8,128)} %dir_ref.1), channel_id=1, source_target_pairs={{4,0},{8,4},{12,8},{16,12},{20,16},{24,20},{28,24},{5,1},{9,5},{13... | collective-permute-start | bytes 393224 | tf_op jit(solution)/shard_map/ppermute | solution.py:360
  1.9 5.5 %collective-permute-start = (f32[16,16,128]{2,1,0:T(8,128)}, f32[16,16,128]{2,1,0:T(8,128)S(1)}, u32[]{:S(2)}, u32[]{:S(2)}) collective-permute-start(f32[16,16,128]{2,1,0:T(8,128)} %dir_ref.1), channel_id=1, source_target_pairs={{0,4},{4,8},{8,12},{12,16},{16,20},{20,24},{24,28},{1,5},{5,9},{9,... | collective-permute-start | bytes 393224 | tf_op jit(solution)/shard_map/ppermute | solution.py:360
  7.4 0.0 copy-start.4
  7.4 0.0 copy-start.1
  7.4 0.0 copy-start
  7.4 0.0 copy-start.6
  7.5 0.0 copy-start.7
  7.5 6.0 %sample_residual.2.s1_in_ref = f32[1024,128]{1,0:T(8,128)} custom-call(f32[4096,128]{1,0:T(8,128)} %bitcast.11, s32[256,16,128]{2,1,0:T(8,128)} %bitcast.15, f32[16,16,16]{2,1,0:T(8,128)} %amp_ref.5, s32[16,16]{1,0:T(8,128)} %counts_ref.4, s32[16,16,16]{2,1,0:T(8,128)} %aper_ref.5, s32[16,16,16]{2,1,0:T(8,128)} %aper_ref.5), custom_call_target="tpu_custom_call" | custom-call | flops 4000000000 | bytes 4000000 | tf_op jit(solution)/shard_map/sample_residual/pallas_call | solution.py:388
  13.5 0.0 copy-done.4
  13.5 0.1 reshape.25.parts_ref
  13.6 0.0 collective-permute-done.1
  13.6 0.0 collective-permute-done
  13.6 0.0 copy-done.1
  13.7 0.0 copy-start.5
  13.7 0.0 copy-start.8
  13.7 1.6 %collective-permute-start.2 = (f32[32,8,128]{2,1,0:T(8,128)S(1)}, f32[32,8,128]{2,1,0:T(8,128)S(1)}, u32[]{:S(2)}, u32[]{:S(2)}) collective-permute-start(f32[32,8,128]{2,1,0:T(8,128)S(1)} %get-tuple-element.20), channel_id=1, source_target_pairs={{0,1},{1,2},{2,3},{4,5},{5,6},{6,7},{8,9},{9,10},{10,11},{12,13},{... | collective-permute-start | bytes 393224 | tf_op jit(solution)/shard_map/ppermute | solution.py:360
  15.3 1.3 %collective-permute-start.3 = (f32[32,8,128]{2,1,0:T(8,128)S(1)}, f32[32,8,128]{2,1,0:T(8,128)S(1)}, u32[]{:S(2)}, u32[]{:S(2)}) collective-permute-start(f32[32,8,128]{2,1,0:T(8,128)S(1)} %get-tuple-element.21), channel_id=1, source_target_pairs={{1,0},{2,1},{3,2},{5,4},{6,5},{7,6},{9,8},{10,9},{11,10},{13,12},{... | collective-permute-start | bytes 393224 | tf_op jit(solution)/shard_map/ppermute | solution.py:360
  16.6 0.0 copy-done
  16.6 0.0 copy-done.6
  16.6 0.0 copy-done.7
  16.6 4.0 %sample_residual.3.s1_more_ref = f32[1024,128]{1,0:T(8,128)S(1)} custom-call(f32[4096,128]{1,0:T(8,128)S(1)} %bitcast.12, s32[256,16,128]{2,1,0:T(8,128)} %bitcast.16, f32[16,16,16]{2,1,0:T(8,128)S(1)} %copy-done.7, s32[16,16]{1,0:T(8,128)S(1)} %copy-done.4, s32[16,16,16]{2,1,0:T(8,128)S(1)} %copy-done.6, s32[16,16,16]{2,1,0:T(8,128)S(1)} %copy-done.6), custom_call_target="tpu_custom_call" | custom-call | flops 4000000000 | bytes 4000000 | tf_op jit(solution)/shard_map/sample_residual/pallas_call | solution.py:388
  20.6 0.0 copy-start.3
  20.6 0.0 copy-start.2
  20.6 0.0 collective-permute-done.2.left_ref
  20.6 0.0 collective-permute-done.3.right_ref
  20.6 0.0 copy-done.5
  20.6 0.0 copy-done.8
  20.7 36.1 %demigrate_and_sample.1 = (f32[4096,128]{1,0:T(8,128)S(1)}, f32[16,128]{1,0:T(8,128)S(1)}, f32[2,32,8,128]{3,2,1,0:T(8,128)S(1)}, f32[2,32,16,128]{3,2,1,0:T(8,128)S(1)}, f32[2,32,8,128]{3,2,1,0:T(8,128)S(1)}) custom-call(s32[16,16,16]{2,1,0:T(8,128)S(1)} %copy-done.6, s32[256,16,128]{2,1,0:T(8,128)S(1)} %bitcast.17, f32[16,16,16]{2,1,0:T(8,128)S(1)} %copy-done.7, ...), custom_call_target="tpu_custom_call" | custom-call | flops 20000000000 | bytes 8000000 | tf_op jit(solution)/shard_map/demigrate_and_sample/pallas_call | solution.py:430
  56.7 5.5 %collective-permute-start.4 = (f32[2,32,8,128]{3,2,1,0:T(8,128)S(1)}, f32[2,32,8,128]{3,2,1,0:T(8,128)S(1)}, u32[]{:S(2)}, u32[]{:S(2)}) collective-permute-start(f32[2,32,8,128]{3,2,1,0:T(8,128)S(1)} %get-tuple-element.25), channel_id=1, source_target_pairs={{0,1},{1,2},{2,3},{4,5},{5,6},{6,7},{8,9},{9,10},{10,11},{12,13},{... | collective-permute-start | bytes 786440 | tf_op jit(solution)/shard_map/ppermute | solution.py:360
  62.2 1.3 %collective-permute-start.5 = (f32[2,32,8,128]{3,2,1,0:T(8,128)S(1)}, f32[2,32,8,128]{3,2,1,0:T(8,128)S(1)}, u32[]{:S(2)}, u32[]{:S(2)}) collective-permute-start(f32[2,32,8,128]{3,2,1,0:T(8,128)S(1)} %get-tuple-element.26), channel_id=1, source_target_pairs={{1,0},{2,1},{3,2},{5,4},{6,5},{7,6},{9,8},{10,9},{11,10},{13,12},{... | collective-permute-start | bytes 786440 | tf_op jit(solution)/shard_map/ppermute | solution.py:360
  63.5 0.0 collective-permute-done.4.low_ref
  63.5 3.1 %collective-permute-done.5.high_ref = f32[2,32,8,128]{3,2,1,0:T(8,128)S(1)} collective-permute-done((f32[2,32,8,128]{3,2,1,0:T(8,128)S(1)}, f32[2,32,8,128]{3,2,1,0:T(8,128)S(1)}, u32[]{:S(2)}, u32[]{:S(2)}) %collective-permute-start.5) | collective-permute-done | bytes 262176 | tf_op jit(solution)/shard_map/ppermute | solution.py:360
  66.5 0.1 fold_y.1
  66.6 4.3 %collective-permute-start.6 = (f32[2,8,16,128]{3,2,1,0:T(8,128)S(1)}, f32[2,8,16,128]{3,2,1,0:T(8,128)S(1)}, u32[]{:S(2)}, u32[]{:S(2)}) collective-permute-start(f32[2,8,16,128]{3,2,1,0:T(8,128)S(1)} %get-tuple-element.28), channel_id=1, source_target_pairs={{0,4},{4,8},{8,12},{12,16},{16,20},{20,24},{24,28},{1,5},{5,9},{9,... | collective-permute-start | bytes 393224 | tf_op jit(solution)/shard_map/ppermute | solution.py:360
  70.9 1.3 %collective-permute-start.7 = (f32[2,8,16,128]{3,2,1,0:T(8,128)S(1)}, f32[2,8,16,128]{3,2,1,0:T(8,128)S(1)}, u32[]{:S(2)}, u32[]{:S(2)}) collective-permute-start(f32[2,8,16,128]{3,2,1,0:T(8,128)S(1)} %get-tuple-element.29), channel_id=1, source_target_pairs={{4,0},{8,4},{12,8},{16,12},{20,16},{24,20},{28,24},{5,1},{9,5},{13... | collective-permute-start | bytes 393224 | tf_op jit(solution)/shard_map/ppermute | solution.py:360
  72.2 1.2 %collective-permute-done.6.low_ref = f32[2,8,16,128]{3,2,1,0:T(8,128)S(1)} collective-permute-done((f32[2,8,16,128]{3,2,1,0:T(8,128)S(1)}, f32[2,8,16,128]{3,2,1,0:T(8,128)S(1)}, u32[]{:S(2)}, u32[]{:S(2)}) %collective-permute-start.6) | collective-permute-done | bytes 131104 | tf_op jit(solution)/shard_map/ppermute | solution.py:360
  73.4 4.4 %collective-permute-done.7.high_ref = f32[2,8,16,128]{3,2,1,0:T(8,128)S(1)} collective-permute-done((f32[2,8,16,128]{3,2,1,0:T(8,128)S(1)}, f32[2,8,16,128]{3,2,1,0:T(8,128)S(1)}, u32[]{:S(2)}, u32[]{:S(2)}) %collective-permute-start.7) | collective-permute-done | bytes 131104 | tf_op jit(solution)/shard_map/ppermute | solution.py:360
  77.8 0.0 copy-done.3
  77.8 0.1 fold_x.1
  77.9 14.8 %all_to_all.5.stats_ref = f32[32,1,128]{2,1,0:T(1,128)S(1)} all-to-all(f32[32,1,128]{2,1,0:T(1,128)S(1)} %get-tuple-element.31), channel_id=1, replica_groups=mesh['gx'=8,'gy'=4] {'gx','gy'}, dimensions={0} | all-to-all | bytes 32768 | tf_op jit(solution)/shard_map/all_to_all | solution.py:489
  92.7 0.0 copy-done.2
  92.7 1.7 %update.1 = (f32[16,16,128]{2,1,0:T(8,128)}, f32[4096,128]{1,0:T(8,128)}, f32[16,16,128]{2,1,0:T(8,128)}) custom-call(f32[32,1,128]{2,1,0:T(1,128)S(1)} %all_to_all.5.stats_ref, f32[4096,128]{1,0:T(8,128)S(1)} %bitcast.14, f32[4096,128]{1,0:T(8,128)S(1)} %get-tuple-element.32.data_ref, f32[16,16,128]{2,1,0:T(8,128)S(1)} %copy-done.2, ...), custom_call_target="tpu_custom_call" | custom-call | tf_op jit(solution)/shard_map/update/pallas_call | solution.py:497
  (4 shorter events, 0.1 us)
Async XLA Ops:
  0.6 12.9 %collective-permute-start.1 = (f32[16,16,128]{2,1,0:T(8,128)}, f32[16,16,128]{2,1,0:T(8,128)S(1)}, u32[]{:S(2)}, u32[]{:S(2)}) collective-permute-start(f32[16,16,128]{2,1,0:T(8,128)} %dir_ref.1), channel_id=1, source_target_pairs={{4,0},{8,4},{12,8},{16,12},{20,16},{24,20},{28,24},{5,1},{9,5},{13... | collective-permute-start | bytes 393224 | tf_op jit(solution)/shard_map/ppermute | solution.py:360
  1.9 11.6 %collective-permute-start = (f32[16,16,128]{2,1,0:T(8,128)}, f32[16,16,128]{2,1,0:T(8,128)S(1)}, u32[]{:S(2)}, u32[]{:S(2)}) collective-permute-start(f32[16,16,128]{2,1,0:T(8,128)} %dir_ref.1), channel_id=1, source_target_pairs={{0,4},{4,8},{8,12},{12,16},{16,20},{20,24},{24,28},{1,5},{5,9},{9,... | collective-permute-start | bytes 393224 | tf_op jit(solution)/shard_map/ppermute | solution.py:360
  7.4 6.1 %copy-start.4 = (s32[16,16]{1,0:T(8,128)S(1)}, s32[16,16]{1,0:T(8,128)}, u32[]{:S(2)}) copy-start(s32[16,16]{1,0:T(8,128)} %counts_ref.4) | copy-start | bytes 3076
  7.4 6.2 %copy-start.1 = (f32[16,16,128]{2,1,0:T(8,128)S(1)}, f32[16,16,128]{2,1,0:T(8,128)}, u32[]{:S(2)}) copy-start(f32[16,16,128]{2,1,0:T(8,128)} %dir_ref.1) | copy-start | bytes 393220
  7.4 9.1 %copy-start = (f32[16,16,2048]{2,1,0:T(8,128)S(1)}, f32[16,16,2048]{2,1,0:T(8,128)}, u32[]{:S(2)}) copy-start(f32[16,16,2048]{2,1,0:T(8,128)} %param.9) | copy-start | bytes 6291460
  7.4 9.1 %copy-start.6 = (s32[16,16,16]{2,1,0:T(8,128)S(1)}, s32[16,16,16]{2,1,0:T(8,128)}, u32[]{:S(2)}) copy-start(s32[16,16,16]{2,1,0:T(8,128)} %aper_ref.5) | copy-start | bytes 49156
  7.5 9.1 %copy-start.7 = (f32[16,16,16]{2,1,0:T(8,128)S(1)}, f32[16,16,16]{2,1,0:T(8,128)}, u32[]{:S(2)}) copy-start(f32[16,16,16]{2,1,0:T(8,128)} %amp_ref.5) | copy-start | bytes 49156
  13.7 7.0 %copy-start.5 = (s32[16,16,16,128]{3,2,1,0:T(8,128)S(1)}, s32[16,16,16,128]{3,2,1,0:T(8,128)}, u32[]{:S(2)}) copy-start(s32[16,16,16,128]{3,2,1,0:T(8,128)} %param.13) | copy-start | bytes 6291460
  13.7 7.0 %copy-start.8 = (f32[1024,128]{1,0:T(8,128)S(1)}, f32[1024,128]{1,0:T(8,128)}, u32[]{:S(2)}) copy-start(f32[1024,128]{1,0:T(8,128)} %sample_residual.2.s1_in_ref) | copy-start | bytes 1572868
  13.7 6.9 %collective-permute-start.2 = (f32[32,8,128]{2,1,0:T(8,128)S(1)}, f32[32,8,128]{2,1,0:T(8,128)S(1)}, u32[]{:S(2)}, u32[]{:S(2)}) collective-permute-start(f32[32,8,128]{2,1,0:T(8,128)S(1)} %get-tuple-element.20), channel_id=1, source_target_pairs={{0,1},{1,2},{2,3},{4,5},{5,6},{6,7},{8,9},{9,10},{10,11},{12,13},{... | collective-permute-start | bytes 393224 | tf_op jit(solution)/shard_map/ppermute | solution.py:360
  15.3 5.3 %collective-permute-start.3 = (f32[32,8,128]{2,1,0:T(8,128)S(1)}, f32[32,8,128]{2,1,0:T(8,128)S(1)}, u32[]{:S(2)}, u32[]{:S(2)}) collective-permute-start(f32[32,8,128]{2,1,0:T(8,128)S(1)} %get-tuple-element.21), channel_id=1, source_target_pairs={{1,0},{2,1},{3,2},{5,4},{6,5},{7,6},{9,8},{10,9},{11,10},{13,12},{... | collective-permute-start | bytes 393224 | tf_op jit(solution)/shard_map/ppermute | solution.py:360
  20.6 57.2 %copy-start.3 = (f32[16,16,128]{2,1,0:T(8,128)S(1)}, f32[16,16,128]{2,1,0:T(8,128)}, u32[]{:S(2)}) copy-start(f32[16,16,128]{2,1,0:T(8,128)} %grad_ref.1) | copy-start | bytes 393220
  20.6 72.1 %copy-start.2 = (f32[16,16,128]{2,1,0:T(8,128)S(1)}, f32[16,16,128]{2,1,0:T(8,128)}, u32[]{:S(2)}) copy-start(f32[16,16,128]{2,1,0:T(8,128)} %model_ref.1) | copy-start | bytes 393220
  56.7 6.8 %collective-permute-start.4 = (f32[2,32,8,128]{3,2,1,0:T(8,128)S(1)}, f32[2,32,8,128]{3,2,1,0:T(8,128)S(1)}, u32[]{:S(2)}, u32[]{:S(2)}) collective-permute-start(f32[2,32,8,128]{3,2,1,0:T(8,128)S(1)} %get-tuple-element.25), channel_id=1, source_target_pairs={{0,1},{1,2},{2,3},{4,5},{5,6},{6,7},{8,9},{9,10},{10,11},{12,13},{... | collective-permute-start | bytes 786440 | tf_op jit(solution)/shard_map/ppermute | solution.py:360
  62.2 4.4 %collective-permute-start.5 = (f32[2,32,8,128]{3,2,1,0:T(8,128)S(1)}, f32[2,32,8,128]{3,2,1,0:T(8,128)S(1)}, u32[]{:S(2)}, u32[]{:S(2)}) collective-permute-start(f32[2,32,8,128]{3,2,1,0:T(8,128)S(1)} %get-tuple-element.26), channel_id=1, source_target_pairs={{1,0},{2,1},{3,2},{5,4},{6,5},{7,6},{9,8},{10,9},{11,10},{13,12},{... | collective-permute-start | bytes 786440 | tf_op jit(solution)/shard_map/ppermute | solution.py:360
  66.6 6.8 %collective-permute-start.6 = (f32[2,8,16,128]{3,2,1,0:T(8,128)S(1)}, f32[2,8,16,128]{3,2,1,0:T(8,128)S(1)}, u32[]{:S(2)}, u32[]{:S(2)}) collective-permute-start(f32[2,8,16,128]{3,2,1,0:T(8,128)S(1)} %get-tuple-element.28), channel_id=1, source_target_pairs={{0,4},{4,8},{8,12},{12,16},{16,20},{20,24},{24,28},{1,5},{5,9},{9,... | collective-permute-start | bytes 393224 | tf_op jit(solution)/shard_map/ppermute | solution.py:360
  70.9 6.9 %collective-permute-start.7 = (f32[2,8,16,128]{3,2,1,0:T(8,128)S(1)}, f32[2,8,16,128]{3,2,1,0:T(8,128)S(1)}, u32[]{:S(2)}, u32[]{:S(2)}) collective-permute-start(f32[2,8,16,128]{3,2,1,0:T(8,128)S(1)} %get-tuple-element.29), channel_id=1, source_target_pairs={{4,0},{8,4},{12,8},{16,12},{20,16},{24,20},{28,24},{5,1},{9,5},{13... | collective-permute-start | bytes 393224 | tf_op jit(solution)/shard_map/ppermute | solution.py:360
